TPU v7x, 512 devices: a whole 4x8x8 slice. The times are simulated.
512 devices in a mesh: row: 64 (over x, z, core), col: 8 (over y).
Axes of the slice: x: 4, y: 8, z: 8, core: 2. Of those that a mesh axis runs over, the one named last changes fastest.
Arguments:
- panel: float32 [32768, 256], P('row', 'col'), may hold values from -0.375 to 0.375
- trailing: float32 [32768, 8192], P('row', 'col'), may hold values from -6 to 6
- pivots: int32 [256], replicated, may hold values from 0 to 32767, as said below
Outputs:
- updated: float32 [32768, 8192], P('row', 'col')
Inputs may be any that keep to these rules, and one draw needn't show every extreme that they name: pivots[i] is a row index from i to 32767.
All inputs are finite; a program needn't handle non-finite values.
Results may differ from a plain program's by a relative error of at most 0.000058.
Values sent between devices are 32-bit elements; how exact they have to be, the bound alone decides.
No kernel may reach another device: no remote copies, remote signals or barrier semaphores. Data moves between devices by JAX's collectives and lax.ppermute only.
A program may use at most 64 MiB of HBM per device.

v0:
```python
import jax
import jax.numpy as jnp
from jax import lax
from jax.sharding import PartitionSpec as P


def broadcast(shard, axis, root):
    mine = lax.axis_index(axis) == root
    return lax.psum(jnp.where(mine, shard, jnp.zeros_like(shard)), axis)


def latest_match(targets, pivots, limit_rows):
    steps = jnp.arange(pivots.shape[0], dtype=jnp.int32)
    hits = pivots[None, :] == targets[:, None]
    if limit_rows:
        hits = hits & (steps[None, :] < targets[:, None])
    return jnp.max(jnp.where(hits, steps[None, :], -1), axis=1)


def pivot_order(pivots, positions):
    panel_width = pivots.shape[0]
    steps = jnp.arange(panel_width, dtype=jnp.int32)
    parent = latest_match(steps, pivots, True)
    pointer = jnp.where(parent < 0, steps, parent)
    for round_index in range(panel_width.bit_length() + 1):
        pointer = jnp.take(pointer, pointer, axis=0)
    earlier_hits = (pivots[None, :] == pivots[:, None]) & (steps[None, :] < steps[:, None])
    earlier = jnp.max(jnp.where(earlier_hits, steps[None, :], -1), axis=1)
    top_order = jnp.where(
        earlier >= 0, jnp.take(pointer, jnp.clip(earlier, 0, panel_width - 1), axis=0), pivots
    )
    last_hit = latest_match(positions, pivots, False)
    moved = jnp.where(
        last_hit >= 0, jnp.take(pointer, jnp.clip(last_hit, 0, panel_width - 1), axis=0), positions
    )
    head = jnp.take(top_order, jnp.clip(positions, 0, panel_width - 1), axis=0)
    return (top_order, jnp.where(positions < panel_width, head, moved))


def shards(panel, trailing, pivots):
    row_count = trailing.shape[0]
    panel_width = pivots.shape[0]
    first_row = lax.axis_index("row") * row_count
    global_rows = first_row + jnp.arange(row_count, dtype=jnp.int32)
    top_order, sources = pivot_order(pivots, global_rows)
    offsets = top_order - first_row
    inside = (offsets >= 0) & (offsets < row_count)
    picked = jnp.take(trailing, jnp.clip(offsets, 0, row_count - 1), axis=0)
    contributions = jnp.where(inside[:, None], picked, 0.0)
    full_top = lax.all_gather(panel[:panel_width], "col", axis=1, tiled=True)
    shipped = broadcast(jnp.concatenate([full_top, trailing[:panel_width]], axis=1), "row", 0)
    triangle = shipped[:, :panel_width]
    former_tops = shipped[:, panel_width:]
    l_block = jnp.tril(triangle, -1) + jnp.eye(panel_width, dtype=jnp.float32)
    top_block = lax.psum(contributions, "row")
    u_block = lax.linalg.triangular_solve(l_block, top_block, left_side=True, lower=True)
    products = jnp.dot(
        lax.all_gather(panel, "col", axis=1, tiled=True), u_block, precision=lax.Precision.HIGHEST
    )
    displaced = sources != global_rows
    incoming = jnp.take(former_tops, jnp.clip(sources, 0, panel_width - 1), axis=0)
    current = jnp.where(displaced[:, None], incoming, trailing)
    result = current - products
    head_rows = jnp.take(u_block, jnp.clip(global_rows, 0, panel_width - 1), axis=0)
    return jnp.where((global_rows < panel_width)[:, None], head_rows, result)


def solution(mesh):
    in_specs = (P("row", "col"), P("row", "col"), P())
    out_specs = P("row", "col")
    return jax.shard_map(shards, mesh=mesh, in_specs=in_specs, out_specs=out_specs, check_vma=False)
```

profile of v0, /device:TPU:1, one launch (start us, length us, event | category | flops | bytes accessed | tf_op | source)
XLA Modules:
  0.0 316.8 jit_solution(16447454364057899551)
XLA Ops:
  7.5 1.9 gather_fusion.1
  9.5 1.9 gather_fusion.2
  11.5 1.9 gather_fusion.3
  13.5 1.9 gather_fusion.4
  15.5 1.9 gather_fusion.5
  17.5 1.9 gather_fusion.6
  19.4 1.9 gather_fusion.7
  21.4 1.9 gather_fusion.8
  23.4 1.9 gather_fusion.9
  25.4 1.9 gather_fusion.10
  27.4 1.9 gather_fusion.11
  29.4 20.9 %all_gather.6 = f32[256,256]{0,1:T(8,128)S(1)} all-gather(f32[256,32]{0,1:T(8,128)S(1)} %slice-done.1), channel_id=1, replica_groups=mesh['row'=64,'col'=8] {'col'}, dimensions={1}, use_global_device_ids=true | all-gather | bytes 294912 | tf_op jit(solution)/shard_map/all_gather | solution.py:50
  56.9 3.5 %gather_fusion.13 = s32[512]{0:T(512)S(1)} fusion(s32[256]{0:T(256)S(1)} %get-tuple-element.31, s32[1024]{0:T(1024)S(1)} %pad_clamp_fusion.2), kind=kCustom, calls=%fused_computation.2.clone | custom fusion | bytes 6144 | tf_op jit(solution)/shard_map/jit(_take)/gather | solution.py:36
  60.4 3.5 %gather_fusion.14 = s32[512]{0:T(512)S(1)} fusion(s32[256]{0:T(256)S(1)} %and_select_fusion.1, s32[1024]{0:T(1024)S(1)} %pad_clamp_fusion.1), kind=kCustom, calls=%fused_computation.14.clone | custom fusion | bytes 6144 | tf_op jit(solution)/shard_map/jit(_take)/gather | solution.py:34
  64.0 21.6 %all_gather.7 = f32[512,256]{0,1:T(8,128)} all-gather(f32[512,32]{0,1:T(8,128)S(1)} %copy-done.4), channel_id=1, replica_groups=mesh['row'=64,'col'=8] {'col'}, dimensions={1}, use_global_device_ids=true | all-gather | bytes 589824 | tf_op jit(solution)/shard_map/all_gather | solution.py:58
  85.6 179.1 %all-reduce.3.cloned.1.call-done = (f32[256,1280]{1,0:T(8,128)}, f32[256,1024]{1,0:T(8,128)}) async-done(((f32[256,1280]{1,0:T(8,128)}, f32[256,1024]{1,0:T(8,128)}), (f32[256,1280]{1,0:T(8,128)}, f32[256,1024]{1,0:T(8,128)})) %all-reduce.3.cloned.1.call-update) | async-done | bytes 2359312 | tf_op jit(solution)/shard_map/psum | solution.py:9
  267.2 4.1 %while.1 = (s32[]{:T(128)}, f32[256,256]{1,0:T(8,128)S(1)}, s32[2,2]{1,0:T(2,128)S(1)}, f32[2,128,128]{2,1,0:T(8,128)S(1)}, s32[]{:T(128)}) while((s32[]{:T(128)}, f32[256,256]{1,0:T(8,128)S(1)}, s32[2,2]{1,0:T(2,128)S(1)}, f32[2,128,128]{2,1,0:T(8,128)S(1)}, s32[]{:T(128)}) %tuple.39), condition=%wide.while_cond, body=%wide.while_body.sunk | while | flops 2 | bytes 131189 | solution.py:56
  271.4 19.7 %custom-call.3 = f32[2,128,128]{1,2,0:T(8,128)S(1)} custom-call(f32[2,128,128]{2,1,0:T(8,128)S(1)} %get-tuple-element.15), custom_call_target="InvertDiagBlocksLowerTriangular" | custom-call | tf_op jit(solution)/shard_map/triangular_solve | solution.py:56
  293.9 1.9 gather_fusion.15
  295.9 1.8 copy.21
  299.0 1.9 gather_fusion.12
  300.9 1.8 copy.20
  302.7 5.5 %fusion = f32[512,1024]{0,1:T(8,128)S(1)} fusion(f32[512,1024]{0,1:T(8,128)} %copy.22, f32[512,1024]{0,1:T(8,128)} %copy.21, f32[512,1024]{0,1:T(8,128)} %copy.20, f32[512,256]{0,1:T(8,128)} %all_gather.7, pred[512]{0:T(512)(128)(4,1)S(1)} %compare_and_fusion, pred[512]{0:T(512)(128)(4,1)S(1)} %get-tuple-element.59, ...), kind=kOutput, calls=%fused_computation.19 | convolution fusion | flops 1613496320 | bytes 9963520 | tf_op jit(solution)/shard_map/dot_general | solution.py:57
  308.2 1.8 copy.23
  (75 shorter events, 18.5 us)
Async XLA Ops:
  6.5 258.2 %all-reduce.3.cloned.1.call-start = ((), (), s32[]{:S(2)}) async-start(), calls=%async_computation | async-start | bytes 4718592 | tf_op jit(solution)/shard_map/psum | solution.py:9
  21.4 7.9 %copy-start.5 = (s32[256]{0:T(256)S(1)}, s32[256]{0:T(256)}, u32[]{:S(2)}) copy-start(s32[256]{0:T(256)} %param.11) | copy-start | bytes 3076
  21.4 8.0 %slice-start.1 = ((f32[512,32]{0,1:T(8,128)}), f32[256,32]{0,1:T(8,128)S(1)}, s32[]{:S(2)}) async-start(f32[512,32]{0,1:T(8,128)} %param.9), calls=%async_computation.2 | async-start | bytes 65536 | tf_op jit(solution)/shard_map/slice | solution.py:50
  27.3 23.1 %copy-start = (f32[512,1024]{1,0:T(8,128)S(1)}, f32[512,1024]{1,0:T(8,128)}, u32[]{:S(2)}) copy-start(f32[512,1024]{1,0:T(8,128)} %param.10) | copy-start | bytes 6291460
  51.5 1.5 slice-start
  53.0 2.1 copy-start.1
  56.9 7.1 %copy-start.4 = (f32[512,32]{0,1:T(8,128)S(1)}, f32[512,32]{0,1:T(8,128)}, u32[]{:S(2)}) copy-start(f32[512,32]{0,1:T(8,128)} %param.9) | copy-start | bytes 196612
  264.7 26.3 %copy-start.3 = (f32[256,1024]{1,0:T(8,128)S(1)}, f32[256,1024]{1,0:T(8,128)}, u32[]{:S(2)}) copy-start(f32[256,1024]{1,0:T(8,128)} %get-tuple-element.27) | copy-start | bytes 3145732
  291.7 0.8 copy-start.2
Sparse Core Ops, SparseCore 0:
  54.3 210.3 all-reduce.2
where the time goes:
time: 318 us; the launch traced here: 317 us
  waiting for transfers between devices  179 us (56%)
  local copies, waits for them, and re-layouts  47.4 us (15%)
  blocking collectives  42.5 us (13%)
  other arithmetic  25.8 us (8%)
  between operations  13.9 us (4%)
  matrix products  8.1 us (3%)
    psum x1, waiting for transfers between devices, broadcast(): return lax.psum(jnp.where(mine, shard, jnp.zeros_like(shard)), axis)  179 us
    another operation x4, other arithmetic, shards(): lax.linalg.triangular_solve(l_block, top_block, left_side=True, lower=True)  22 us
    all_gather x1, blocking collectives, shards(): lax.all_gather(panel, 'col', axis=1, tiled=True)  21.6 us
    all_gather x1, blocking collectives, shards(): full_top = lax.all_gather(panel[:panel_width], 'col', axis=1, tiled=True)  20.9 us
    gather x10, local copies, waits for them, and re-layouts, pivot_order(): pointer = jnp.take(pointer, pointer, axis=0)  19.4 us
  transfers between devices with their start and end apart: 1, of which 1 were waited for; matrix products, arithmetic and copies ran while one was open for 3% of the time, Pallas kernels for 0%

commit v1 on v0

v1 whole, which is shorter than its diff:
```python
import functools

import jax
import jax.numpy as jnp
from jax import lax
from jax.experimental import pallas as pl
from jax.experimental.pallas import tpu as pltpu
from jax.sharding import Mesh, PartitionSpec as P

NB = 256
ORDER = 32768
LANES = 128
X, Z, C, Y = 4, 8, 2, 8
BLOCKS = X * C
ROWS = ORDER // (X * Z * C)
COLS = BLOCKS * LANES
NARROW = 64
HIGHEST = lax.Precision.HIGHEST
VMEM = pl.BlockSpec(memory_space=pltpu.VMEM)
SMEM = pl.BlockSpec(memory_space=pltpu.SMEM)
PARAMS = pltpu.CompilerParams(vmem_limit_bytes=48 * 1024 * 1024)


def loop(count, body, unroll=1):
    def step(i, carry):
        body(i)
        return carry

    lax.fori_loop(0, count, step, 0, unroll=unroll)


def tile_of(row):
    return pl.ds(pl.multiple_of(lax.div(row, 8) * 8, 8), 8)


def picked(row, width):
    return lax.broadcasted_iota(jnp.int32, (8, width), 0) == lax.rem(row, 8)


def load_row(ref, row):
    tile = ref[tile_of(row), :]
    return jnp.sum(jnp.where(picked(row, tile.shape[1]), tile, 0.0), axis=0, keepdims=True)


def store_row(ref, row, values):
    at = tile_of(row)
    tile = ref[at, :]
    ref[at, :] = jnp.where(picked(row, tile.shape[1]), values, tile)


def plan_kernel(pivots, source, filler, place, slot_of, count, most, content):
    def start(i):
        content[pivots[i]] = pivots[i]

    def start_top(i):
        content[i] = i

    def exchange(i):
        at = pivots[i]
        left, right = content[i], content[at]
        content[i] = right
        content[at] = left

    loop(NB, start, 8)
    loop(NB, start_top, 8)
    loop(NB, exchange, 4)
    for z in range(Z):
        count[z] = 0

    def rank(i):
        origin = content[i]
        source[i] = origin
        filler[i] = jnp.where(origin >= NB, content[origin], 0)
        plane = lax.rem(lax.div(origin, ROWS * C), Z)
        have = count[plane]
        place[i] = plane * NB + have
        slot_of[plane * NB + have] = i
        count[plane] = have + 1

    loop(NB, rank, 4)
    peak = count[0]
    for z in range(1, Z):
        peak = jnp.maximum(peak, count[z])
    most[0] = peak


def make_plan(pivots):
    shape = lambda n: jax.ShapeDtypeStruct((n,), jnp.int32)
    return pl.pallas_call(
        plan_kernel,
        out_shape=[shape(NB), shape(NB), shape(NB), shape(Z * NB), shape(Z), shape(1)],
        in_specs=[SMEM],
        out_specs=[SMEM] * 6,
        scratch_shapes=[pltpu.SMEM((ORDER,), jnp.int32)],
        name="plan",
    )(pivots)


def first_row():
    return ((lax.axis_index("x") * Z + lax.axis_index("z")) * C + lax.axis_index("c")) * ROWS


def pack_kernel(cap, source, slot_of, count, trailing, panel_t, out):
    z = lax.axis_index("z")
    first = first_row()
    for b in range(BLOCKS):
        out[b, :cap, :] = jnp.zeros((cap, LANES), jnp.float32)
        out[b, cap : cap + NB, :] = trailing[:NB, b * LANES : (b + 1) * LANES]
        q, h = b // 2, b % 2
        out[b, cap + NB :, :] = panel_t[8 * q : 8 * q + 8, h * LANES : (h + 1) * LANES]

    def put(r):
        local = source[slot_of[z * NB + r]] - first

        @pl.when((local >= 0) & (local < ROWS))
        def _():
            row = load_row(trailing, local)
            for b in range(BLOCKS):
                out[b, pl.ds(r, 1), :] = row[:, b * LANES : (b + 1) * LANES]

    loop(count[z], put)


def spread_kernel(cap, filler, place, got, out):
    rows = got[0, :cap, :]
    for s in range(1, BLOCKS):
        rows = rows + got[s, :cap, :]
    for z in range(Z):
        out[z, :cap, :] = rows
        out[z, 2 * cap :, :] = got[0, cap + NB :, :]

    def put(i):
        where = place[i]
        plane, rank = lax.div(where, NB), lax.rem(where, NB)
        out[plane, pl.ds(cap + rank, 1), :] = got[0, pl.ds(cap + filler[i], 1), :]

    loop(NB, put, 8)


def collect_kernel(cap, place, got, out, lower):
    def take(i):
        where = place[i]
        plane, rank = lax.div(where, NB), lax.rem(where, NB)
        out[0, pl.ds(i, 1), :] = got[plane, pl.ds(rank, 1), :]

    loop(NB, take, 8)
    out[0, NB:, :] = got[0, cap : 2 * cap, :]
    for x in range(1, X):
        out[x] = out[0]
    piece = got[0, 2 * cap :, :]
    for k in range(BLOCKS * Y):
        lower[k] = piece


def invert_kernel(pieces, out, upper):
    for b in range(BLOCKS):
        q, h = b // 2, b % 2
        for y in range(Y):
            at = 32 * y + 8 * q
            upper[at : at + 8, h * LANES : (h + 1) * LANES] = pieces[b * Y + y]
    rows = lax.broadcasted_iota(jnp.int32, (NB, NB), 0)
    cols = lax.broadcasted_iota(jnp.int32, (NB, NB), 1)
    values = upper[...]
    dot = functools.partial(jnp.dot, precision=HIGHEST, preferred_element_type=jnp.float32)
    inverse = jnp.where(rows == cols, 1.0, 0.0)
    inverse = inverse - jnp.where((cols == rows + 1) & (rows % 2 == 0), values, 0.0)
    size = 2
    while size < NB:
        mask = (rows // (2 * size) == cols // (2 * size)) & (rows // size < cols // size)
        inverse = inverse - dot(dot(inverse, jnp.where(mask, values, 0.0)), inverse)
        size *= 2
    out[...] = inverse.T


def finish_kernel(cap, source, slot_of, count, own, other, inverse, panel_t, trailing, out,
                  top, upper, current, multipliers):
    c = lax.axis_index("c")
    z = lax.axis_index("z")
    first = first_row()
    for x in range(X):
        for side, ref in ((c, own), (1 - c, other)):
            lanes = pl.ds(pl.multiple_of((x * C + side) * LANES, LANES), LANES)
            top[:, lanes] = ref[x]
    upper[...] = jnp.dot(inverse[...], top[:NB], precision=HIGHEST, preferred_element_type=jnp.float32)
    multipliers[...] = panel_t[...].T
    current[...] = trailing[...]

    def put(r):
        local = source[slot_of[z * NB + r]] - first

        @pl.when((local >= 0) & (local < ROWS))
        def _():
            store_row(current, local, load_row(top, NB + r))

    loop(count[z], put)
    step = 128

    def rows(k):
        at = pl.ds(pl.multiple_of(k * step, step), step)
        out[at, :] = current[at, :] - jnp.dot(
            multipliers[at, :], upper[...], precision=HIGHEST, preferred_element_type=jnp.float32
        )

    loop(ROWS // step, rows)

    @pl.when(first == 0)
    def _():
        out[:NB, :] = upper[...]


def call(kernel, out_shape, smem, vmem, scratch=(), name=None):
    single = not isinstance(out_shape, list)
    shapes = [out_shape] if single else out_shape
    got = pl.pallas_call(
        kernel,
        out_shape=[jax.ShapeDtypeStruct(s, jnp.float32) for s in shapes],
        in_specs=[SMEM] * len(smem) + [VMEM] * len(vmem),
        out_specs=[VMEM] * len(shapes),
        scratch_shapes=list(scratch),
        compiler_params=PARAMS,
        name=name,
    )(*smem, *vmem)
    return got[0] if single else got


def step(cap, panel_t, trailing, source, filler, place, slot_of, count):
    spread = functools.partial(lax.all_to_all, split_axis=0, concat_axis=0, tiled=True)
    whole_t = spread(jnp.broadcast_to(panel_t[None], (Y,) + panel_t.shape), "y").reshape(NB, ROWS)
    packed = call(functools.partial(pack_kernel, cap), (BLOCKS, cap + NB + 8, LANES),
                  (source, slot_of, count), (trailing, panel_t), name="pack")
    packed = spread(packed, ("x", "c"))
    planes = call(functools.partial(spread_kernel, cap), (Z, 2 * cap + 8, LANES),
                  (filler, place), (packed,), name="spread")
    planes = spread(planes, "z")
    blocks, pieces = call(functools.partial(collect_kernel, cap),
                          [(X, NB + cap, LANES), (BLOCKS * Y, 8, LANES)],
                          (place,), (planes,), name="collect")
    pieces = spread(pieces, ("x", "c", "y"))
    own = spread(blocks, "x")
    other = lax.ppermute(own, "c", [(0, 1), (1, 0)])
    inverse = call(invert_kernel, (NB, NB), (), (pieces,),
                   [pltpu.VMEM((NB, NB), jnp.float32)], name="invert")
    scratch = [pltpu.VMEM(s, jnp.float32)
               for s in ((NB + cap, COLS), (NB, COLS), (ROWS, COLS), (ROWS, NB))]
    return call(functools.partial(finish_kernel, cap), (ROWS, COLS), (source, slot_of, count),
                (own, other, inverse, whole_t, trailing), scratch, name="finish")


def shards(panel, trailing, pivots):
    source, filler, place, slot_of, count, most = make_plan(pivots)
    return lax.cond(
        most[0] <= NARROW,
        functools.partial(step, NARROW),
        functools.partial(step, NB),
        panel.T, trailing, source, filler, place, slot_of, count,
    )


def solution(mesh):
    fine = Mesh(mesh.devices.reshape(X, Z, C, Y), ("x", "z", "c", "y"))
    split = P(("x", "z", "c"), "y")
    return jax.shard_map(shards, mesh=fine, in_specs=(split, split, P()), out_specs=split, check_vma=False)
```

time: 318 us -> 128 us (0.40)
  waiting for transfers between devices: 179 us -> 6.46 us
  local copies, waits for them, and re-layouts: 47.4 us -> 2.17 us
  blocking collectives: 42.5 us -> 85.6 us
  other arithmetic: 25.8 us -> 0 us
  Pallas kernels: 0 us -> 24.7 us
  between operations: 13.9 us -> 0.67 us
  matrix products: 8.1 us -> 0 us
  starting transfers between devices: 0.01 us -> 7.24 us
    psum x1 -> x0, waiting for transfers between devices: 179 us -> none  [broadcast(): return lax.psum(jnp.where(mine, shard, jnp.zeros_like(shard)), axis)]
    all_to_all x0 -> x4, blocking collectives: none -> 85.6 us  [the longest x1 28 us: step(): packed = spread(packed, ('x', 'c'))]
    all_gather x2 -> x0, blocking collectives: 42.5 us -> none  [the longest x1 21.6 us: shards(): lax.all_gather(panel, 'col', axis=1, tiled=True)]
    gather x18 -> x0, local copies, waits for them, and re-layouts: 36.9 us -> none  [the longest x10 19.4 us: pivot_order(): pointer = jnp.take(pointer, pointer, axis=0)]
    pallas_call x0 -> x6, Pallas kernels: none -> 24.7 us  [the longest x5 18.7 us: call(): pl.pallas_call(kernel, out_shape=[jax.ShapeDtypeStruct(s, jnp.float32) fo...]
    another operation x4 -> x0, other arithmetic: 22 us -> none  [shards(): lax.linalg.triangular_solve(l_block, top_block, left_side=True, lower=True)]
    all_to_all x0 -> x1, waiting for transfers between devices: none -> 6.46 us  [step(): spread(jnp.broadcast_to(panel_t[None], (Y,) + panel_t.shape), 'y')]
    dot_general x1 -> x0, matrix products: 5.46 us -> none  [shards(): jnp.dot(lax.all_gather(panel, 'col', axis=1, tiled=True), u_block, precis...]
  transfers between devices with their start and end apart: 1 -> 2, of which waited for: 1 -> 1; matrix products, arithmetic and copies ran while one was open for 3% -> 0% of each run, Pallas kernels for 0% -> 5%
where the time goes in v1:
time: 128 us; the launch traced here: 127 us
  blocking collectives  85.6 us (67%)
  Pallas kernels  24.7 us (19%)
  starting transfers between devices  7.24 us (6%)
  waiting for transfers between devices  6.46 us (5%)
  local copies, waits for them, and re-layouts  2.17 us (2%)
    all_to_all x1, blocking collectives, step(): packed = spread(packed, ('x', 'c'))  28 us
    all_to_all x1, blocking collectives, step(): pieces = spread(pieces, ('x', 'c', 'y'))  23.4 us
    all_to_all x1, blocking collectives, step(): planes = spread(planes, 'z')  23.3 us
    pallas_call x5, Pallas kernels, call(): pl.pallas_call(kernel, out_shape=[jax.ShapeDtypeStruct(s, jnp.float32) fo...  18.7 us
    all_to_all x1, blocking collectives, step(): own = spread(blocks, 'x')  10.9 us
    all_to_all x1, waiting for transfers between devices, step(): spread(jnp.broadcast_to(panel_t[None], (Y,) + panel_t.shape), 'y')  6.46 us
    pallas_call x1, Pallas kernels, make_plan(): pl.pallas_call(plan_kernel, out_shape=[shape(NB), shape(NB), shape(NB), s...  6.02 us
    all_to_all x1, starting transfers between devices, step(): spread(jnp.broadcast_to(panel_t[None], (Y,) + panel_t.shape), 'y')  3.76 us
  transfers between devices with their start and end apart: 2, of which 1 were waited for; matrix products, arithmetic and copies ran while one was open for 0% of the time, Pallas kernels for 5%

profile of v1, /device:TPU:1, one launch (start us, length us, event | category | flops | bytes accessed | tf_op | source)
XLA Modules:
  0.0 127.1 jit_solution(6125010012589907048)
XLA Ops:
  0.0 6.0 %plan.1 = (s32[256]{0:T(256)S(1)}, s32[256]{0:T(256)S(1)}, s32[256]{0:T(256)S(1)}, s32[2048]{0:T(1024)S(1)}, s32[8]{0:T(128)S(1)}, /*index=5*/s32[1]{0:T(128)}) custom-call(s32[256]{0:T(256)} %pivots.1), custom_call_target="tpu_custom_call" | custom-call | tf_op jit(solution)/shard_map/plan/pallas_call | solution.py:89
  6.7 119.1 %conditional.1 = (f32[512,1024]{1,0:T(8,128)S(1)}) conditional(s32[]{:T(128)} %bitcast.2, (s32[256]{0:T(256)S(1)}, s32[2048]{0:T(1024)S(1)}, s32[8]{0:T(128)S(1)}, f32[512,1024]{1,0:T(8,128)}, f32[32,512]{1,0:T(8,128)}, /*index=5*/s32[256]{0:T(256)S(1)}, s32[256]{0:T(256)S(1)}) %tuple.17, (s32[256]{0:T(256)S(1)}, s32[2048]{0:T(1024)S(1)}, ...), branch_computations={%region_0.0_spmd, %region_1.0_spmd} | conditional | bytes 18022540 | solution.py:251
  6.7 2.3 %pack.3 = f32[8,328,128]{2,1,0:T(8,128)S(1)} custom-call(s32[256]{0:T(256)S(1)} %get-tuple-element.45.source, s32[2048]{0:T(1024)S(1)} %get-tuple-element.46.slot_of, s32[8]{0:T(128)S(1)} %get-tuple-element.47.count, f32[512,1024]{1,0:T(8,128)} %get-tuple-element.70.trailing, f32[32,512]{1,0:T(8,128)} %get-tuple-element.51.panel_t), custom_call_target="tpu_custom_call" | custom-call | tf_op jit(solution)/shard_map/cond/branch_1_fun/pack/pallas_call | solution.py:214
  9.0 28.0 %all_to_all.43.got = f32[8,328,128]{2,1,0:T(8,128)S(1)} all-to-all(f32[8,328,128]{2,1,0:T(8,128)S(1)} %pack.3), channel_id=1, replica_groups=mesh['x'=4,'z'=8,'c'=2,'y'=8] {'x','c'}, dimensions={0} | all-to-all | bytes 2686976 | tf_op jit(solution)/shard_map/cond/branch_1_fun/all_to_all | solution.py:231
  37.0 1.8 %spread.3 = f32[8,136,128]{2,1,0:T(8,128)S(1)} custom-call(s32[256]{0:T(256)S(1)} %get-tuple-element.49.filler, s32[256]{0:T(256)S(1)} %get-tuple-element.48.place, f32[8,328,128]{2,1,0:T(8,128)S(1)} %all_to_all.43.got), custom_call_target="tpu_custom_call" | custom-call | tf_op jit(solution)/shard_map/cond/branch_1_fun/spread/pallas_call | solution.py:214
  38.8 0.0 copy-start.2
  38.8 23.3 %all_to_all.44.got = f32[8,136,128]{2,1,0:T(8,128)S(1)} all-to-all(f32[8,136,128]{2,1,0:T(8,128)S(1)} %spread.3), channel_id=1, replica_groups=mesh['x'=4,'z'=8,'c'=2,'y'=8] {'z'}, dimensions={0} | all-to-all | bytes 1114112 | tf_op jit(solution)/shard_map/cond/branch_1_fun/all_to_all | solution.py:234
  62.1 1.7 %collect.3 = (f32[4,320,128]{2,1,0:T(8,128)S(1)}, f32[64,8,128]{2,1,0:T(8,128)S(1)}) custom-call(s32[256]{0:T(256)S(1)} %get-tuple-element.48.place, f32[8,136,128]{2,1,0:T(8,128)S(1)} %all_to_all.44.got), custom_call_target="tpu_custom_call" | custom-call | tf_op jit(solution)/shard_map/cond/branch_1_fun/collect/pallas_call | solution.py:214
  63.8 10.9 %all_to_all.45.own = f32[4,320,128]{2,1,0:T(8,128)S(1)} all-to-all(f32[4,320,128]{2,1,0:T(8,128)S(1)} %get-tuple-element.52), channel_id=1, replica_groups=mesh['x'=4,'z'=8,'c'=2,'y'=8] {'x'}, dimensions={0} | all-to-all | bytes 1310720 | tf_op jit(solution)/shard_map/cond/branch_1_fun/all_to_all | solution.py:239
  74.7 23.4 %all_to_all.46.pieces = f32[64,8,128]{2,1,0:T(8,128)S(1)} all-to-all(f32[64,8,128]{2,1,0:T(8,128)S(1)} %get-tuple-element.53), channel_id=1, replica_groups=mesh['x'=4,'z'=8,'c'=2,'y'=8] {'x','c','y'}, dimensions={0} | all-to-all | bytes 524288 | tf_op jit(solution)/shard_map/cond/branch_1_fun/all_to_all | solution.py:238
  98.1 0.0 copy-done.2
  98.1 0.9 broadcast_in_dim.2
  99.0 3.8 %all-to-all-start.9 = ((f32[8,32,512]{2,1,0:T(8,128)}), f32[8,32,512]{2,1,0:T(8,128)S(1)}, u32[]{:S(2)}, u32[]{:S(2)}) async-start(f32[8,32,512]{2,1,0:T(8,128)} %broadcast_in_dim.2), calls=%async_computation.9 | async-start | bytes 1048576 | tf_op jit(solution)/shard_map/cond/branch_1_fun/all_to_all | solution.py:228
  102.7 3.5 %collective-permute-start.1 = (f32[4,320,128]{2,1,0:T(8,128)S(1)}, f32[4,320,128]{2,1,0:T(8,128)S(1)}, u32[]{:S(2)}, u32[]{:S(2)}) collective-permute-start(f32[4,320,128]{2,1,0:T(8,128)S(1)} %all_to_all.45.own), channel_id=1, source_target_pairs={{0,8},{8,0},{1,9},{9,1},{2,10},{10,2},{3,11},{11,3},{4,12},{12,4},... | collective-permute-start | bytes 1966088 | tf_op jit(solution)/shard_map/cond/branch_1_fun/ppermute | solution.py:240
  106.2 6.8 %invert.3.inverse = f32[256,256]{1,0:T(8,128)S(1)} custom-call(f32[64,8,128]{2,1,0:T(8,128)S(1)} %all_to_all.46.pieces), custom_call_target="tpu_custom_call" | custom-call | tf_op jit(solution)/shard_map/cond/branch_1_fun/invert/pallas_call | solution.py:214
  113.0 6.5 %all-to-all-done.9 = f32[8,32,512]{2,1,0:T(8,128)S(1)} async-done(((f32[8,32,512]{2,1,0:T(8,128)}), f32[8,32,512]{2,1,0:T(8,128)S(1)}, u32[]{:S(2)}, u32[]{:S(2)}) %all-to-all-start.9) | async-done | bytes 524320 | tf_op jit(solution)/shard_map/cond/branch_1_fun/all_to_all | solution.py:228
  119.5 0.0 collective-permute-done.1.other
  119.5 6.1 %finish.3 = f32[512,1024]{1,0:T(8,128)S(1)} custom-call(s32[256]{0:T(256)S(1)} %get-tuple-element.45.source, s32[2048]{0:T(1024)S(1)} %get-tuple-element.46.slot_of, s32[8]{0:T(128)S(1)} %get-tuple-element.47.count, f32[4,320,128]{2,1,0:T(8,128)S(1)} %all_to_all.45.own, f32[4,320,128]{2,1,0:T(8,128)S(1)} %collective-permute-done.1.other, ...), custom_call_target="tpu_custom_call" | custom-call | tf_op jit(solution)/shard_map/cond/branch_1_fun/finish/pallas_call | solution.py:214
  125.8 0.0 copy-start
  125.8 1.3 %copy-done = f32[512,1024]{1,0:T(8,128)} copy-done((f32[512,1024]{1,0:T(8,128)}, f32[512,1024]{1,0:T(8,128)S(1)}, u32[]{:S(2)}) %copy-start) | copy-done | bytes 2097176
Async XLA Ops:
  38.8 59.3 %copy-start.2 = (f32[32,512]{1,0:T(8,128)S(1)}, f32[32,512]{1,0:T(8,128)}, u32[]{:S(2)}) copy-start(f32[32,512]{1,0:T(8,128)} %get-tuple-element.51.panel_t) | copy-start | bytes 196612 | tf_op jit(solution)/shard_map/cond
  99.0 20.5 %all-to-all-start.9 = ((f32[8,32,512]{2,1,0:T(8,128)}), f32[8,32,512]{2,1,0:T(8,128)S(1)}, u32[]{:S(2)}, u32[]{:S(2)}) async-start(f32[8,32,512]{2,1,0:T(8,128)} %broadcast_in_dim.2), calls=%async_computation.9 | async-start | bytes 1048576 | tf_op jit(solution)/shard_map/cond/branch_1_fun/all_to_all | solution.py:228
  102.7 16.7 %collective-permute-start.1 = (f32[4,320,128]{2,1,0:T(8,128)S(1)}, f32[4,320,128]{2,1,0:T(8,128)S(1)}, u32[]{:S(2)}, u32[]{:S(2)}) collective-permute-start(f32[4,320,128]{2,1,0:T(8,128)S(1)} %all_to_all.45.own), channel_id=1, source_target_pairs={{0,8},{8,0},{1,9},{9,1},{2,10},{10,2},{3,11},{11,3},{4,12},{12,4},... | collective-permute-start | bytes 1966088 | tf_op jit(solution)/shard_map/cond/branch_1_fun/ppermute | solution.py:240
  125.8 1.3 %copy-start = (f32[512,1024]{1,0:T(8,128)}, f32[512,1024]{1,0:T(8,128)S(1)}, u32[]{:S(2)}) copy-start(f32[512,1024]{1,0:T(8,128)S(1)} %get-tuple-element.80) | copy-start | bytes 6291460

commit v2 on v1

v2 whole, which is shorter than its diff:
```python
import functools

import jax
import jax.numpy as jnp
from jax import lax
from jax.experimental import pallas as pl
from jax.experimental.pallas import tpu as pltpu
from jax.sharding import Mesh, PartitionSpec as P

NB = 256
ORDER = 32768
LANES = 128
X, Z, C, Y = 4, 8, 2, 8
BLOCKS = X * C
ROWS = ORDER // (X * Z * C)
COLS = BLOCKS * LANES
NARROW = 64
HIGHEST = lax.Precision.HIGHEST
VMEM = pl.BlockSpec(memory_space=pltpu.VMEM)
SMEM = pl.BlockSpec(memory_space=pltpu.SMEM)
PARAMS = pltpu.CompilerParams(vmem_limit_bytes=48 * 1024 * 1024)


def loop(count, body, unroll=1):
    def step(i, carry):
        body(i)
        return carry

    lax.fori_loop(0, count, step, 0, unroll=unroll)


def tile_of(row):
    return pl.ds(pl.multiple_of(lax.div(row, 8) * 8, 8), 8)


def picked(row, width):
    return lax.broadcasted_iota(jnp.int32, (8, width), 0) == lax.rem(row, 8)


def load_row(ref, row):
    tile = ref[tile_of(row), :]
    return jnp.sum(jnp.where(picked(row, tile.shape[1]), tile, 0.0), axis=0, keepdims=True)


def store_row(ref, row, values):
    at = tile_of(row)
    tile = ref[at, :]
    ref[at, :] = jnp.where(picked(row, tile.shape[1]), values, tile)


def plane_of(row):
    return lax.rem(lax.div(row, ROWS * C), Z)


def plan_kernel(pivots, source, filler, place, slot_of, count, most, content):
    def start(i):
        content[pivots[i]] = pivots[i]

    def start_top(i):
        content[i] = i

    def exchange(i):
        at = pivots[i]
        left, right = content[i], content[at]
        content[i] = right
        content[at] = left

    loop(NB, start, 8)
    loop(NB, start_top, 8)
    loop(NB, exchange, 4)
    for z in range(Z):
        count[z] = 0

    def rank(i):
        origin = content[i]
        source[i] = origin
        filler[i] = jnp.where(origin >= NB, content[origin], 0)
        plane = plane_of(origin)
        have = count[plane]
        place[i] = plane * NB + have
        slot_of[plane * NB + have] = i
        count[plane] = have + 1

    loop(NB, rank, 4)
    peak = count[0]
    for z in range(1, Z):
        peak = jnp.maximum(peak, count[z])
    most[0] = peak


def make_plan(pivots):
    shape = lambda n: jax.ShapeDtypeStruct((n,), jnp.int32)
    return pl.pallas_call(
        plan_kernel,
        out_shape=[shape(NB), shape(NB), shape(NB), shape(Z * NB), shape(Z), shape(1)],
        in_specs=[SMEM],
        out_specs=[SMEM] * 6,
        scratch_shapes=[pltpu.SMEM((ORDER,), jnp.int32)],
        cost_estimate=pl.CostEstimate(flops=0, bytes_accessed=16 * 1024 * 1024, transcendentals=0),
        name="plan",
    )(pivots)


def first_row():
    return ((lax.axis_index("x") * Z + lax.axis_index("z")) * C + lax.axis_index("c")) * ROWS


def pack_kernel(cap, pivots, trailing, panel_t, out, seen):
    z = lax.axis_index("z")
    first = first_row()
    for b in range(BLOCKS):
        out[b, :cap, :] = jnp.zeros((cap, LANES), jnp.float32)
        out[b, cap : cap + NB, :] = trailing[:NB, b * LANES : (b + 1) * LANES]
        q, h = b // 2, b % 2
        out[b, cap + NB :, :] = panel_t[8 * q : 8 * q + 8, h * LANES : (h + 1) * LANES]

    def clear(i):
        seen[pivots[i]] = 0

    loop(NB, clear, 8)

    def put(i, rank):
        row = pivots[i]
        again = seen[row]
        seen[row] = 1
        local = row - first

        @pl.when((again == 0) & (local >= 0) & (local < ROWS))
        def _():
            values = load_row(trailing, local)
            at = pl.ds(jnp.minimum(rank, cap - 1), 1)
            for b in range(BLOCKS):
                out[b, at, :] = values[:, b * LANES : (b + 1) * LANES]

        plane = jnp.where(again == 1, 0, plane_of(row))
        return rank + (plane == z).astype(jnp.int32)

    lax.fori_loop(0, NB, put, jnp.int32(0), unroll=4)


def spread_kernel(cap, source, filler, place, slot_of, count, got, out):
    for z in range(Z):
        out[z, 2 * cap :, :] = got[0, cap + NB :, :]
    rows = got[0, :cap, :]
    for s in range(1, BLOCKS):
        rows = rows + got[s, :cap, :]
    out[0, :cap, :] = rows

    @pl.when(lax.axis_index("z") == 0)
    def _():
        def top(r):
            origin = source[slot_of[r]]

            @pl.when(origin < NB)
            def _():
                out[0, pl.ds(r, 1), :] = got[0, pl.ds(cap + origin, 1), :]

        loop(jnp.minimum(count[0], cap), top)

        def put(i):
            where = place[i]
            plane, rank = lax.div(where, NB), jnp.minimum(lax.rem(where, NB), cap - 1)
            out[plane, pl.ds(cap + rank, 1), :] = got[0, pl.ds(cap + filler[i], 1), :]

        loop(NB, put, 8)

    for z in range(1, Z):
        out[z, :cap, :] = out[0, :cap, :]


def collect_kernel(cap, place, got, pieces, out):
    def take(i):
        where = place[i]
        plane, rank = lax.div(where, NB), jnp.minimum(lax.rem(where, NB), cap - 1)
        out[0, pl.ds(i, 1), :] = got[plane, pl.ds(rank, 1), :]

    loop(NB, take, 8)
    out[0, NB : NB + cap, :] = got[0, cap : 2 * cap, :]
    for y in range(Y):
        out[0, NB + cap + 8 * y : NB + cap + 8 * y + 8, :] = pieces[y]
    for x in range(1, X):
        out[x] = out[0]


def invert_kernel(cap, own, other, out, upper):
    c = lax.axis_index("c")
    for x in range(X):
        for side, ref in ((c, own), (1 - c, other)):
            lanes = pl.ds(pl.multiple_of(side * LANES, LANES), LANES)
            for y in range(Y):
                at = 32 * y + 8 * x
                upper[at : at + 8, lanes] = ref[x, NB + cap + 8 * y : NB + cap + 8 * y + 8, :]
    rows = lax.broadcasted_iota(jnp.int32, (NB, NB), 0)
    cols = lax.broadcasted_iota(jnp.int32, (NB, NB), 1)
    values = upper[...]
    dot = functools.partial(jnp.dot, precision=HIGHEST, preferred_element_type=jnp.float32)
    inverse = jnp.where(rows == cols, 1.0, 0.0)
    inverse = inverse - jnp.where((cols == rows + 1) & (rows % 2 == 0), values, 0.0)
    size = 2
    while size < NB:
        mask = (rows // (2 * size) == cols // (2 * size)) & (rows // size < cols // size)
        inverse = inverse - dot(dot(inverse, jnp.where(mask, values, 0.0)), inverse)
        size *= 2
    out[...] = inverse.T


def finish_kernel(cap, source, slot_of, count, own, other, inverse, whole_t, trailing, out,
                  top, upper, current, multipliers, sem):
    copy = pltpu.make_async_copy(trailing, current, sem)
    copy.start()
    c = lax.axis_index("c")
    z = lax.axis_index("z")
    first = first_row()
    for x in range(X):
        for side, ref in ((c, own), (1 - c, other)):
            lanes = pl.ds(pl.multiple_of((x * C + side) * LANES, LANES), LANES)
            top[:, lanes] = ref[x, : NB + cap]
    upper[...] = jnp.dot(inverse[...], top[:NB], precision=HIGHEST, preferred_element_type=jnp.float32)
    for y in range(Y):
        multipliers[:, 32 * y : 32 * y + 32] = whole_t[y, c].T
    copy.wait()

    def put(r):
        local = source[slot_of[z * NB + r]] - first

        @pl.when((local >= 0) & (local < ROWS))
        def _():
            store_row(current, local, load_row(top, NB + r))

    loop(jnp.minimum(count[z], cap), put)
    step = 128

    def rows(k):
        at = pl.ds(pl.multiple_of(k * step, step), step)
        out[at, :] = current[at, :] - jnp.dot(
            multipliers[at, :], upper[...], precision=HIGHEST, preferred_element_type=jnp.float32
        )

    loop(ROWS // step, rows)

    @pl.when(first == 0)
    def _():
        out[:NB, :] = upper[...]


def call(kernel, shape, smem, vmem, scratch=(), name=None, last=VMEM, busy=2):
    return pl.pallas_call(
        kernel,
        out_shape=jax.ShapeDtypeStruct(shape, jnp.float32),
        in_specs=[SMEM] * len(smem) + [VMEM] * (len(vmem) - 1) + [last],
        out_specs=VMEM,
        scratch_shapes=list(scratch),
        compiler_params=PARAMS,
        cost_estimate=pl.CostEstimate(flops=0, bytes_accessed=busy * 2**20, transcendentals=0),
        name=name,
    )(*smem, *vmem)


def exchange(cap, panel_t, trailing, pivots, plan):
    source, filler, place, slot_of, count = plan
    spread = functools.partial(lax.all_to_all, split_axis=0, concat_axis=0, tiled=True)
    packed = call(functools.partial(pack_kernel, cap), (BLOCKS, cap + NB + 8, LANES),
                  (pivots,), (trailing, panel_t), [pltpu.SMEM((ORDER,), jnp.int32)], name="pack")
    packed = spread(packed, ("x", "c"))
    planes = call(functools.partial(spread_kernel, cap), (Z, 2 * cap + 8, LANES),
                  (source, filler, place, slot_of, count), (packed,), name="spread")
    planes = spread(planes, "z")
    pieces = spread(jnp.broadcast_to(planes[:1, 2 * cap :], (Y, 8, LANES)), "y")
    blocks = call(functools.partial(collect_kernel, cap), (X, NB + cap + 8 * Y, LANES),
                  (place,), (planes, pieces), name="collect")
    own = spread(blocks, "x")
    other = lax.ppermute(own, "c", [(0, 1), (1, 0)])
    inverse = call(functools.partial(invert_kernel, cap), (NB, NB), (), (own, other),
                   [pltpu.VMEM((NB, NB), jnp.float32)], name="invert", busy=16)
    return own, other, inverse


def finish(cap, own, other, inverse, whole_t, trailing, plan):
    source, _, _, slot_of, count = plan
    scratch = [pltpu.VMEM(s, jnp.float32)
               for s in ((NB + cap, COLS), (NB, COLS), (ROWS, COLS), (ROWS, NB))]
    return call(functools.partial(finish_kernel, cap), (ROWS, COLS), (source, slot_of, count),
                (own, other, inverse, whole_t, trailing), scratch + [pltpu.SemaphoreType.DMA],
                name="finish", last=pl.BlockSpec(memory_space=pl.ANY), busy=16)


def shards(panel, trailing, pivots):
    panel_t = panel.T
    whole_t = lax.all_gather(panel_t, ("y", "c"), axis=0).reshape(Y, C, 32, ROWS)
    *plan, most = make_plan(pivots)
    ready = exchange(NARROW, panel_t, trailing, pivots, plan)

    def narrow(ready, panel_t, whole_t, trailing, pivots, plan):
        return finish(NARROW, *ready, whole_t, trailing, plan)

    def wide(ready, panel_t, whole_t, trailing, pivots, plan):
        return finish(NB, *exchange(NB, panel_t, trailing, pivots, plan), whole_t, trailing, plan)

    return lax.cond(most[0] <= NARROW, narrow, wide, ready, panel_t, whole_t, trailing, pivots, plan)


def solution(mesh):
    fine = Mesh(mesh.devices.reshape(X, Z, C, Y), ("x", "z", "c", "y"))
    split = P(("x", "z", "c"), "y")
    return jax.shard_map(shards, mesh=fine, in_specs=(split, split, P()), out_specs=split, check_vma=False)
```

time: 128 us -> 127 us (level)
  blocking collectives: 85.6 us -> 25.9 us
  waiting for transfers between devices: 6.46 us -> 32.3 us
  between operations: 0.67 us -> 14.1 us
  starting transfers between devices: 7.24 us -> 19.3 us
  Pallas kernels: 24.7 us -> 32.9 us
    all_to_all x4 -> x2, blocking collectives: 85.6 us -> 25.9 us  [the longest x1 13.5 us: exchange(): pieces = spread(jnp.broadcast_to(planes[:1, 2 * cap:], (Y, 8, LANES)), 'y')]
    all_to_all x1 -> x2, waiting for transfers between devices: 6.46 us -> 30.3 us  [the longest x1 17.9 us: exchange(): planes = spread(planes, 'z')]
    all_to_all x1 -> x2, starting transfers between devices: 3.76 us -> 14 us  [the longest x1 10.5 us: exchange(): packed = spread(packed, ('x', 'c'))]
    pallas_call x5, Pallas kernels: 18.7 us -> 27.1 us  [call(): pl.pallas_call(kernel, out_shape=jax.ShapeDtypeStruct(shape, jnp.float32)...]
    ppermute x1, starting transfers between devices: 3.48 us -> 5.18 us  [exchange(): other = lax.ppermute(own, 'c', [(0, 1), (1, 0)])]
    ppermute x1, waiting for transfers between devices: 0.01 us -> 1.38 us  [exchange(): other = lax.ppermute(own, 'c', [(0, 1), (1, 0)])]
  transfers between devices with their start and end apart: 2 -> 4, of which waited for: 1 -> 3; matrix products, arithmetic and copies ran while one was open for 0% -> 0% of each run, Pallas kernels for 5% -> 6%
where the time goes in v2:
time: 127 us; the launch traced here: 126 us
  Pallas kernels  32.9 us (26%)
  waiting for transfers between devices  32.3 us (25%)
  blocking collectives  25.9 us (20%)
  starting transfers between devices  19.3 us (15%)
  between operations  14.1 us (11%)
  local copies, waits for them, and re-layouts  1.33 us (1%)
    pallas_call x5, Pallas kernels, call(): pl.pallas_call(kernel, out_shape=jax.ShapeDtypeStruct(shape, jnp.float32)...  27.1 us
    all_to_all x1, waiting for transfers between devices, exchange(): planes = spread(planes, 'z')  17.9 us
    all_to_all x1, blocking collectives, exchange(): pieces = spread(jnp.broadcast_to(planes[:1, 2 * cap:], (Y, 8, LANES)), 'y')  13.5 us
    all_to_all x1, waiting for transfers between devices, exchange(): packed = spread(packed, ('x', 'c'))  12.4 us
    all_to_all x1, blocking collectives, exchange(): own = spread(blocks, 'x')  12.4 us
    all_to_all x1, starting transfers between devices, exchange(): packed = spread(packed, ('x', 'c'))  10.5 us
    pallas_call x1, Pallas kernels, make_plan(): pl.pallas_call(plan_kernel, out_shape=[shape(NB), shape(NB), shape(NB), s...  5.89 us
    ppermute x1, starting transfers between devices, exchange(): other = lax.ppermute(own, 'c', [(0, 1), (1, 0)])  5.18 us
  transfers between devices with their start and end apart: 4, of which 3 were waited for; matrix products, arithmetic and copies ran while one was open for 0% of the time, Pallas kernels for 6%

profile of v2, /device:TPU:1, one launch (start us, length us, event | category | flops | bytes accessed | tf_op | source)
XLA Modules:
  0.0 126.1 jit_solution(8429819950419268956)
XLA Ops:
  6.5 7.6 %pack.3 = f32[8,328,128]{2,1,0:T(8,128)} custom-call(s32[256]{0:T(256)} %pivots.3, f32[512,1024]{1,0:T(8,128)} %trailing.1, f32[32,512]{1,0:T(8,128)} %bitcast.9), custom_call_target="tpu_custom_call" | custom-call | bytes 2097152 | tf_op jit(solution)/shard_map/pack/pallas_call | solution.py:247
  14.1 0.0 copy-start.4
  14.1 10.5 %all-to-all-start.4 = ((f32[8,328,128]{2,1,0:T(8,128)}), f32[8,328,128]{2,1,0:T(8,128)S(1)}, u32[]{:S(2)}, u32[]{:S(2)}) async-start(f32[8,328,128]{2,1,0:T(8,128)} %pack.3), calls=%async_computation.4 | async-start | bytes 2686976 | tf_op jit(solution)/shard_map/all_to_all | solution.py:264
  24.6 0.0 copy-done.4
  24.6 5.9 %plan.1 = (s32[256]{0:T(256)S(1)}, s32[256]{0:T(256)S(1)}, s32[256]{0:T(256)S(1)}, s32[2048]{0:T(1024)S(1)}, s32[8]{0:T(128)S(1)}, /*index=5*/s32[1]{0:T(128)}) custom-call(s32[256]{0:T(256)S(1)} %copy-done.4), custom_call_target="tpu_custom_call" | custom-call | bytes 16777216 | tf_op jit(solution)/shard_map/plan/pallas_call | solution.py:93
  30.5 12.4 %all-to-all-done.4.got = f32[8,328,128]{2,1,0:T(8,128)S(1)} async-done(((f32[8,328,128]{2,1,0:T(8,128)}), f32[8,328,128]{2,1,0:T(8,128)S(1)}, u32[]{:S(2)}, u32[]{:S(2)}) %all-to-all-start.4) | async-done | bytes 1343520 | tf_op jit(solution)/shard_map/all_to_all | solution.py:264
  42.9 3.5 %spread.3 = f32[8,136,128]{2,1,0:T(8,128)} custom-call(s32[256]{0:T(256)S(1)} %get-tuple-element.66.source, s32[256]{0:T(256)S(1)} %get-tuple-element.67.filler, s32[256]{0:T(256)S(1)} %get-tuple-element.68.place, s32[2048]{0:T(1024)S(1)} %get-tuple-element.69.slot_of, s32[8]{0:T(128)S(1)} %get-tuple-element.70.count, f32[8,328,128]{2,1,0:T(8,128)S(1)} %all-to-all-done.4.got), custom_call_target="tpu_custom_call" | custom-call | bytes 2097152 | tf_op jit(solution)/shard_map/spread/pallas_call | solution.py:247
  46.4 3.6 %all-to-all-start.5 = ((f32[8,136,128]{2,1,0:T(8,128)}), f32[8,136,128]{2,1,0:T(8,128)S(1)}, u32[]{:S(2)}, u32[]{:S(2)}) async-start(f32[8,136,128]{2,1,0:T(8,128)} %spread.3), calls=%async_computation.5 | async-start | bytes 1114112 | tf_op jit(solution)/shard_map/all_to_all | solution.py:267
  49.9 0.0 all-gather.3.cloned.1.call-start
  50.0 0.7 all-gather.3.cloned.1.call-update
  50.6 17.9 %all-to-all-done.5.got = f32[8,136,128]{2,1,0:T(8,128)S(1)} async-done(((f32[8,136,128]{2,1,0:T(8,128)}), f32[8,136,128]{2,1,0:T(8,128)S(1)}, u32[]{:S(2)}, u32[]{:S(2)}) %all-to-all-start.5) | async-done | bytes 557088 | tf_op jit(solution)/shard_map/all_to_all | solution.py:267
  68.5 13.5 %all_to_all.40.pieces = f32[8,8,128]{2,1,0:T(8,128)S(1)} all-to-all(f32[8,8,128]{2,1,0:T(8,128)S(1)} %broadcast_in_dim.15), channel_id=1, replica_groups=mesh['x'=4,'z'=8,'c'=2,'y'=8] {'y'}, dimensions={0} | all-to-all | bytes 65536 | tf_op jit(solution)/shard_map/all_to_all | solution.py:268
  82.0 1.8 %collect.3 = f32[4,384,128]{2,1,0:T(8,128)S(1)} custom-call(s32[256]{0:T(256)S(1)} %get-tuple-element.68.place, f32[8,136,128]{2,1,0:T(8,128)S(1)} %all-to-all-done.5.got, f32[8,8,128]{2,1,0:T(8,128)S(1)} %all_to_all.40.pieces), custom_call_target="tpu_custom_call" | custom-call | bytes 2097152 | tf_op jit(solution)/shard_map/collect/pallas_call | solution.py:247
  83.8 12.4 %all_to_all.41.own = f32[4,384,128]{2,1,0:T(8,128)S(1)} all-to-all(f32[4,384,128]{2,1,0:T(8,128)S(1)} %collect.3), channel_id=1, replica_groups=mesh['x'=4,'z'=8,'c'=2,'y'=8] {'x'}, dimensions={0} | all-to-all | bytes 1572864 | tf_op jit(solution)/shard_map/all_to_all | solution.py:271
  96.2 5.2 %collective-permute-start.1 = (f32[4,384,128]{2,1,0:T(8,128)S(1)}, f32[4,384,128]{2,1,0:T(8,128)}, u32[]{:S(2)}, u32[]{:S(2)}) collective-permute-start(f32[4,384,128]{2,1,0:T(8,128)S(1)} %all_to_all.41.own), channel_id=1, source_target_pairs={{0,8},{8,0},{1,9},{9,1},{2,10},{10,2},{3,11},{11,3},{4,12},{12,4},... | collective-permute-start | bytes 2359304 | tf_op jit(solution)/shard_map/ppermute | solution.py:272
  102.0 0.0 all-gather.3.cloned.1.call-done
  102.0 1.4 %collective-permute-done.1.other = f32[4,384,128]{2,1,0:T(8,128)} collective-permute-done((f32[4,384,128]{2,1,0:T(8,128)S(1)}, f32[4,384,128]{2,1,0:T(8,128)}, u32[]{:S(2)}, u32[]{:S(2)}) %collective-permute-start.1) | collective-permute-done | bytes 786464 | tf_op jit(solution)/shard_map/ppermute | solution.py:272
  103.4 7.9 %invert.3 = f32[256,256]{1,0:T(8,128)S(1)} custom-call(f32[4,384,128]{2,1,0:T(8,128)S(1)} %all_to_all.41.own, f32[4,384,128]{2,1,0:T(8,128)} %collective-permute-done.1.other), custom_call_target="tpu_custom_call" | custom-call | bytes 16777216 | tf_op jit(solution)/shard_map/invert/pallas_call | solution.py:247
  111.4 0.0 copy-done
  111.4 0.0 copy-done.3
  111.4 6.5 %conditional.1 = (f32[512,1024]{1,0:T(8,128)S(1)}) conditional(s32[]{:T(128)} %bitcast.1, (s32[256]{0:T(256)S(1)}, f32[512,1024]{1,0:T(8,128)S(1)}, f32[32,512]{1,0:T(8,128)S(1)}, s32[256]{0:T(256)S(1)}, s32[256]{0:T(256)S(1)}, /*index=5*/s32[256]{0:T(256)S(1)}, s32[2048]{0:T(1024)S(1)}, s32[8]{0:T(128)S(1)}, f32[8,2,32,512]{3,2,1,0:T(8,128)}) %tuple.25, ...), branch_computations={%region_0.0_spmd, %region_1.0_spmd} | conditional | bytes 59748428 | solution.py:299
  111.6 6.3 %finish.3 = f32[512,1024]{1,0:T(8,128)S(1)} custom-call(s32[256]{0:T(256)S(1)} %get-tuple-element.51.source, s32[2048]{0:T(1024)S(1)} %get-tuple-element.52.slot_of, s32[8]{0:T(128)S(1)} %get-tuple-element.53.count, f32[4,384,128]{2,1,0:T(8,128)S(1)} %get-tuple-element.54.own, f32[4,384,128]{2,1,0:T(8,128)} %get-tuple-element.55.other, ...), custom_call_target="tpu_custom_call" | custom-call | bytes 16777216 | tf_op jit(solution)/shard_map/cond/branch_1_fun/finish/pallas_call | solution.py:247
  117.9 0.0 copy-start.2
  117.9 1.3 %copy-done.2 = f32[512,1024]{1,0:T(8,128)} copy-done((f32[512,1024]{1,0:T(8,128)}, f32[512,1024]{1,0:T(8,128)S(1)}, u32[]{:S(2)}) %copy-start.2) | copy-done | bytes 2097176
  (4 shorter events, 0.0 us)
Async XLA Ops:
  14.1 10.5 %copy-start.4 = (s32[256]{0:T(256)S(1)}, s32[256]{0:T(256)}, u32[]{:S(2)}) copy-start(s32[256]{0:T(256)} %pivots.3) | copy-start | bytes 3076
  14.1 28.8 %all-to-all-start.4 = ((f32[8,328,128]{2,1,0:T(8,128)}), f32[8,328,128]{2,1,0:T(8,128)S(1)}, u32[]{:S(2)}, u32[]{:S(2)}) async-start(f32[8,328,128]{2,1,0:T(8,128)} %pack.3), calls=%async_computation.4 | async-start | bytes 2686976 | tf_op jit(solution)/shard_map/all_to_all | solution.py:264
  46.4 22.2 %all-to-all-start.5 = ((f32[8,136,128]{2,1,0:T(8,128)}), f32[8,136,128]{2,1,0:T(8,128)S(1)}, u32[]{:S(2)}, u32[]{:S(2)}) async-start(f32[8,136,128]{2,1,0:T(8,128)} %spread.3), calls=%async_computation.5 | async-start | bytes 1114112 | tf_op jit(solution)/shard_map/all_to_all | solution.py:267
  49.9 52.1 %all-gather.3.cloned.1.call-start = ((), (), s32[]{:S(2)}) async-start(), calls=%async_computation.8 | async-start | bytes 1114112 | tf_op jit(solution)/shard_map/all_gather | solution.py:289
  82.0 29.3 %copy-start = (f32[512,1024]{1,0:T(8,128)S(1)}, f32[512,1024]{1,0:T(8,128)}, u32[]{:S(2)}) copy-start(f32[512,1024]{1,0:T(8,128)} %trailing.1) | copy-start | bytes 6291460
  82.0 29.3 %copy-start.3 = (f32[512,32]{0,1:T(8,128)S(1)}, f32[512,32]{0,1:T(8,128)}, u32[]{:S(2)}) copy-start(f32[512,32]{0,1:T(8,128)} %param.5) | copy-start | bytes 196612
  96.2 7.2 %collective-permute-start.1 = (f32[4,384,128]{2,1,0:T(8,128)S(1)}, f32[4,384,128]{2,1,0:T(8,128)}, u32[]{:S(2)}, u32[]{:S(2)}) collective-permute-start(f32[4,384,128]{2,1,0:T(8,128)S(1)} %all_to_all.41.own), channel_id=1, source_target_pairs={{0,8},{8,0},{1,9},{9,1},{2,10},{10,2},{3,11},{11,3},{4,12},{12,4},... | collective-permute-start | bytes 2359304 | tf_op jit(solution)/shard_map/ppermute | solution.py:272
  117.9 1.3 %copy-start.2 = (f32[512,1024]{1,0:T(8,128)}, f32[512,1024]{1,0:T(8,128)S(1)}, u32[]{:S(2)}) copy-start(f32[512,1024]{1,0:T(8,128)S(1)} %get-tuple-element.81) | copy-start | bytes 6291460
Sparse Core Ops, SparseCore 0:
  52.9 41.3 all-gather.2

commit v3 on v2

v3 whole, which is shorter than its diff:
```python
import functools

import jax
import jax.numpy as jnp
from jax import lax
from jax.experimental import pallas as pl
from jax.experimental.pallas import tpu as pltpu
from jax.sharding import Mesh, PartitionSpec as P

NB = 256
ORDER = 32768
LANES = 128
X, Z, C, Y = 4, 8, 2, 8
BLOCKS = X * C
ROWS = ORDER // (X * Z * C)
COLS = BLOCKS * LANES
DIAG = NB // Y
BATCH = 16
BITS = NB.bit_length() - 1
PLANE_BITS = (ROWS * C).bit_length() - 1
NARROW = 64
HIGHEST = lax.Precision.HIGHEST
VMEM = pl.BlockSpec(memory_space=pltpu.VMEM)
SMEM = pl.BlockSpec(memory_space=pltpu.SMEM)
PARAMS = pltpu.CompilerParams(vmem_limit_bytes=48 * 1024 * 1024)


def loop(count, body, unroll=1):
    def step(i, carry):
        body(i)
        return carry

    lax.fori_loop(0, count, step, 0, unroll=unroll)


def tile_of(row):
    return pl.ds(pl.multiple_of(row & -8, 8), 8)


def picked(row, width):
    return lax.broadcasted_iota(jnp.int32, (8, width), 0) == (row & 7)


def load_row(ref, row):
    tile = ref[tile_of(row), :]
    return jnp.sum(jnp.where(picked(row, tile.shape[1]), tile, 0.0), axis=0, keepdims=True)


def store_row(ref, row, values):
    at = tile_of(row)
    tile = ref[at, :]
    ref[at, :] = jnp.where(picked(row, tile.shape[1]), values, tile)


def plane_of(row):
    return (row >> PLANE_BITS) & (Z - 1)


def first_row():
    return ((lax.axis_index("x") * Z + lax.axis_index("z")) * C + lax.axis_index("c")) * ROWS


def plan_kernel(pivots, filler, place, slot_of, tops, count, most, content):
    def start(i):
        content[pivots[i]] = pivots[i]

    def start_top(i):
        content[i] = i

    loop(NB, start, 8)
    loop(NB, start_top, 8)

    def exchange(i, found):
        at = pivots[i]
        left, right = content[i], content[at]
        content[i] = right
        content[at] = left
        tops[found] = i * NB + right
        return found + (right != at).astype(jnp.int32)

    found = lax.fori_loop(0, NB, exchange, jnp.int32(0), unroll=4)
    for z in range(Z):
        count[z] = 0

    def rank(i):
        row = pivots[i]
        filler[i] = jnp.where(row < NB, 0, content[row])
        plane = plane_of(row)
        have = count[plane]
        place[i] = plane * NB + have
        slot_of[plane * NB + have] = i
        count[plane] = have + 1

    loop(NB, rank, 4)
    count[Z] = found
    peak = count[0]
    for z in range(1, Z):
        peak = jnp.maximum(peak, count[z])
    most[0] = peak + found


def make_plan(pivots):
    sizes = (NB, NB, Z * NB, NB + 8, Z + 1, 1)
    return pl.pallas_call(
        plan_kernel,
        out_shape=[jax.ShapeDtypeStruct((n,), jnp.int32) for n in sizes],
        in_specs=[SMEM],
        out_specs=[SMEM] * len(sizes),
        scratch_shapes=[pltpu.SMEM((ORDER,), jnp.int32)],
        cost_estimate=pl.CostEstimate(flops=0, bytes_accessed=16 * 1024 * 1024, transcendentals=0),
        name="plan",
    )(pivots)


def invert_diagonal(panel_t, at):
    y = lax.axis_index("y")
    lanes = pl.ds(pl.multiple_of((y * DIAG) & -LANES, LANES), LANES)
    shift = (y * DIAG) & (LANES - 1)
    window = pltpu.roll(panel_t[:, lanes], (LANES - shift) & (LANES - 1), axis=1)
    rows = lax.broadcasted_iota(jnp.int32, (DIAG, LANES), 0)
    cols = lax.broadcasted_iota(jnp.int32, (DIAG, LANES), 1)
    strict = (cols > rows) & (cols < DIAG)
    values = jnp.where(strict, window, 0.0)
    inverse = jnp.where(rows == cols, 1.0, 0.0)
    for k in range(DIAG - 1, 0, -1):
        inverse = inverse - values[:, k : k + 1] * inverse[k : k + 1, :]
    window = jnp.where(strict, inverse, window)
    at[:, :] = panel_t[:, :NB]
    at[:, lanes] = pltpu.roll(window, shift, axis=1)


def pack_kernel(cap, pivots, panel_t, trailing, out, triangle, rows, mine, sem):
    copy = pltpu.make_async_copy(trailing, rows, sem)
    copy.start()
    z = lax.axis_index("z")
    first = first_row()

    def find(i, carry):
        rank, found = carry
        row = pivots[i]
        local = row - first
        mine[found] = local * NB + jnp.minimum(rank, cap - 1)
        hit = (local >= 0) & (local < ROWS)
        return rank + (plane_of(row) == z).astype(jnp.int32), found + hit.astype(jnp.int32)

    _, found = lax.fori_loop(0, NB, find, (jnp.int32(0), jnp.int32(0)), unroll=16)
    invert_diagonal(panel_t, triangle)
    for b in range(BLOCKS):
        out[b, :cap, :] = jnp.zeros((cap, LANES), jnp.float32)
        q, h = b // C, b % C
        out[b, cap + NB :, :] = triangle[8 * q : 8 * q + 8, h * LANES : (h + 1) * LANES]
    copy.wait()
    for b in range(BLOCKS):
        out[b, cap : cap + NB, :] = rows[:NB, b * LANES : (b + 1) * LANES]

    def put(k):
        entry = mine[k]
        values = load_row(rows, entry >> BITS)
        at = pl.ds(entry & (NB - 1), 1)
        for b in range(BLOCKS):
            out[b, at, :] = values[:, b * LANES : (b + 1) * LANES]

    loop(found, put)


def spread_kernel(cap, room, filler, place, tops, count, got, out):
    for z in range(Z):
        out[z, cap + room :, :] = got[0, cap + NB :, :]
    rows = got[0, :cap, :]
    for s in range(1, BLOCKS):
        rows = rows + got[s, :cap, :]
    for z in range(Z):
        out[z, :cap, :] = rows

    @pl.when(lax.axis_index("z") == 0)
    def _():
        def put(k):
            moves = []
            for i in range(BATCH):
                where = place[k * BATCH + i]
                rank = jnp.minimum(where & (NB - 1), cap - 1)
                values = got[0, pl.ds(cap + filler[k * BATCH + i], 1), :]
                moves.append((where >> BITS, cap + rank, values))
            for plane, at, values in moves:
                out[plane, pl.ds(at, 1), :] = values

        loop(NB // BATCH, put)

        def top(k):
            values = got[0, pl.ds(cap + (tops[k] & (NB - 1)), 1), :]
            for z in range(Z):
                out[z, pl.ds(cap + jnp.minimum(count[z] + k, room - 1), 1), :] = values

        loop(count[Z], top)


def collect_kernel(cap, room, place, tops, count, got, pieces, out):
    z = lax.axis_index("z")

    def take(k):
        base = pl.multiple_of(k * BATCH, BATCH)
        rows = []
        for i in range(BATCH):
            where = place[base + i]
            rank = jnp.minimum(where & (NB - 1), cap - 1)
            rows.append(got[where >> BITS, pl.ds(rank, 1), :])
        for i in range(BATCH):
            out[0, pl.ds(base + i, 1), :] = rows[i]

    loop(NB // BATCH, take)

    def top(k):
        at = cap + jnp.minimum(count[z] + k, room - 1)
        out[0, pl.ds(tops[k] >> BITS, 1), :] = got[0, pl.ds(at, 1), :]

    loop(count[Z], top)
    out[0, NB : NB + cap, :] = got[0, cap : 2 * cap, :]
    for y in range(Y):
        out[0, NB + cap + 8 * y : NB + cap + 8 * y + 8, :] = pieces[y]
    for x in range(1, X):
        out[x] = out[0]


def dot(a, b):
    return jnp.dot(a, b, precision=HIGHEST, preferred_element_type=jnp.float32)


def invert(upper):
    half = NB // 2
    rows = lax.broadcasted_iota(jnp.int32, (half, half), 0)
    cols = lax.broadcasted_iota(jnp.int32, (half, half), 1)
    parts = []
    for k in range(2):
        values = upper[k * half : (k + 1) * half, k * half : (k + 1) * half]
        part = jnp.where((rows // DIAG == cols // DIAG) & (rows < cols), values, 0.0)
        part = part + jnp.where(rows == cols, 1.0, 0.0)
        parts.append((values, part))
    size = DIAG
    while size < half:
        mask = (rows // (2 * size) == cols // (2 * size)) & (rows // size < cols // size)
        parts = [(v, p - dot(dot(p, jnp.where(mask, v, 0.0)), p)) for v, p in parts]
        size *= 2
    (_, first), (_, second) = parts
    corner = -dot(dot(first, upper[:half, half:]), second)
    left = jnp.concatenate([first.T, corner.T], axis=0)
    right = jnp.concatenate([jnp.zeros((half, half), jnp.float32), second.T], axis=0)
    return jnp.concatenate([left, right], axis=1)


def turn_kernel(whole_t, out):
    c = lax.axis_index("c")
    for y in range(Y):
        out[:, DIAG * y : DIAG * (y + 1)] = whole_t[y, c].T


def finish_kernel(cap, pivots, slot_of, count, own, other, multipliers, trailing, out,
                  upper, inverse, block, current, in_sem, out_sem):
    copy = pltpu.make_async_copy(trailing, current, in_sem)
    copy.start()
    c = lax.axis_index("c")
    z = lax.axis_index("z")
    first = first_row()
    sides = ((pl.multiple_of(c * LANES, LANES), own), (pl.multiple_of((1 - c) * LANES, LANES), other))
    for x in range(X):
        for lane, ref in sides:
            for y in range(Y):
                at = DIAG * y + 8 * x
                upper[at : at + 8, pl.ds(lane, LANES)] = ref[x, NB + cap + 8 * y : NB + cap + 8 * y + 8, :]
    inverse[...] = invert(upper)
    copy.wait()

    def put(r):
        local = pivots[slot_of[z * NB + r]] - first

        @pl.when((local >= 0) & (local < ROWS))
        def _():
            at = tile_of(local)
            hit = picked(local, LANES)
            for x in range(X):
                for lane, ref in sides:
                    lanes = pl.ds(pl.multiple_of(x * C * LANES + lane, LANES), LANES)
                    current[at, lanes] = jnp.where(hit, ref[x, pl.ds(NB + r, 1), :], current[at, lanes])

    loop(jnp.minimum(count[z], cap), put)
    copies = []
    width = C * LANES
    for x in range(X):
        lanes = slice(x * width, (x + 1) * width)
        for lane, ref in sides:
            block[x, :, pl.ds(lane, LANES)] = ref[x, :NB, :]
        solved = dot(inverse[...], block[x])
        block[x] = solved
        current[:, lanes] = current[:, lanes] - dot(multipliers[...], solved)

        @pl.when(first == 0)
        def _():
            current[:NB, lanes] = block[x]

        copies.append(pltpu.make_async_copy(current.at[:, lanes], out.at[:, lanes], out_sem.at[x]))
        copies[-1].start()
    for copy in copies:
        copy.wait()


def call(kernel, shape, smem, vmem, scratch=(), name=None, last=VMEM, out=VMEM, busy=2):
    return pl.pallas_call(
        kernel,
        out_shape=jax.ShapeDtypeStruct(shape, jnp.float32),
        in_specs=[SMEM] * len(smem) + [VMEM] * (len(vmem) - 1) + [last],
        out_specs=out,
        scratch_shapes=list(scratch),
        compiler_params=PARAMS,
        cost_estimate=pl.CostEstimate(flops=0, bytes_accessed=busy * 2**20, transcendentals=0),
        name=name,
    )(*smem, *vmem)


def pack(cap, pivots, trailing, panel_t):
    scratch = [pltpu.VMEM((DIAG, NB), jnp.float32), pltpu.VMEM((ROWS, COLS), jnp.float32),
               pltpu.SMEM((NB + 8,), jnp.int32), pltpu.SemaphoreType.DMA]
    return call(functools.partial(pack_kernel, cap), (BLOCKS, cap + NB + 8, LANES),
                (pivots,), (panel_t, trailing), scratch, name="pack", last=pl.BlockSpec(memory_space=pl.ANY))


def spread(cap, room, plan, packed):
    filler, place, _, tops, count = plan
    return call(functools.partial(spread_kernel, cap, room), (Z, cap + room + 8, LANES),
                (filler, place, tops, count), (packed,), name="spread")


def collect(cap, room, plan, planes, pieces):
    _, place, _, tops, count = plan
    return call(functools.partial(collect_kernel, cap, room), (X, NB + cap + 8 * Y, LANES),
                (place, tops, count), (planes, pieces), name="collect")


def finish(cap, pivots, plan, own, other, multipliers, trailing):
    _, _, slot_of, _, count = plan
    scratch = [pltpu.VMEM(s, jnp.float32) for s in ((NB, NB), (NB, NB), (X, NB, C * LANES), (ROWS, COLS))]
    scratch += [pltpu.SemaphoreType.DMA, pltpu.SemaphoreType.DMA((X,))]
    return call(functools.partial(finish_kernel, cap), (ROWS, COLS), (pivots, slot_of, count),
                (own, other, multipliers, trailing), scratch, name="finish",
                last=pl.BlockSpec(memory_space=pl.ANY), out=pl.BlockSpec(memory_space=pltpu.HBM), busy=16)


def exchange(cap, room, panel_t, trailing, pivots, plan):
    swap = functools.partial(lax.all_to_all, split_axis=0, concat_axis=0, tiled=True)
    packed = swap(pack(cap, pivots, trailing, panel_t), ("x", "c"))
    planes = swap(spread(cap, room, plan, packed), "z")
    pieces = swap(jnp.broadcast_to(planes[:1, cap + room :], (Y, 8, LANES)), "y")
    own = swap(collect(cap, room, plan, planes, pieces), "x")
    return own, lax.ppermute(own, "c", [(0, 1), (1, 0)])


def shards(panel, trailing, pivots):
    panel_t = panel.T
    whole_t = lax.all_gather(panel_t, ("y", "c"), axis=0).reshape(Y, C, DIAG, ROWS)
    multipliers = call(turn_kernel, (ROWS, NB), (), (whole_t,), name="turn")
    *plan, most = make_plan(pivots)

    def with_room(cap, room):
        ready = exchange(cap, room, panel_t, trailing, pivots, plan)
        return finish(cap, pivots, plan, *ready, multipliers, trailing)

    def pending(carry):
        return carry[0]

    def again(carry):
        return jnp.zeros_like(carry[0]), with_room(NB, 2 * NB)

    return lax.while_loop(pending, again, (most[0] > NARROW, with_room(NARROW, NARROW)))[1]


def solution(mesh):
    fine = Mesh(mesh.devices.reshape(X, Z, C, Y), ("x", "z", "c", "y"))
    split = P(("x", "z", "c"), "y")
    return jax.shard_map(shards, mesh=fine, in_specs=(split, split, P()), out_specs=split, check_vma=False)
```

time: 127 us -> 117 us (0.921)
  Pallas kernels: 32.9 us -> 23.9 us
    pallas_call x5, Pallas kernels: 27.1 us -> 18.3 us  [call(): pl.pallas_call(kernel, out_shape=jax.ShapeDtypeStruct(shape, jnp.float32)...]
    ppermute x1, waiting for transfers between devices: 1.38 us -> 0.01 us  [exchange(): return (own, lax.ppermute(own, 'c', [(0, 1), (1, 0)]))]
  transfers between devices with their start and end apart: 4 -> 4, of which waited for: 3 -> 2; matrix products, arithmetic and copies ran while one was open for 0% -> 0% of each run, Pallas kernels for 6% -> 7%
where the time goes in v3:
time: 117 us
  waiting for transfers between devices  31.3 us (27%)
  blocking collectives  25.9 us (22%)
  Pallas kernels  23.9 us (20%)
  starting transfers between devices  20.2 us (17%)
  between operations  14.2 us (12%)
  local copies, waits for them, and re-layouts  1.25 us (1%)
    pallas_call x5, Pallas kernels, call(): pl.pallas_call(kernel, out_shape=jax.ShapeDtypeStruct(shape, jnp.float32)...  18.3 us
    all_to_all x1, waiting for transfers between devices, exchange(): planes = swap(spread(cap, room, plan, packed), 'z')  17.9 us
    all_to_all x1, blocking collectives, exchange(): pieces = swap(jnp.broadcast_to(planes[:1, cap + room:], (Y, 8, LANES)), 'y')  13.5 us
    all_to_all x1, waiting for transfers between devices, exchange(): packed = swap(pack(cap, pivots, trailing, panel_t), ('x', 'c'))  12.7 us
    all_to_all x1, blocking collectives, exchange(): own = swap(collect(cap, room, plan, planes, pieces), 'x')  12.4 us
    all_to_all x1, starting transfers between devices, exchange(): packed = swap(pack(cap, pivots, trailing, panel_t), ('x', 'c'))  10.3 us
    pallas_call x1, Pallas kernels, make_plan(): pl.pallas_call(plan_kernel, out_shape=[jax.ShapeDtypeStruct((n,), jnp.int...  5.59 us
    ppermute x1, starting transfers between devices, exchange(): return (own, lax.ppermute(own, 'c', [(0, 1), (1, 0)]))  5.18 us
  transfers between devices with their start and end apart: 4, of which 2 were waited for; matrix products, arithmetic and copies ran while one was open for 0% of the time, Pallas kernels for 7%

profile of v3, /device:TPU:1, one launch (start us, length us, event | category | flops | bytes accessed | tf_op | source)
XLA Modules:
  0.0 116.7 jit_solution(2610214143486339825)
XLA Ops:
  6.5 4.0 %pack.3 = f32[8,328,128]{2,1,0:T(8,128)} custom-call(s32[256]{0:T(256)} %pivots.5, f32[32,512]{1,0:T(8,128)} %bitcast.8, f32[512,1024]{1,0:T(8,128)} %trailing.3), custom_call_target="tpu_custom_call" | custom-call | bytes 2097152 | tf_op jit(solution)/shard_map/pack/pallas_call | solution.py:306
  10.6 0.0 copy-start.4
  10.6 10.3 %all-to-all-start.4 = ((f32[8,328,128]{2,1,0:T(8,128)}), f32[8,328,128]{2,1,0:T(8,128)S(1)}, u32[]{:S(2)}, u32[]{:S(2)}) async-start(f32[8,328,128]{2,1,0:T(8,128)} %pack.3), calls=%async_computation.4 | async-start | bytes 2686976 | tf_op jit(solution)/shard_map/all_to_all | solution.py:348
  20.9 5.6 %plan.1 = (s32[256]{0:T(256)S(1)}, s32[256]{0:T(256)S(1)}, s32[2048]{0:T(1024)S(1)}, s32[264]{0:T(512)S(1)}, s32[9]{0:T(128)S(1)}, /*index=5*/s32[1]{0:T(128)}) custom-call(s32[256]{0:T(256)S(1)} %copy-done.4), custom_call_target="tpu_custom_call" | custom-call | bytes 16777216 | tf_op jit(solution)/shard_map/plan/pallas_call | solution.py:104
  26.5 12.7 %all-to-all-done.4.got = f32[8,328,128]{2,1,0:T(8,128)S(1)} async-done(((f32[8,328,128]{2,1,0:T(8,128)}), f32[8,328,128]{2,1,0:T(8,128)S(1)}, u32[]{:S(2)}, u32[]{:S(2)}) %all-to-all-start.4) | async-done | bytes 1343520 | tf_op jit(solution)/shard_map/all_to_all | solution.py:348
  39.2 2.3 %spread.3 = f32[8,136,128]{2,1,0:T(8,128)} custom-call(s32[256]{0:T(256)S(1)} %get-tuple-element.111.filler, s32[256]{0:T(256)S(1)} %get-tuple-element.112.place, s32[264]{0:T(512)S(1)} %get-tuple-element.113.tops, s32[9]{0:T(128)S(1)} %get-tuple-element.114.count, f32[8,328,128]{2,1,0:T(8,128)S(1)} %all-to-all-done.4.got), custom_call_target="tpu_custom_call" | custom-call | bytes 2097152 | tf_op jit(solution)/shard_map/spread/pallas_call | solution.py:306
  41.5 4.6 %all-to-all-start.5 = ((f32[8,136,128]{2,1,0:T(8,128)}), f32[8,136,128]{2,1,0:T(8,128)S(1)}, u32[]{:S(2)}, u32[]{:S(2)}) async-start(f32[8,136,128]{2,1,0:T(8,128)} %spread.3), calls=%async_computation.5 | async-start | bytes 1114112 | tf_op jit(solution)/shard_map/all_to_all | solution.py:349
  46.1 0.0 all-gather.3.cloned.1.call-start
  46.1 0.7 all-gather.3.cloned.1.call-update
  46.8 17.9 %all-to-all-done.5.got = f32[8,136,128]{2,1,0:T(8,128)S(1)} async-done(((f32[8,136,128]{2,1,0:T(8,128)}), f32[8,136,128]{2,1,0:T(8,128)S(1)}, u32[]{:S(2)}, u32[]{:S(2)}) %all-to-all-start.5) | async-done | bytes 557088 | tf_op jit(solution)/shard_map/all_to_all | solution.py:349
  64.7 13.5 %all_to_all.40.pieces = f32[8,8,128]{2,1,0:T(8,128)S(1)} all-to-all(f32[8,8,128]{2,1,0:T(8,128)S(1)} %broadcast_in_dim.15), channel_id=1, replica_groups=mesh['x'=4,'z'=8,'c'=2,'y'=8] {'y'}, dimensions={0} | all-to-all | bytes 65536 | tf_op jit(solution)/shard_map/all_to_all | solution.py:350
  78.2 1.3 %collect.3 = f32[4,384,128]{2,1,0:T(8,128)S(1)} custom-call(s32[256]{0:T(256)S(1)} %get-tuple-element.112.place, s32[264]{0:T(512)S(1)} %get-tuple-element.113.tops, s32[9]{0:T(128)S(1)} %get-tuple-element.114.count, f32[8,136,128]{2,1,0:T(8,128)S(1)} %all-to-all-done.5.got, f32[8,8,128]{2,1,0:T(8,128)S(1)} %all_to_all.40.pieces), custom_call_target="tpu_custom_call" | custom-call | bytes 2097152 | tf_op jit(solution)/shard_map/collect/pallas_call | solution.py:306
  79.6 12.4 %all_to_all.41.own = f32[4,384,128]{2,1,0:T(8,128)S(1)} all-to-all(f32[4,384,128]{2,1,0:T(8,128)S(1)} %collect.3), channel_id=1, replica_groups=mesh['x'=4,'z'=8,'c'=2,'y'=8] {'x'}, dimensions={0} | all-to-all | bytes 1572864 | tf_op jit(solution)/shard_map/all_to_all | solution.py:351
  91.9 5.2 %collective-permute-start.1 = (f32[4,384,128]{2,1,0:T(8,128)S(1)}, f32[4,384,128]{2,1,0:T(8,128)S(1)}, u32[]{:S(2)}, u32[]{:S(2)}) collective-permute-start(f32[4,384,128]{2,1,0:T(8,128)S(1)} %all_to_all.41.own), channel_id=1, source_target_pairs={{0,8},{8,0},{1,9},{9,1},{2,10},{10,2},{3,11},{11,3},{4,12},{12,4},... | collective-permute-start | bytes 2359304 | tf_op jit(solution)/shard_map/ppermute | solution.py:352
  97.7 0.0 all-gather.3.cloned.1.call-done
  97.8 1.2 %copy-done = f32[512,512]{1,0:T(8,128)S(1)} copy-done((f32[512,512]{1,0:T(8,128)S(1)}, f32[512,512]{1,0:T(8,128)}, u32[]{:S(2)}) %copy-start) | copy-done | bytes 1048600
  99.0 1.0 turn.1.multipliers
  100.0 0.0 collective-permute-done.1.other
  100.0 0.0 copy-start.1
  100.0 0.0 copy-start.3
  100.1 9.6 %finish.3 = f32[512,1024]{1,0:T(8,128)} custom-call(s32[256]{0:T(256)S(1)} %copy-done.4, s32[2048]{0:T(1024)S(1)} %get-tuple-element.115.slot_of, s32[9]{0:T(128)S(1)} %get-tuple-element.114.count, f32[4,384,128]{2,1,0:T(8,128)S(1)} %all_to_all.41.own, f32[4,384,128]{2,1,0:T(8,128)S(1)} %collective-permute-done.1.other, f32[512,256]{1,0:T(8,128)S(1)} %turn.1.multipliers, ...), custom_call_target="tpu_custom_call" | custom-call | bytes 16777216 | tf_op jit(solution)/shard_map/finish/pallas_call | solution.py:306
  109.7 0.0 copy-done.1
  109.7 0.0 copy-done.3
  109.7 0.2 while.9
  (4 shorter events, 0.0 us)
Async XLA Ops:
  10.6 10.3 %copy-start.4 = (s32[256]{0:T(256)S(1)}, s32[256]{0:T(256)}, u32[]{:S(2)}) copy-start(s32[256]{0:T(256)} %pivots.5) | copy-start | bytes 3076
  10.6 28.6 %all-to-all-start.4 = ((f32[8,328,128]{2,1,0:T(8,128)}), f32[8,328,128]{2,1,0:T(8,128)S(1)}, u32[]{:S(2)}, u32[]{:S(2)}) async-start(f32[8,328,128]{2,1,0:T(8,128)} %pack.3), calls=%async_computation.4 | async-start | bytes 2686976 | tf_op jit(solution)/shard_map/all_to_all | solution.py:348
  41.5 23.3 %all-to-all-start.5 = ((f32[8,136,128]{2,1,0:T(8,128)}), f32[8,136,128]{2,1,0:T(8,128)S(1)}, u32[]{:S(2)}, u32[]{:S(2)}) async-start(f32[8,136,128]{2,1,0:T(8,128)} %spread.3), calls=%async_computation.5 | async-start | bytes 1114112 | tf_op jit(solution)/shard_map/all_to_all | solution.py:349
  46.1 51.7 %all-gather.3.cloned.1.call-start = ((), (), s32[]{:S(2)}) async-start(), calls=%async_computation.8 | async-start | bytes 1114112 | tf_op jit(solution)/shard_map/all_gather | solution.py:357
  91.9 8.1 %collective-permute-start.1 = (f32[4,384,128]{2,1,0:T(8,128)S(1)}, f32[4,384,128]{2,1,0:T(8,128)S(1)}, u32[]{:S(2)}, u32[]{:S(2)}) collective-permute-start(f32[4,384,128]{2,1,0:T(8,128)S(1)} %all_to_all.41.own), channel_id=1, source_target_pairs={{0,8},{8,0},{1,9},{9,1},{2,10},{10,2},{3,11},{11,3},{4,12},{12,4},... | collective-permute-start | bytes 2359304 | tf_op jit(solution)/shard_map/ppermute | solution.py:352
  97.8 1.2 %copy-start = (f32[512,512]{1,0:T(8,128)S(1)}, f32[512,512]{1,0:T(8,128)}, u32[]{:S(2)}) copy-start(f32[512,512]{1,0:T(8,128)} %all-gather.3.cloned.1.call-done) | copy-start | bytes 3145732
  100.0 9.6 %copy-start.1 = (f32[512,1024]{1,0:T(8,128)S(1)}, f32[512,1024]{1,0:T(8,128)}, u32[]{:S(2)}) copy-start(f32[512,1024]{1,0:T(8,128)} %trailing.3) | copy-start | bytes 6291460
  100.0 9.6 %copy-start.3 = (f32[512,32]{0,1:T(8,128)S(1)}, f32[512,32]{0,1:T(8,128)}, u32[]{:S(2)}) copy-start(f32[512,32]{0,1:T(8,128)} %param.5) | copy-start | bytes 196612
Sparse Core Ops, SparseCore 0:
  49.1 41.3 all-gather.2

commit v4 on v3

--- a/solution.py
+++ b/solution.py
@@ -129,10 +129,11 @@
     at[:, lanes] = pltpu.roll(window, shift, axis=1)
 
 
-def pack_kernel(cap, pivots, panel_t, trailing, out, triangle, rows, mine, sem):
+def pack_kernel(cap, pivots, panel_t, trailing, keep, send, triangle, rows, mine, sem):
     copy = pltpu.make_async_copy(trailing, rows, sem)
     copy.start()
     z = lax.axis_index("z")
+    c = lax.axis_index("c")
     first = first_row()
 
     def find(i, carry):
@@ -145,32 +146,54 @@
 
     _, found = lax.fori_loop(0, NB, find, (jnp.int32(0), jnp.int32(0)), unroll=16)
     invert_diagonal(panel_t, triangle)
-    for b in range(BLOCKS):
-        out[b, :cap, :] = jnp.zeros((cap, LANES), jnp.float32)
-        q, h = b // C, b % C
-        out[b, cap + NB :, :] = triangle[8 * q : 8 * q + 8, h * LANES : (h + 1) * LANES]
+    sides = ((keep, c), (send, 1 - c))
+    for out, side in sides:
+        for x in range(X):
+            out[x, :cap, :] = jnp.zeros((cap, LANES), jnp.float32)
+            lanes = pl.ds(pl.multiple_of(side * LANES, LANES), LANES)
+            out[x, cap + NB :, :] = triangle[8 * x : 8 * x + 8, lanes]
     copy.wait()
-    for b in range(BLOCKS):
-        out[b, cap : cap + NB, :] = rows[:NB, b * LANES : (b + 1) * LANES]
+    for out, side in sides:
+        for x in range(X):
+            lanes = pl.ds(pl.multiple_of((x * C + side) * LANES, LANES), LANES)
+            out[x, cap : cap + NB, :] = rows[:NB, lanes]
 
     def put(k):
         entry = mine[k]
-        values = load_row(rows, entry >> BITS)
+        row = entry >> BITS
         at = pl.ds(entry & (NB - 1), 1)
-        for b in range(BLOCKS):
-            out[b, at, :] = values[:, b * LANES : (b + 1) * LANES]
+        hit = picked(row, LANES)
+        for out, side in sides:
+            for x in range(X):
+                lanes = pl.ds(pl.multiple_of((x * C + side) * LANES, LANES), LANES)
+                tile = jnp.where(hit, rows[tile_of(row), lanes], 0.0)
+                out[x, at, :] = jnp.sum(tile, axis=0, keepdims=True)
 
     loop(found, put)
 
 
-def spread_kernel(cap, room, filler, place, tops, count, got, out):
-    for z in range(Z):
-        out[z, cap + room :, :] = got[0, cap + NB :, :]
-    rows = got[0, :cap, :]
-    for s in range(1, BLOCKS):
-        rows = rows + got[s, :cap, :]
+def join_kernel(cap, keep, got, *blocks):
+    x = lax.axis_index("x")
+    c = lax.axis_index("c")
+    for s, out in enumerate(blocks):
+        at = (x + s) & (X - 1)
+        out[:cap, :] = keep[at, :cap, :] + got[at, :cap, :]
+        out[cap:, :] = jnp.where(c == 0, keep[at, cap:, :], got[at, cap:, :])
+
+
+def spread_kernel(cap, room, filler, place, tops, count, *refs):
+    blocks, out, former = refs[:X], refs[-2], refs[-1]
+    x = lax.axis_index("x")
+    rest = blocks[0][cap:, :]
+    for s in range(1, X):
+        rest = jnp.where(x == s, blocks[s][cap:, :], rest)
+    former[...] = rest
+    rows = blocks[0][:cap, :]
+    for s in range(1, X):
+        rows = rows + blocks[s][:cap, :]
     for z in range(Z):
         out[z, :cap, :] = rows
+        out[z, cap + room :, :] = former[NB:, :]
 
     @pl.when(lax.axis_index("z") == 0)
     def _():
@@ -179,15 +202,14 @@
             for i in range(BATCH):
                 where = place[k * BATCH + i]
                 rank = jnp.minimum(where & (NB - 1), cap - 1)
-                values = got[0, pl.ds(cap + filler[k * BATCH + i], 1), :]
-                moves.append((where >> BITS, cap + rank, values))
+                moves.append((where >> BITS, cap + rank, former[pl.ds(filler[k * BATCH + i], 1), :]))
             for plane, at, values in moves:
                 out[plane, pl.ds(at, 1), :] = values
 
         loop(NB // BATCH, put)
 
         def top(k):
-            values = got[0, pl.ds(cap + (tops[k] & (NB - 1)), 1), :]
+            values = former[pl.ds(tops[k] & (NB - 1), 1), :]
             for z in range(Z):
                 out[z, pl.ds(cap + jnp.minimum(count[z] + k, room - 1), 1), :] = values
 
@@ -248,9 +270,8 @@
 
 
 def turn_kernel(whole_t, out):
-    c = lax.axis_index("c")
     for y in range(Y):
-        out[:, DIAG * y : DIAG * (y + 1)] = whole_t[y, c].T
+        out[:, DIAG * y : DIAG * (y + 1)] = whole_t[y].T
 
 
 def finish_kernel(cap, pivots, slot_of, count, own, other, multipliers, trailing, out,
@@ -303,29 +324,40 @@
 
 
 def call(kernel, shape, smem, vmem, scratch=(), name=None, last=VMEM, out=VMEM, busy=2):
-    return pl.pallas_call(
+    many = isinstance(shape, list)
+    shapes = shape if many else [shape]
+    got = pl.pallas_call(
         kernel,
-        out_shape=jax.ShapeDtypeStruct(shape, jnp.float32),
+        out_shape=[jax.ShapeDtypeStruct(s, jnp.float32) for s in shapes],
         in_specs=[SMEM] * len(smem) + [VMEM] * (len(vmem) - 1) + [last],
-        out_specs=out,
+        out_specs=[out] * len(shapes),
         scratch_shapes=list(scratch),
         compiler_params=PARAMS,
         cost_estimate=pl.CostEstimate(flops=0, bytes_accessed=busy * 2**20, transcendentals=0),
         name=name,
     )(*smem, *vmem)
+    return list(got) if many else got[0]
+
+
+ANY = pl.BlockSpec(memory_space=pl.ANY)
 
 
 def pack(cap, pivots, trailing, panel_t):
     scratch = [pltpu.VMEM((DIAG, NB), jnp.float32), pltpu.VMEM((ROWS, COLS), jnp.float32),
                pltpu.SMEM((NB + 8,), jnp.int32), pltpu.SemaphoreType.DMA]
-    return call(functools.partial(pack_kernel, cap), (BLOCKS, cap + NB + 8, LANES),
-                (pivots,), (panel_t, trailing), scratch, name="pack", last=pl.BlockSpec(memory_space=pl.ANY))
-
-
-def spread(cap, room, plan, packed):
+    return call(functools.partial(pack_kernel, cap), [(X, cap + NB + 8, LANES)] * 2,
+                (pivots,), (panel_t, trailing), scratch, name="pack", last=ANY)
+
+
+def join(cap, keep, got):
+    return call(functools.partial(join_kernel, cap), [keep.shape[1:]] * X, (), (keep, got), name="join")
+
+
+def spread(cap, room, plan, blocks, whole_t):
     filler, place, _, tops, count = plan
     return call(functools.partial(spread_kernel, cap, room), (Z, cap + room + 8, LANES),
-                (filler, place, tops, count), (packed,), name="spread")
+                (filler, place, tops, count), (*blocks, whole_t),
+                [pltpu.VMEM((NB + 8, LANES), jnp.float32)], name="spread", last=ANY)
 
 
 def collect(cap, room, plan, planes, pieces):
@@ -340,26 +372,35 @@
     scratch += [pltpu.SemaphoreType.DMA, pltpu.SemaphoreType.DMA((X,))]
     return call(functools.partial(finish_kernel, cap), (ROWS, COLS), (pivots, slot_of, count),
                 (own, other, multipliers, trailing), scratch, name="finish",
-                last=pl.BlockSpec(memory_space=pl.ANY), out=pl.BlockSpec(memory_space=pltpu.HBM), busy=16)
-
-
-def exchange(cap, room, panel_t, trailing, pivots, plan):
-    swap = functools.partial(lax.all_to_all, split_axis=0, concat_axis=0, tiled=True)
-    packed = swap(pack(cap, pivots, trailing, panel_t), ("x", "c"))
-    planes = swap(spread(cap, room, plan, packed), "z")
+                last=ANY, out=pl.BlockSpec(memory_space=pltpu.HBM), busy=16)
+
+
+swap = functools.partial(lax.all_to_all, split_axis=0, concat_axis=0, tiled=True)
+
+
+def other_core(values):
+    return lax.ppermute(values, "c", [(0, 1), (1, 0)])
+
+
+def exchange(cap, room, panel_t, trailing, pivots, plan, whole_t):
+    keep, send = pack(cap, pivots, trailing, panel_t)
+    blocks = join(cap, keep, other_core(send))
+    for s in range(1, X):
+        blocks[s] = lax.ppermute(blocks[s], "x", [(x, (x + s) % X) for x in range(X)])
+    planes = swap(spread(cap, room, plan, blocks, whole_t), "z")
     pieces = swap(jnp.broadcast_to(planes[:1, cap + room :], (Y, 8, LANES)), "y")
     own = swap(collect(cap, room, plan, planes, pieces), "x")
-    return own, lax.ppermute(own, "c", [(0, 1), (1, 0)])
+    return own, other_core(own)
 
 
 def shards(panel, trailing, pivots):
     panel_t = panel.T
-    whole_t = lax.all_gather(panel_t, ("y", "c"), axis=0).reshape(Y, C, DIAG, ROWS)
+    whole_t = swap(jnp.broadcast_to(panel_t[None], (Y, DIAG, ROWS)), "y")
     multipliers = call(turn_kernel, (ROWS, NB), (), (whole_t,), name="turn")
     *plan, most = make_plan(pivots)
 
     def with_room(cap, room):
-        ready = exchange(cap, room, panel_t, trailing, pivots, plan)
+        ready = exchange(cap, room, panel_t, trailing, pivots, plan, whole_t)
         return finish(cap, pivots, plan, *ready, multipliers, trailing)
 
     def pending(carry):

time: 117 us -> 106 us (0.906)
  waiting for transfers between devices: 31.3 us -> 2.06 us
  blocking collectives: 25.9 us -> 50.7 us
  between operations: 14.2 us -> 0.92 us
  starting transfers between devices: 20.2 us -> 27.7 us
  Pallas kernels: 23.9 us -> 22.6 us
    all_to_all x2 -> x1, waiting for transfers between devices: 30.6 us -> 0.01 us  [shards(): whole_t = swap(jnp.broadcast_to(panel_t[None], (Y, DIAG, ROWS)), 'y')]
    all_to_all x0 -> x1, blocking collectives: none -> 25 us  [exchange(): planes = swap(spread(cap, room, plan, blocks, whole_t), 'z')]
    ppermute x1 -> x5, starting transfers between devices: 5.18 us -> 20 us  [the longest x2 11.3 us: other_core(): return lax.ppermute(values, 'c', [(0, 1), (1, 0)])]
    all_to_all x2 -> x1, starting transfers between devices: 15 us -> 7.78 us  [shards(): whole_t = swap(jnp.broadcast_to(panel_t[None], (Y, DIAG, ROWS)), 'y')]
    ppermute x1 -> x5, waiting for transfers between devices: 0.01 us -> 2.06 us  [the longest x2 1.96 us: other_core(): return lax.ppermute(values, 'c', [(0, 1), (1, 0)])]
    broadcast_in_dim x0 -> x1, local copies, waits for them, and re-layouts: none -> 1.69 us  [shards(): whole_t = swap(jnp.broadcast_to(panel_t[None], (Y, DIAG, ROWS)), 'y')]
    pallas_call x5 -> x6, Pallas kernels: 18.3 us -> 17 us  [call(): pl.pallas_call(kernel, out_shape=[jax.ShapeDtypeStruct(s, jnp.float32) fo...]
    unnamed x8 -> x6, local copies, waits for them, and re-layouts: 1.24 us -> 0.01 us
  transfers between devices with their start and end apart: 4 -> 6, of which waited for: 2 -> 3; matrix products, arithmetic and copies ran while one was open for 0% -> 0% of each run, Pallas kernels for 7% -> 9%
where the time goes in v4:
time: 106 us
  blocking collectives  50.7 us (48%)
  starting transfers between devices  27.7 us (26%)
  Pallas kernels  22.6 us (21%)
  waiting for transfers between devices  2.06 us (2%)
  local copies, waits for them, and re-layouts  1.71 us (2%)
    all_to_all x1, blocking collectives, exchange(): planes = swap(spread(cap, room, plan, blocks, whole_t), 'z')  25 us
    pallas_call x6, Pallas kernels, call(): pl.pallas_call(kernel, out_shape=[jax.ShapeDtypeStruct(s, jnp.float32) fo...  17 us
    all_to_all x1, blocking collectives, exchange(): pieces = swap(jnp.broadcast_to(planes[:1, cap + room:], (Y, 8, LANES)), 'y')  13.7 us
    all_to_all x1, blocking collectives, exchange(): own = swap(collect(cap, room, plan, planes, pieces), 'x')  11.9 us
    ppermute x2, starting transfers between devices, other_core(): return lax.ppermute(values, 'c', [(0, 1), (1, 0)])  11.3 us
    ppermute x3, starting transfers between devices, exchange(): lax.ppermute(blocks[s], 'x', [(x, (x + s) % X) for x in range(X)])  8.62 us
    all_to_all x1, starting transfers between devices, shards(): whole_t = swap(jnp.broadcast_to(panel_t[None], (Y, DIAG, ROWS)), 'y')  7.78 us
    pallas_call x1, Pallas kernels, make_plan(): pl.pallas_call(plan_kernel, out_shape=[jax.ShapeDtypeStruct((n,), jnp.int...  5.59 us
  transfers between devices with their start and end apart: 6, of which 3 were waited for; matrix products, arithmetic and copies ran while one was open for 0% of the time, Pallas kernels for 9%

profile of v4, /device:TPU:1, one launch (start us, length us, event | category | flops | bytes accessed | tf_op | source)
XLA Modules:
  0.0 106.0 jit_solution(15664709532499502696)
XLA Ops:
  0.0 1.7 %broadcast_in_dim.20 = f32[8,32,512]{2,1,0:T(8,128)} broadcast(f32[32,512]{1,0:T(8,128)} %bitcast.6), dimensions={1,2} | broadcast | bytes 589824 | tf_op jit(solution)/shard_map/broadcast_in_dim | solution.py:398
  1.7 7.8 %all-to-all-start.3 = ((f32[8,32,512]{2,1,0:T(8,128)}), f32[8,32,512]{2,1,0:T(8,128)S(1)}, u32[]{:S(2)}, u32[]{:S(2)}) async-start(f32[8,32,512]{2,1,0:T(8,128)} %broadcast_in_dim.20), calls=%async_computation.3 | async-start | bytes 1048576 | tf_op jit(solution)/shard_map/all_to_all | solution.py:398
  9.5 3.2 %pack.3 = (f32[4,328,128]{2,1,0:T(8,128)S(1)}, f32[4,328,128]{2,1,0:T(8,128)S(1)}) custom-call(s32[256]{0:T(256)} %pivots.5, f32[32,512]{1,0:T(8,128)} %bitcast.7, f32[512,1024]{1,0:T(8,128)} %trailing.3), custom_call_target="tpu_custom_call" | custom-call | bytes 2097152 | tf_op jit(solution)/shard_map/pack/pallas_call | solution.py:329
  12.7 4.6 %collective-permute-start.5 = (f32[4,328,128]{2,1,0:T(8,128)S(1)}, f32[4,328,128]{2,1,0:T(8,128)S(1)}, u32[]{:S(2)}, u32[]{:S(2)}) collective-permute-start(f32[4,328,128]{2,1,0:T(8,128)S(1)} %get-tuple-element.90), channel_id=1, source_target_pairs={{0,8},{8,0},{1,9},{9,1},{2,10},{10,2},{3,11},{11,3},{4,12},{12,4},... | collective-permute-start | bytes 2015240 | tf_op jit(solution)/shard_map/ppermute | solution.py:382
  17.2 1.7 %collective-permute-done.5.got = f32[4,328,128]{2,1,0:T(8,128)S(1)} collective-permute-done((f32[4,328,128]{2,1,0:T(8,128)S(1)}, f32[4,328,128]{2,1,0:T(8,128)S(1)}, u32[]{:S(2)}, u32[]{:S(2)}) %collective-permute-start.5) | collective-permute-done | bytes 671776 | tf_op jit(solution)/shard_map/ppermute | solution.py:382
  19.0 0.1 join.3
  19.0 1.9 %collective-permute-start.6 = (f32[328,128]{1,0:T(8,128)S(1)}, f32[328,128]{1,0:T(8,128)S(1)}, u32[]{:S(2)}, u32[]{:S(2)}) collective-permute-start(f32[328,128]{1,0:T(8,128)S(1)} %get-tuple-element.92), channel_id=1, source_target_pairs={{0,128},{128,256},{256,384},{384,0},{1,129},{129,257},{257,385},{3... | collective-permute-start | bytes 503816 | tf_op jit(solution)/shard_map/ppermute | solution.py:389
  21.0 3.7 %collective-permute-start.7 = (f32[328,128]{1,0:T(8,128)S(1)}, f32[328,128]{1,0:T(8,128)S(1)}, u32[]{:S(2)}, u32[]{:S(2)}) collective-permute-start(f32[328,128]{1,0:T(8,128)S(1)} %get-tuple-element.93), channel_id=1, source_target_pairs={{0,256},{128,384},{256,0},{384,128},{1,257},{129,385},{257,1},{385... | collective-permute-start | bytes 503816 | tf_op jit(solution)/shard_map/ppermute | solution.py:389
  24.7 3.0 %collective-permute-start.8 = (f32[328,128]{1,0:T(8,128)S(1)}, f32[328,128]{1,0:T(8,128)S(1)}, u32[]{:S(2)}, u32[]{:S(2)}) collective-permute-start(f32[328,128]{1,0:T(8,128)S(1)} %get-tuple-element.94), channel_id=1, source_target_pairs={{0,384},{128,0},{256,128},{384,256},{1,385},{129,1},{257,129},{385... | collective-permute-start | bytes 503816 | tf_op jit(solution)/shard_map/ppermute | solution.py:389
  27.7 5.6 %plan.1 = (s32[256]{0:T(256)S(1)}, s32[256]{0:T(256)S(1)}, s32[2048]{0:T(1024)S(1)}, s32[264]{0:T(512)S(1)}, s32[9]{0:T(128)S(1)}, /*index=5*/s32[1]{0:T(128)}) custom-call(s32[256]{0:T(256)S(1)} %copy-done.3), custom_call_target="tpu_custom_call" | custom-call | bytes 16777216 | tf_op jit(solution)/shard_map/plan/pallas_call | solution.py:104
  33.3 0.0 collective-permute-done.6.refs_1_
  33.3 0.0 collective-permute-done.7.refs_2_
  33.3 0.1 collective-permute-done.8.refs_3_
  33.4 0.0 all-to-all-done.3.refs_4_.whole_t
  33.4 1.5 %spread.3 = f32[8,136,128]{2,1,0:T(8,128)S(1)} custom-call(s32[256]{0:T(256)S(1)} %get-tuple-element.137.filler, s32[256]{0:T(256)S(1)} %get-tuple-element.138.place, s32[264]{0:T(512)S(1)} %get-tuple-element.139.tops, s32[9]{0:T(128)S(1)} %get-tuple-element.140.count, f32[328,128]{1,0:T(8,128)S(1)} %get-tuple-element.91.refs_0_, ...), custom_call_target="tpu_custom_call" | custom-call | bytes 2097152 | tf_op jit(solution)/shard_map/spread/pallas_call | solution.py:329
  34.9 25.0 %all_to_all.35.got = f32[8,136,128]{2,1,0:T(8,128)S(1)} all-to-all(f32[8,136,128]{2,1,0:T(8,128)S(1)} %spread.3), channel_id=1, replica_groups=mesh['x'=4,'z'=8,'c'=2,'y'=8] {'z'}, dimensions={0} | all-to-all | bytes 1114112 | tf_op jit(solution)/shard_map/all_to_all | solution.py:390
  60.0 13.7 %all_to_all.36.pieces = f32[8,8,128]{2,1,0:T(8,128)S(1)} all-to-all(f32[8,8,128]{2,1,0:T(8,128)S(1)} %broadcast_in_dim.22), channel_id=1, replica_groups=mesh['x'=4,'z'=8,'c'=2,'y'=8] {'y'}, dimensions={0} | all-to-all | bytes 65536 | tf_op jit(solution)/shard_map/all_to_all | solution.py:391
  73.7 1.3 %collect.3 = f32[4,384,128]{2,1,0:T(8,128)S(1)} custom-call(s32[256]{0:T(256)S(1)} %get-tuple-element.138.place, s32[264]{0:T(512)S(1)} %get-tuple-element.139.tops, s32[9]{0:T(128)S(1)} %get-tuple-element.140.count, f32[8,136,128]{2,1,0:T(8,128)S(1)} %all_to_all.35.got, f32[8,8,128]{2,1,0:T(8,128)S(1)} %all_to_all.36.pieces), custom_call_target="tpu_custom_call" | custom-call | bytes 2097152 | tf_op jit(solution)/shard_map/collect/pallas_call | solution.py:329
  75.1 11.9 %all_to_all.37.own = f32[4,384,128]{2,1,0:T(8,128)S(1)} all-to-all(f32[4,384,128]{2,1,0:T(8,128)S(1)} %collect.3), channel_id=1, replica_groups=mesh['x'=4,'z'=8,'c'=2,'y'=8] {'x'}, dimensions={0} | all-to-all | bytes 1572864 | tf_op jit(solution)/shard_map/all_to_all | solution.py:392
  87.0 6.8 %collective-permute-start.9 = (f32[4,384,128]{2,1,0:T(8,128)S(1)}, f32[4,384,128]{2,1,0:T(8,128)S(1)}, u32[]{:S(2)}, u32[]{:S(2)}) collective-permute-start(f32[4,384,128]{2,1,0:T(8,128)S(1)} %all_to_all.37.own), channel_id=1, source_target_pairs={{0,8},{8,0},{1,9},{9,1},{2,10},{10,2},{3,11},{11,3},{4,12},{12,4},... | collective-permute-start | bytes 2359304 | tf_op jit(solution)/shard_map/ppermute | solution.py:382
  94.4 1.0 turn.1.multipliers
  95.5 0.2 collective-permute-done.9.other
  95.7 9.9 %finish.3 = f32[512,1024]{1,0:T(8,128)} custom-call(s32[256]{0:T(256)S(1)} %copy-done.3, s32[2048]{0:T(1024)S(1)} %get-tuple-element.142.slot_of, s32[9]{0:T(128)S(1)} %get-tuple-element.140.count, f32[4,384,128]{2,1,0:T(8,128)S(1)} %all_to_all.37.own, f32[4,384,128]{2,1,0:T(8,128)S(1)} %collective-permute-done.9.other, f32[512,256]{1,0:T(8,128)S(1)} %turn.1.multipliers, ...), custom_call_target="tpu_custom_call" | custom-call | bytes 16777216 | tf_op jit(solution)/shard_map/finish/pallas_call | solution.py:329
  105.6 0.2 while.9
  (8 shorter events, 0.0 us)
Async XLA Ops:
  1.7 26.0 %copy-start.3 = (s32[256]{0:T(256)S(1)}, s32[256]{0:T(256)}, u32[]{:S(2)}) copy-start(s32[256]{0:T(256)} %pivots.5) | copy-start | bytes 3076
  1.7 31.7 %all-to-all-start.3 = ((f32[8,32,512]{2,1,0:T(8,128)}), f32[8,32,512]{2,1,0:T(8,128)S(1)}, u32[]{:S(2)}, u32[]{:S(2)}) async-start(f32[8,32,512]{2,1,0:T(8,128)} %broadcast_in_dim.20), calls=%async_computation.3 | async-start | bytes 1048576 | tf_op jit(solution)/shard_map/all_to_all | solution.py:398
  12.7 6.3 %collective-permute-start.5 = (f32[4,328,128]{2,1,0:T(8,128)S(1)}, f32[4,328,128]{2,1,0:T(8,128)S(1)}, u32[]{:S(2)}, u32[]{:S(2)}) collective-permute-start(f32[4,328,128]{2,1,0:T(8,128)S(1)} %get-tuple-element.90), channel_id=1, source_target_pairs={{0,8},{8,0},{1,9},{9,1},{2,10},{10,2},{3,11},{11,3},{4,12},{12,4},... | collective-permute-start | bytes 2015240 | tf_op jit(solution)/shard_map/ppermute | solution.py:382
  19.0 14.3 %collective-permute-start.6 = (f32[328,128]{1,0:T(8,128)S(1)}, f32[328,128]{1,0:T(8,128)S(1)}, u32[]{:S(2)}, u32[]{:S(2)}) collective-permute-start(f32[328,128]{1,0:T(8,128)S(1)} %get-tuple-element.92), channel_id=1, source_target_pairs={{0,128},{128,256},{256,384},{384,0},{1,129},{129,257},{257,385},{3... | collective-permute-start | bytes 503816 | tf_op jit(solution)/shard_map/ppermute | solution.py:389
  21.0 12.3 %collective-permute-start.7 = (f32[328,128]{1,0:T(8,128)S(1)}, f32[328,128]{1,0:T(8,128)S(1)}, u32[]{:S(2)}, u32[]{:S(2)}) collective-permute-start(f32[328,128]{1,0:T(8,128)S(1)} %get-tuple-element.93), channel_id=1, source_target_pairs={{0,256},{128,384},{256,0},{384,128},{1,257},{129,385},{257,1},{385... | collective-permute-start | bytes 503816 | tf_op jit(solution)/shard_map/ppermute | solution.py:389
  24.7 8.8 %collective-permute-start.8 = (f32[328,128]{1,0:T(8,128)S(1)}, f32[328,128]{1,0:T(8,128)S(1)}, u32[]{:S(2)}, u32[]{:S(2)}) collective-permute-start(f32[328,128]{1,0:T(8,128)S(1)} %get-tuple-element.94), channel_id=1, source_target_pairs={{0,384},{128,0},{256,128},{384,256},{1,385},{129,1},{257,129},{385... | collective-permute-start | bytes 503816 | tf_op jit(solution)/shard_map/ppermute | solution.py:389
  60.0 35.7 %copy-start = (f32[512,1024]{1,0:T(8,128)S(1)}, f32[512,1024]{1,0:T(8,128)}, u32[]{:S(2)}) copy-start(f32[512,1024]{1,0:T(8,128)} %trailing.3) | copy-start | bytes 6291460
  87.0 8.7 %collective-permute-start.9 = (f32[4,384,128]{2,1,0:T(8,128)S(1)}, f32[4,384,128]{2,1,0:T(8,128)S(1)}, u32[]{:S(2)}, u32[]{:S(2)}) collective-permute-start(f32[4,384,128]{2,1,0:T(8,128)S(1)} %all_to_all.37.own), channel_id=1, source_target_pairs={{0,8},{8,0},{1,9},{9,1},{2,10},{10,2},{3,11},{11,3},{4,12},{12,4},... | collective-permute-start | bytes 2359304 | tf_op jit(solution)/shard_map/ppermute | solution.py:382
  95.7 9.9 %copy-start.2 = (f32[512,32]{0,1:T(8,128)S(1)}, f32[512,32]{0,1:T(8,128)}, u32[]{:S(2)}) copy-start(f32[512,32]{0,1:T(8,128)} %param.5) | copy-start | bytes 196612

commit v5 on v4

--- a/solution.py
+++ b/solution.py
@@ -18,10 +18,11 @@
 BATCH = 16
 BITS = NB.bit_length() - 1
 PLANE_BITS = (ROWS * C).bit_length() - 1
-NARROW = 64
+NARROW = 56
 HIGHEST = lax.Precision.HIGHEST
 VMEM = pl.BlockSpec(memory_space=pltpu.VMEM)
 SMEM = pl.BlockSpec(memory_space=pltpu.SMEM)
+ANY = pl.BlockSpec(memory_space=pl.ANY)
 PARAMS = pltpu.CompilerParams(vmem_limit_bytes=48 * 1024 * 1024)
 
 
@@ -99,17 +100,29 @@
     most[0] = peak + found
 
 
-def make_plan(pivots):
+def early_plan_kernel(*refs):
+    @pl.when(lax.axis_index("z") == 0)
+    def _():
+        plan_kernel(*refs)
+
+
+def late_plan_kernel(pivots, after, *refs):
+    plan_kernel(pivots, *refs)
+
+
+def make_plan(pivots, after=None):
     sizes = (NB, NB, Z * NB, NB + 8, Z + 1, 1)
+    early = after is None
     return pl.pallas_call(
-        plan_kernel,
+        early_plan_kernel if early else late_plan_kernel,
         out_shape=[jax.ShapeDtypeStruct((n,), jnp.int32) for n in sizes],
-        in_specs=[SMEM],
+        in_specs=[SMEM] if early else [SMEM, VMEM],
         out_specs=[SMEM] * len(sizes),
         scratch_shapes=[pltpu.SMEM((ORDER,), jnp.int32)],
+        compiler_params=PARAMS,
         cost_estimate=pl.CostEstimate(flops=0, bytes_accessed=16 * 1024 * 1024, transcendentals=0),
         name="plan",
-    )(pivots)
+    )(*([pivots] if early else [pivots, after]))
 
 
 def invert_diagonal(panel_t, at):
@@ -129,7 +142,7 @@
     at[:, lanes] = pltpu.roll(window, shift, axis=1)
 
 
-def pack_kernel(cap, pivots, panel_t, trailing, keep, send, triangle, rows, mine, sem):
+def pack_kernel(cap, pivots, panel_t, trailing, keep, send, mine, triangle, rows, sem):
     copy = pltpu.make_async_copy(trailing, rows, sem)
     copy.start()
     z = lax.axis_index("z")
@@ -170,6 +183,7 @@
                 out[x, at, :] = jnp.sum(tile, axis=0, keepdims=True)
 
     loop(found, put)
+    mine[NB] = found
 
 
 def join_kernel(cap, keep, got, *blocks):
@@ -214,6 +228,11 @@
                 out[z, pl.ds(cap + jnp.minimum(count[z] + k, room - 1), 1), :] = values
 
         loop(count[Z], top)
+
+
+def pieces_kernel(count, got, out):
+    for y in range(Y):
+        out[y] = got[0, got.shape[1] - 8 :, :]
 
 
 def collect_kernel(cap, room, place, tops, count, got, pieces, out):
@@ -269,17 +288,21 @@
     return jnp.concatenate([left, right], axis=1)
 
 
+def repeat_kernel(values, out):
+    for y in range(Y):
+        out[y] = values[...]
+
+
 def turn_kernel(whole_t, out):
     for y in range(Y):
         out[:, DIAG * y : DIAG * (y + 1)] = whole_t[y].T
 
 
-def finish_kernel(cap, pivots, slot_of, count, own, other, multipliers, trailing, out,
+def finish_kernel(cap, mine, own, other, multipliers, trailing, out,
                   upper, inverse, block, current, in_sem, out_sem):
     copy = pltpu.make_async_copy(trailing, current, in_sem)
     copy.start()
     c = lax.axis_index("c")
-    z = lax.axis_index("z")
     first = first_row()
     sides = ((pl.multiple_of(c * LANES, LANES), own), (pl.multiple_of((1 - c) * LANES, LANES), other))
     for x in range(X):
@@ -290,19 +313,18 @@
     inverse[...] = invert(upper)
     copy.wait()
 
-    def put(r):
-        local = pivots[slot_of[z * NB + r]] - first
-
-        @pl.when((local >= 0) & (local < ROWS))
-        def _():
-            at = tile_of(local)
-            hit = picked(local, LANES)
-            for x in range(X):
-                for lane, ref in sides:
-                    lanes = pl.ds(pl.multiple_of(x * C * LANES + lane, LANES), LANES)
-                    current[at, lanes] = jnp.where(hit, ref[x, pl.ds(NB + r, 1), :], current[at, lanes])
-
-    loop(jnp.minimum(count[z], cap), put)
+    def put(k):
+        entry = mine[k]
+        row = entry >> BITS
+        rank = pl.ds(NB + (entry & (NB - 1)), 1)
+        at = tile_of(row)
+        hit = picked(row, LANES)
+        for x in range(X):
+            for lane, ref in sides:
+                lanes = pl.ds(pl.multiple_of(x * C * LANES + lane, LANES), LANES)
+                current[at, lanes] = jnp.where(hit, ref[x, rank, :], current[at, lanes])
+
+    loop(mine[NB], put)
     copies = []
     width = C * LANES
     for x in range(X):
@@ -323,14 +345,18 @@
         copy.wait()
 
 
-def call(kernel, shape, smem, vmem, scratch=(), name=None, last=VMEM, out=VMEM, busy=2):
+def call(kernel, shape, smem, vmem, scratch=(), name=None, last=VMEM, out=VMEM, busy=2, table=None):
     many = isinstance(shape, list)
-    shapes = shape if many else [shape]
+    shapes = [jax.ShapeDtypeStruct(s, jnp.float32) for s in (shape if many else [shape])]
+    specs = [out] * len(shapes)
+    if table is not None:
+        shapes.append(jax.ShapeDtypeStruct((table,), jnp.int32))
+        specs.append(SMEM)
     got = pl.pallas_call(
         kernel,
-        out_shape=[jax.ShapeDtypeStruct(s, jnp.float32) for s in shapes],
+        out_shape=shapes,
         in_specs=[SMEM] * len(smem) + [VMEM] * (len(vmem) - 1) + [last],
-        out_specs=[out] * len(shapes),
+        out_specs=specs,
         scratch_shapes=list(scratch),
         compiler_params=PARAMS,
         cost_estimate=pl.CostEstimate(flops=0, bytes_accessed=busy * 2**20, transcendentals=0),
@@ -339,14 +365,10 @@
     return list(got) if many else got[0]
 
 
-ANY = pl.BlockSpec(memory_space=pl.ANY)
-
-
 def pack(cap, pivots, trailing, panel_t):
-    scratch = [pltpu.VMEM((DIAG, NB), jnp.float32), pltpu.VMEM((ROWS, COLS), jnp.float32),
-               pltpu.SMEM((NB + 8,), jnp.int32), pltpu.SemaphoreType.DMA]
+    scratch = [pltpu.VMEM((DIAG, NB), jnp.float32), pltpu.VMEM((ROWS, COLS), jnp.float32), pltpu.SemaphoreType.DMA]
     return call(functools.partial(pack_kernel, cap), [(X, cap + NB + 8, LANES)] * 2,
-                (pivots,), (panel_t, trailing), scratch, name="pack", last=ANY)
+                (pivots,), (panel_t, trailing), scratch, name="pack", last=ANY, table=NB + 8)
 
 
 def join(cap, keep, got):
@@ -357,7 +379,7 @@
     filler, place, _, tops, count = plan
     return call(functools.partial(spread_kernel, cap, room), (Z, cap + room + 8, LANES),
                 (filler, place, tops, count), (*blocks, whole_t),
-                [pltpu.VMEM((NB + 8, LANES), jnp.float32)], name="spread", last=ANY)
+                [pltpu.VMEM((NB + 8, LANES), jnp.float32)], name="spread")
 
 
 def collect(cap, room, plan, planes, pieces):
@@ -366,11 +388,10 @@
                 (place, tops, count), (planes, pieces), name="collect")
 
 
-def finish(cap, pivots, plan, own, other, multipliers, trailing):
-    _, _, slot_of, _, count = plan
+def finish(cap, mine, own, other, multipliers, trailing):
     scratch = [pltpu.VMEM(s, jnp.float32) for s in ((NB, NB), (NB, NB), (X, NB, C * LANES), (ROWS, COLS))]
     scratch += [pltpu.SemaphoreType.DMA, pltpu.SemaphoreType.DMA((X,))]
-    return call(functools.partial(finish_kernel, cap), (ROWS, COLS), (pivots, slot_of, count),
+    return call(functools.partial(finish_kernel, cap), (ROWS, COLS), (mine,),
                 (own, other, multipliers, trailing), scratch, name="finish",
                 last=ANY, out=pl.BlockSpec(memory_space=pltpu.HBM), busy=16)
 
@@ -382,34 +403,40 @@
     return lax.ppermute(values, "c", [(0, 1), (1, 0)])
 
 
-def exchange(cap, room, panel_t, trailing, pivots, plan, whole_t):
-    keep, send = pack(cap, pivots, trailing, panel_t)
+def first_phase(cap, room, panel_t, trailing, pivots, whole_t):
+    keep, send, mine = pack(cap, pivots, trailing, panel_t)
     blocks = join(cap, keep, other_core(send))
     for s in range(1, X):
         blocks[s] = lax.ppermute(blocks[s], "x", [(x, (x + s) % X) for x in range(X)])
-    planes = swap(spread(cap, room, plan, blocks, whole_t), "z")
-    pieces = swap(jnp.broadcast_to(planes[:1, cap + room :], (Y, 8, LANES)), "y")
+    plan = make_plan(pivots)
+    return spread(cap, room, plan[:-1], blocks, whole_t), mine
+
+
+def later_phases(cap, room, planes, plan):
+    planes = swap(planes, "z")
+    pieces = swap(call(pieces_kernel, (Y, 8, LANES), (plan[-1],), (planes,), name="pieces"), "y")
     own = swap(collect(cap, room, plan, planes, pieces), "x")
     return own, other_core(own)
 
 
 def shards(panel, trailing, pivots):
     panel_t = panel.T
-    whole_t = swap(jnp.broadcast_to(panel_t[None], (Y, DIAG, ROWS)), "y")
+    whole_t = swap(call(repeat_kernel, (Y, DIAG, ROWS), (), (panel_t,), name="repeat"), "y")
     multipliers = call(turn_kernel, (ROWS, NB), (), (whole_t,), name="turn")
-    *plan, most = make_plan(pivots)
-
-    def with_room(cap, room):
-        ready = exchange(cap, room, panel_t, trailing, pivots, plan, whole_t)
-        return finish(cap, pivots, plan, *ready, multipliers, trailing)
+    planes, mine = first_phase(NARROW, NARROW, panel_t, trailing, pivots, whole_t)
+    *plan, most = make_plan(pivots, planes)
+    ready = later_phases(NARROW, NARROW, planes, plan)
+    result = finish(NARROW, mine, *ready, multipliers, trailing)
 
     def pending(carry):
         return carry[0]
 
     def again(carry):
-        return jnp.zeros_like(carry[0]), with_room(NB, 2 * NB)
-
-    return lax.while_loop(pending, again, (most[0] > NARROW, with_room(NARROW, NARROW)))[1]
+        planes, mine = first_phase(NB, 2 * NB, panel_t, trailing, pivots, whole_t)
+        ready = later_phases(NB, 2 * NB, planes, plan)
+        return jnp.zeros_like(carry[0]), finish(NB, mine, *ready, multipliers, trailing)
+
+    return lax.while_loop(pending, again, (most[0] > NARROW, result))[1]
 
 
 def solution(mesh):

time: 106 us -> 107 us (level)
  blocking collectives: 50.7 us -> 30.5 us
  Pallas kernels: 22.6 us -> 31.2 us
  waiting for transfers between devices: 2.06 us -> 10.3 us
  starting transfers between devices: 27.7 us -> 33.4 us
  local copies, waits for them, and re-layouts: 1.71 us -> 0.01 us
    all_to_all x3 -> x2, blocking collectives: 50.7 us -> 30.5 us  [the longest x1 16.8 us: later_phases(): own = swap(collect(cap, room, plan, planes, pieces), 'x')]
    pallas_call x7 -> x10, Pallas kernels: 22.6 us -> 31.2 us  [the longest x8 19.4 us: call(): pl.pallas_call(kernel, out_shape=shapes, in_specs=[SMEM] * len(smem) + [V...]
    all_to_all x1 -> x2, waiting for transfers between devices: 0.01 us -> 8.45 us  [the longest x1 8.45 us: later_phases(): planes = swap(planes, 'z')]
    all_to_all x1 -> x2, starting transfers between devices: 7.78 us -> 15 us  [the longest x1 7.78 us: shards(): swap(call(repeat_kernel, (Y, DIAG, ROWS), (), (panel_t,), name='repeat'),...]
    broadcast_in_dim x3 -> x0, local copies, waits for them, and re-layouts: 1.7 us -> none  [the longest x1 1.69 us: shards(): whole_t = swap(jnp.broadcast_to(panel_t[None], (Y, DIAG, ROWS)), 'y')]
    ppermute x2, starting transfers between devices: 11.3 us -> 9.73 us  [other_core(): return lax.ppermute(values, 'c', [(0, 1), (1, 0)])]
  transfers between devices with their start and end apart: 6 -> 7, of which waited for: 3 -> 3; matrix products, arithmetic and copies ran while one was open for 0% -> 0% of each run, Pallas kernels for 9% -> 15%
where the time goes in v5:
time: 107 us
  starting transfers between devices  33.4 us (31%)
  Pallas kernels  31.2 us (29%)
  blocking collectives  30.5 us (29%)
  waiting for transfers between devices  10.3 us (10%)
    pallas_call x8, Pallas kernels, call(): pl.pallas_call(kernel, out_shape=shapes, in_specs=[SMEM] * len(smem) + [V...  19.4 us
    all_to_all x1, blocking collectives, later_phases(): own = swap(collect(cap, room, plan, planes, pieces), 'x')  16.8 us
    all_to_all x1, blocking collectives, later_phases(): swap(call(pieces_kernel, (Y, 8, LANES), (plan[-1],), (planes,), name='pie...  13.7 us
    pallas_call x2, Pallas kernels, make_plan(): pl.pallas_call(early_plan_kernel if early else late_plan_kernel, out_shap...  11.7 us
    ppermute x2, starting transfers between devices, other_core(): return lax.ppermute(values, 'c', [(0, 1), (1, 0)])  9.73 us
    ppermute x3, starting transfers between devices, first_phase(): lax.ppermute(blocks[s], 'x', [(x, (x + s) % X) for x in range(X)])  8.72 us
    all_to_all x1, waiting for transfers between devices, later_phases(): planes = swap(planes, 'z')  8.45 us
    all_to_all x1, starting transfers between devices, shards(): swap(call(repeat_kernel, (Y, DIAG, ROWS), (), (panel_t,), name='repeat'),...  7.78 us
  transfers between devices with their start and end apart: 7, of which 3 were waited for; matrix products, arithmetic and copies ran while one was open for 0% of the time, Pallas kernels for 15%

profile of v5, /device:TPU:1, one launch (start us, length us, event | category | flops | bytes accessed | tf_op | source)
XLA Modules:
  0.0 106.6 jit_solution(7374241009677189420)
XLA Ops:
  0.0 1.7 %repeat.1 = f32[8,32,512]{2,1,0:T(8,128)} custom-call(f32[32,512]{1,0:T(8,128)} %bitcast.2), custom_call_target="tpu_custom_call" | custom-call | bytes 2097152 | tf_op jit(solution)/shard_map/repeat/pallas_call | solution.py:355
  1.7 7.8 %all-to-all-start.3 = ((f32[8,32,512]{2,1,0:T(8,128)}), f32[8,32,512]{2,1,0:T(8,128)S(1)}, u32[]{:S(2)}, u32[]{:S(2)}) async-start(f32[8,32,512]{2,1,0:T(8,128)} %repeat.1), calls=%async_computation.3 | async-start | bytes 1048576 | tf_op jit(solution)/shard_map/all_to_all | solution.py:424
  9.5 3.7 %pack.3 = (f32[4,320,128]{2,1,0:T(8,128)S(1)}, f32[4,320,128]{2,1,0:T(8,128)S(1)}, s32[264]{0:T(512)S(1)}) custom-call(s32[256]{0:T(256)} %pivots.3, f32[32,512]{1,0:T(8,128)} %bitcast.3, f32[512,1024]{1,0:T(8,128)} %trailing.3), custom_call_target="tpu_custom_call" | custom-call | bytes 2097152 | tf_op jit(solution)/shard_map/pack/pallas_call | solution.py:355
  13.1 4.7 %collective-permute-start.5 = (f32[4,320,128]{2,1,0:T(8,128)S(1)}, f32[4,320,128]{2,1,0:T(8,128)S(1)}, u32[]{:S(2)}, u32[]{:S(2)}) collective-permute-start(f32[4,320,128]{2,1,0:T(8,128)S(1)} %get-tuple-element.86), channel_id=1, source_target_pairs={{0,8},{8,0},{1,9},{9,1},{2,10},{10,2},{3,11},{11,3},{4,12},{12,4},... | collective-permute-start | bytes 1966088 | tf_op jit(solution)/shard_map/ppermute | solution.py:403
  17.8 1.7 %collective-permute-done.5.got = f32[4,320,128]{2,1,0:T(8,128)S(1)} collective-permute-done((f32[4,320,128]{2,1,0:T(8,128)S(1)}, f32[4,320,128]{2,1,0:T(8,128)S(1)}, u32[]{:S(2)}, u32[]{:S(2)}) %collective-permute-start.5) | collective-permute-done | bytes 655392 | tf_op jit(solution)/shard_map/ppermute | solution.py:403
  19.5 0.1 join.3
  19.6 1.9 %collective-permute-start.6 = (f32[320,128]{1,0:T(8,128)S(1)}, f32[320,128]{1,0:T(8,128)S(1)}, u32[]{:S(2)}, u32[]{:S(2)}) collective-permute-start(f32[320,128]{1,0:T(8,128)S(1)} %get-tuple-element.88), channel_id=1, source_target_pairs={{0,128},{128,256},{256,384},{384,0},{1,129},{129,257},{257,385},{3... | collective-permute-start | bytes 491528 | tf_op jit(solution)/shard_map/ppermute | solution.py:410
  21.5 3.7 %collective-permute-start.7 = (f32[320,128]{1,0:T(8,128)S(1)}, f32[320,128]{1,0:T(8,128)S(1)}, u32[]{:S(2)}, u32[]{:S(2)}) collective-permute-start(f32[320,128]{1,0:T(8,128)S(1)} %get-tuple-element.89), channel_id=1, source_target_pairs={{0,256},{128,384},{256,0},{384,128},{1,257},{129,385},{257,1},{385... | collective-permute-start | bytes 491528 | tf_op jit(solution)/shard_map/ppermute | solution.py:410
  25.2 3.1 %collective-permute-start.8 = (f32[320,128]{1,0:T(8,128)S(1)}, f32[320,128]{1,0:T(8,128)S(1)}, u32[]{:S(2)}, u32[]{:S(2)}) collective-permute-start(f32[320,128]{1,0:T(8,128)S(1)} %get-tuple-element.90), channel_id=1, source_target_pairs={{0,384},{128,0},{256,128},{384,256},{1,385},{129,1},{257,129},{385... | collective-permute-start | bytes 491528 | tf_op jit(solution)/shard_map/ppermute | solution.py:410
  28.4 5.6 %plan.4 = (s32[256]{0:T(256)S(1)}, s32[256]{0:T(256)S(1)}, s32[2048]{0:T(1024)}, s32[264]{0:T(512)S(1)}, s32[9]{0:T(128)S(1)}, /*index=5*/s32[1]{0:T(128)}) custom-call(s32[256]{0:T(256)S(1)} %copy-done.3), custom_call_target="tpu_custom_call" | custom-call | bytes 16777216 | tf_op jit(solution)/shard_map/plan/pallas_call | solution.py:116
  34.0 2.3 %spread.3.after = f32[8,120,128]{2,1,0:T(8,128)} custom-call(s32[256]{0:T(256)S(1)} %get-tuple-element.81.filler, s32[256]{0:T(256)S(1)} %get-tuple-element.82.place, s32[264]{0:T(512)S(1)} %get-tuple-element.83.tops, s32[9]{0:T(128)S(1)} %get-tuple-element.84.count, f32[320,128]{1,0:T(8,128)S(1)} %get-tuple-element.87.refs_0_, ...), custom_call_target="tpu_custom_call" | custom-call | bytes 2097152 | tf_op jit(solution)/shard_map/spread/pallas_call | solution.py:355
  36.3 7.2 %all-to-all-start.4 = ((f32[8,120,128]{2,1,0:T(8,128)}), f32[8,120,128]{2,1,0:T(8,128)S(1)}, u32[]{:S(2)}, u32[]{:S(2)}) async-start(f32[8,120,128]{2,1,0:T(8,128)} %spread.3.after), calls=%async_computation.4 | async-start | bytes 983040 | tf_op jit(solution)/shard_map/all_to_all | solution.py:416
  43.4 6.1 %plan.5 = (s32[256]{0:T(256)}, s32[256]{0:T(256)S(1)}, s32[2048]{0:T(1024)}, s32[264]{0:T(512)S(1)}, s32[9]{0:T(128)S(1)}, /*index=5*/s32[1]{0:T(128)}) custom-call(s32[256]{0:T(256)S(1)} %copy-done.3, f32[8,120,128]{2,1,0:T(8,128)} %spread.3.after), custom_call_target="tpu_custom_call" | custom-call | bytes 16777216 | tf_op jit(solution)/shard_map/plan/pallas_call | solution.py:116
  49.6 8.5 %all-to-all-done.4.got = f32[8,120,128]{2,1,0:T(8,128)S(1)} async-done(((f32[8,120,128]{2,1,0:T(8,128)}), f32[8,120,128]{2,1,0:T(8,128)S(1)}, u32[]{:S(2)}, u32[]{:S(2)}) %all-to-all-start.4) | async-done | bytes 491552 | tf_op jit(solution)/shard_map/all_to_all | solution.py:416
  58.0 0.5 pieces.3
  58.6 0.0 copy-start
  58.6 13.7 %all_to_all.35.pieces = f32[8,8,128]{2,1,0:T(8,128)S(1)} all-to-all(f32[8,8,128]{2,1,0:T(8,128)S(1)} %pieces.3), channel_id=1, replica_groups=mesh['x'=4,'z'=8,'c'=2,'y'=8] {'y'}, dimensions={0} | all-to-all | bytes 65536 | tf_op jit(solution)/shard_map/all_to_all | solution.py:417
  72.3 1.3 %collect.3 = f32[4,376,128]{2,1,0:T(8,128)S(1)} custom-call(s32[256]{0:T(256)S(1)} %get-tuple-element.134.place, s32[264]{0:T(512)S(1)} %get-tuple-element.135.tops, s32[9]{0:T(128)S(1)} %get-tuple-element.133.count, f32[8,120,128]{2,1,0:T(8,128)S(1)} %all-to-all-done.4.got, f32[8,8,128]{2,1,0:T(8,128)S(1)} %all_to_all.35.pieces), custom_call_target="tpu_custom_call" | custom-call | bytes 2097152 | tf_op jit(solution)/shard_map/collect/pallas_call | solution.py:355
  73.7 16.8 %all_to_all.36.own = f32[4,376,128]{2,1,0:T(8,128)S(1)} all-to-all(f32[4,376,128]{2,1,0:T(8,128)S(1)} %collect.3), channel_id=1, replica_groups=mesh['x'=4,'z'=8,'c'=2,'y'=8] {'x'}, dimensions={0} | all-to-all | bytes 1540096 | tf_op jit(solution)/shard_map/all_to_all | solution.py:418
  90.5 5.0 %collective-permute-start.9 = (f32[4,376,128]{2,1,0:T(8,128)S(1)}, f32[4,376,128]{2,1,0:T(8,128)S(1)}, u32[]{:S(2)}, u32[]{:S(2)}) collective-permute-start(f32[4,376,128]{2,1,0:T(8,128)S(1)} %all_to_all.36.own), channel_id=1, source_target_pairs={{0,8},{8,0},{1,9},{9,1},{2,10},{10,2},{3,11},{11,3},{4,12},{12,4},... | collective-permute-start | bytes 2310152 | tf_op jit(solution)/shard_map/ppermute | solution.py:403
  96.2 1.0 turn.1.multipliers
  97.2 0.2 collective-permute-done.9.other
  97.4 8.9 %finish.3 = f32[512,1024]{1,0:T(8,128)} custom-call(s32[264]{0:T(512)S(1)} %get-tuple-element.92.mine, f32[4,376,128]{2,1,0:T(8,128)S(1)} %all_to_all.36.own, f32[4,376,128]{2,1,0:T(8,128)S(1)} %collective-permute-done.9.other, f32[512,256]{1,0:T(8,128)S(1)} %turn.1.multipliers, f32[512,1024]{1,0:T(8,128)S(1)} %copy-done), custom_call_target="tpu_custom_call" | custom-call | bytes 16777216 | tf_op jit(solution)/shard_map/finish/pallas_call | solution.py:355
  106.3 0.2 while.9
  (9 shorter events, 0.0 us)
Async XLA Ops:
  1.7 26.7 %copy-start.3 = (s32[256]{0:T(256)S(1)}, s32[256]{0:T(256)}, u32[]{:S(2)}) copy-start(s32[256]{0:T(256)} %pivots.3) | copy-start | bytes 3076
  1.7 32.3 %all-to-all-start.3 = ((f32[8,32,512]{2,1,0:T(8,128)}), f32[8,32,512]{2,1,0:T(8,128)S(1)}, u32[]{:S(2)}, u32[]{:S(2)}) async-start(f32[8,32,512]{2,1,0:T(8,128)} %repeat.1), calls=%async_computation.3 | async-start | bytes 1048576 | tf_op jit(solution)/shard_map/all_to_all | solution.py:424
  13.1 6.4 %collective-permute-start.5 = (f32[4,320,128]{2,1,0:T(8,128)S(1)}, f32[4,320,128]{2,1,0:T(8,128)S(1)}, u32[]{:S(2)}, u32[]{:S(2)}) collective-permute-start(f32[4,320,128]{2,1,0:T(8,128)S(1)} %get-tuple-element.86), channel_id=1, source_target_pairs={{0,8},{8,0},{1,9},{9,1},{2,10},{10,2},{3,11},{11,3},{4,12},{12,4},... | collective-permute-start | bytes 1966088 | tf_op jit(solution)/shard_map/ppermute | solution.py:403
  19.6 14.4 %collective-permute-start.6 = (f32[320,128]{1,0:T(8,128)S(1)}, f32[320,128]{1,0:T(8,128)S(1)}, u32[]{:S(2)}, u32[]{:S(2)}) collective-permute-start(f32[320,128]{1,0:T(8,128)S(1)} %get-tuple-element.88), channel_id=1, source_target_pairs={{0,128},{128,256},{256,384},{384,0},{1,129},{129,257},{257,385},{3... | collective-permute-start | bytes 491528 | tf_op jit(solution)/shard_map/ppermute | solution.py:410
  21.5 12.4 %collective-permute-start.7 = (f32[320,128]{1,0:T(8,128)S(1)}, f32[320,128]{1,0:T(8,128)S(1)}, u32[]{:S(2)}, u32[]{:S(2)}) collective-permute-start(f32[320,128]{1,0:T(8,128)S(1)} %get-tuple-element.89), channel_id=1, source_target_pairs={{0,256},{128,384},{256,0},{384,128},{1,257},{129,385},{257,1},{385... | collective-permute-start | bytes 491528 | tf_op jit(solution)/shard_map/ppermute | solution.py:410
  25.2 8.7 %collective-permute-start.8 = (f32[320,128]{1,0:T(8,128)S(1)}, f32[320,128]{1,0:T(8,128)S(1)}, u32[]{:S(2)}, u32[]{:S(2)}) collective-permute-start(f32[320,128]{1,0:T(8,128)S(1)} %get-tuple-element.90), channel_id=1, source_target_pairs={{0,384},{128,0},{256,128},{384,256},{1,385},{129,1},{257,129},{385... | collective-permute-start | bytes 491528 | tf_op jit(solution)/shard_map/ppermute | solution.py:410
  36.3 21.7 %all-to-all-start.4 = ((f32[8,120,128]{2,1,0:T(8,128)}), f32[8,120,128]{2,1,0:T(8,128)S(1)}, u32[]{:S(2)}, u32[]{:S(2)}) async-start(f32[8,120,128]{2,1,0:T(8,128)} %spread.3.after), calls=%async_computation.4 | async-start | bytes 983040 | tf_op jit(solution)/shard_map/all_to_all | solution.py:416
  58.6 38.8 %copy-start = (f32[512,1024]{1,0:T(8,128)S(1)}, f32[512,1024]{1,0:T(8,128)}, u32[]{:S(2)}) copy-start(f32[512,1024]{1,0:T(8,128)} %trailing.3) | copy-start | bytes 6291460
  90.5 6.9 %collective-permute-start.9 = (f32[4,376,128]{2,1,0:T(8,128)S(1)}, f32[4,376,128]{2,1,0:T(8,128)S(1)}, u32[]{:S(2)}, u32[]{:S(2)}) collective-permute-start(f32[4,376,128]{2,1,0:T(8,128)S(1)} %all_to_all.36.own), channel_id=1, source_target_pairs={{0,8},{8,0},{1,9},{9,1},{2,10},{10,2},{3,11},{11,3},{4,12},{12,4},... | collective-permute-start | bytes 2310152 | tf_op jit(solution)/shard_map/ppermute | solution.py:403
  97.4 8.9 %copy-start.2 = (f32[512,32]{0,1:T(8,128)S(1)}, f32[512,32]{0,1:T(8,128)}, u32[]{:S(2)}) copy-start(f32[512,32]{0,1:T(8,128)} %param.5) | copy-start | bytes 196612

commit v6 on v5

--- a/solution.py
+++ b/solution.py
@@ -16,6 +16,7 @@
 COLS = BLOCKS * LANES
 DIAG = NB // Y
 BATCH = 16
+DISTANCES = (4, 2, 1)
 BITS = NB.bit_length() - 1
 PLANE_BITS = (ROWS * C).bit_length() - 1
 NARROW = 56
@@ -230,12 +231,12 @@
         loop(count[Z], top)
 
 
-def pieces_kernel(count, got, out):
+def pieces_kernel(count, slices, got, out):
     for y in range(Y):
         out[y] = got[0, got.shape[1] - 8 :, :]
 
 
-def collect_kernel(cap, room, place, tops, count, got, pieces, out):
+def collect_kernel(cap, room, place, tops, count, slices, got, pieces, out):
     z = lax.axis_index("z")
 
     def take(k):
@@ -288,14 +289,25 @@
     return jnp.concatenate([left, right], axis=1)
 
 
-def repeat_kernel(values, out):
-    for y in range(Y):
-        out[y] = values[...]
-
-
-def turn_kernel(whole_t, out):
-    for y in range(Y):
-        out[:, DIAG * y : DIAG * (y + 1)] = whole_t[y].T
+def later_kernel(values, after, out):
+    out[...] = values[...]
+
+
+def double_kernel(first, second, out):
+    half = first.shape[0]
+    out[:half] = first[...]
+    out[half:] = second[...]
+
+
+def turn_kernel(slices, out, ordered):
+    y = lax.axis_index("y")
+    columns = [y]
+    for distance in DISTANCES:
+        columns += [column ^ distance for column in columns]
+    for k, column in enumerate(columns):
+        at = pl.ds(pl.multiple_of(column * DIAG, DIAG), DIAG)
+        ordered[at, :] = slices[k * DIAG : (k + 1) * DIAG, :]
+    out[...] = ordered[...].T
 
 
 def finish_kernel(cap, mine, own, other, multipliers, trailing, out,
@@ -375,17 +387,17 @@
     return call(functools.partial(join_kernel, cap), [keep.shape[1:]] * X, (), (keep, got), name="join")
 
 
-def spread(cap, room, plan, blocks, whole_t):
+def spread(cap, room, plan, blocks):
     filler, place, _, tops, count = plan
     return call(functools.partial(spread_kernel, cap, room), (Z, cap + room + 8, LANES),
-                (filler, place, tops, count), (*blocks, whole_t),
+                (filler, place, tops, count), blocks,
                 [pltpu.VMEM((NB + 8, LANES), jnp.float32)], name="spread")
 
 
-def collect(cap, room, plan, planes, pieces):
+def collect(cap, room, plan, planes, pieces, slices):
     _, place, _, tops, count = plan
     return call(functools.partial(collect_kernel, cap, room), (X, NB + cap + 8 * Y, LANES),
-                (place, tops, count), (planes, pieces), name="collect")
+                (place, tops, count), (slices, planes, pieces), name="collect")
 
 
 def finish(cap, mine, own, other, multipliers, trailing):
@@ -403,38 +415,51 @@
     return lax.ppermute(values, "c", [(0, 1), (1, 0)])
 
 
-def first_phase(cap, room, panel_t, trailing, pivots, whole_t):
+def first_phase(cap, room, panel_t, trailing, pivots):
     keep, send, mine = pack(cap, pivots, trailing, panel_t)
     blocks = join(cap, keep, other_core(send))
     for s in range(1, X):
         blocks[s] = lax.ppermute(blocks[s], "x", [(x, (x + s) % X) for x in range(X)])
     plan = make_plan(pivots)
-    return spread(cap, room, plan[:-1], blocks, whole_t), mine
-
-
-def later_phases(cap, room, planes, plan):
+    return spread(cap, room, plan[:-1], blocks), mine
+
+
+def from_column(values, distance):
+    return lax.ppermute(values, "y", [(y, y ^ distance) for y in range(Y)])
+
+
+def doubled(slices, distance):
+    shape = (2 * slices.shape[0], ROWS)
+    return call(double_kernel, shape, (), (slices, from_column(slices, distance)), name="double")
+
+
+def later_phases(cap, room, planes, plan, panel_t):
+    slices = call(later_kernel, panel_t.shape, (), (panel_t, planes), name="later")
+    slices = doubled(slices, DISTANCES[0])
     planes = swap(planes, "z")
-    pieces = swap(call(pieces_kernel, (Y, 8, LANES), (plan[-1],), (planes,), name="pieces"), "y")
-    own = swap(collect(cap, room, plan, planes, pieces), "x")
-    return own, other_core(own)
+    pieces = call(pieces_kernel, (Y, 8, LANES), (plan[-1],), (slices, planes), name="pieces")
+    slices = doubled(slices, DISTANCES[1])
+    blocks = collect(cap, room, plan, planes, swap(pieces, "y"), slices)
+    slices = doubled(slices, DISTANCES[2])
+    multipliers = call(turn_kernel, (ROWS, NB), (), (slices,), [pltpu.VMEM((NB, ROWS), jnp.float32)], name="turn")
+    own, multipliers = lax.optimization_barrier((swap(blocks, "x"), multipliers))
+    return own, other_core(own), multipliers
 
 
 def shards(panel, trailing, pivots):
     panel_t = panel.T
-    whole_t = swap(call(repeat_kernel, (Y, DIAG, ROWS), (), (panel_t,), name="repeat"), "y")
-    multipliers = call(turn_kernel, (ROWS, NB), (), (whole_t,), name="turn")
-    planes, mine = first_phase(NARROW, NARROW, panel_t, trailing, pivots, whole_t)
+    planes, mine = first_phase(NARROW, NARROW, panel_t, trailing, pivots)
     *plan, most = make_plan(pivots, planes)
-    ready = later_phases(NARROW, NARROW, planes, plan)
-    result = finish(NARROW, mine, *ready, multipliers, trailing)
+    ready = later_phases(NARROW, NARROW, planes, plan, panel_t)
+    result = finish(NARROW, mine, *ready, trailing)
 
     def pending(carry):
         return carry[0]
 
     def again(carry):
-        planes, mine = first_phase(NB, 2 * NB, panel_t, trailing, pivots, whole_t)
-        ready = later_phases(NB, 2 * NB, planes, plan)
-        return jnp.zeros_like(carry[0]), finish(NB, mine, *ready, multipliers, trailing)
+        planes, mine = first_phase(NB, 2 * NB, panel_t, trailing, pivots)
+        ready = later_phases(NB, 2 * NB, planes, plan, panel_t)
+        return jnp.zeros_like(carry[0]), finish(NB, mine, *ready, trailing)
 
     return lax.while_loop(pending, again, (most[0] > NARROW, result))[1]
 

time: 107 us -> 103 us (0.963)
  blocking collectives: 30.5 us -> 0 us
  starting transfers between devices: 33.4 us -> 52.3 us
  waiting for transfers between devices: 10.3 us -> 17.4 us
    all_to_all x2 -> x0, blocking collectives: 30.5 us -> none  [the longest x1 16.8 us: later_phases(): own = swap(collect(cap, room, plan, planes, pieces), 'x')]
    ppermute x0 -> x3, starting transfers between devices: none -> 14.3 us  [from_column(): return lax.ppermute(values, 'y', [(y, y ^ distance) for y in range(Y)])]
    all_to_all x1, waiting for transfers between devices: 8.45 us -> 0.01 us  [later_phases(): planes = swap(planes, 'z')]
    all_to_all x1 -> x2, waiting for transfers between devices: 0.01 us -> 7.42 us  [the longest x1 6.84 us: later_phases(): blocks = collect(cap, room, plan, planes, swap(pieces, 'y'), slices)]
    ppermute x0 -> x3, waiting for transfers between devices: none -> 6.92 us  [from_column(): return lax.ppermute(values, 'y', [(y, y ^ distance) for y in range(Y)])]
    ppermute x2, starting transfers between devices: 9.73 us -> 15.9 us  [other_core(): return lax.ppermute(values, 'c', [(0, 1), (1, 0)])]
    all_to_all x1, starting transfers between devices: 7.17 us -> 3.91 us  [later_phases(): planes = swap(planes, 'z')]
    all_to_all x1 -> x2, starting transfers between devices: 7.78 us -> 9.74 us  [the longest x1 4.92 us: later_phases(): swap(blocks, 'x')]
  transfers between devices with their start and end apart: 7 -> 11, of which waited for: 3 -> 7; matrix products, arithmetic and copies ran while one was open for 0% -> 0% of each run, Pallas kernels for 15% -> 14%
where the time goes in v6:
time: 103 us; the launch traced here: 102 us
  starting transfers between devices  52.3 us (51%)
  Pallas kernels  31.4 us (30%)
  waiting for transfers between devices  17.4 us (17%)
    pallas_call x11, Pallas kernels, call(): pl.pallas_call(kernel, out_shape=shapes, in_specs=[SMEM] * len(smem) + [V...  19.7 us
    ppermute x2, starting transfers between devices, other_core(): return lax.ppermute(values, 'c', [(0, 1), (1, 0)])  15.9 us
    ppermute x3, starting transfers between devices, from_column(): return lax.ppermute(values, 'y', [(y, y ^ distance) for y in range(Y)])  14.3 us
    pallas_call x2, Pallas kernels, make_plan(): pl.pallas_call(early_plan_kernel if early else late_plan_kernel, out_shap...  11.7 us
    ppermute x3, starting transfers between devices, first_phase(): lax.ppermute(blocks[s], 'x', [(x, (x + s) % X) for x in range(X)])  8.41 us
    ppermute x3, waiting for transfers between devices, from_column(): return lax.ppermute(values, 'y', [(y, y ^ distance) for y in range(Y)])  6.92 us
    all_to_all x1, waiting for transfers between devices, later_phases(): blocks = collect(cap, room, plan, planes, swap(pieces, 'y'), slices)  6.84 us
    all_to_all x1, starting transfers between devices, later_phases(): swap(blocks, 'x')  4.92 us
  transfers between devices with their start and end apart: 11, of which 7 were waited for; matrix products, arithmetic and copies ran while one was open for 0% of the time, Pallas kernels for 14%

profile of v6, /device:TPU:1, one launch (start us, length us, event | category | flops | bytes accessed | tf_op | source)
XLA Modules:
  0.0 102.3 jit_solution(6711833471988842315)
XLA Ops:
  0.0 3.6 %pack.3 = (f32[4,320,128]{2,1,0:T(8,128)S(1)}, f32[4,320,128]{2,1,0:T(8,128)S(1)}, s32[264]{0:T(512)S(1)}) custom-call(s32[256]{0:T(256)} %pivots.3, f32[32,512]{1,0:T(8,128)} %bitcast.2, f32[512,1024]{1,0:T(8,128)} %trailing.3), custom_call_target="tpu_custom_call" | custom-call | bytes 2097152 | tf_op jit(solution)/shard_map/pack/pallas_call | solution.py:367
  3.7 8.9 %collective-permute-start.8 = (f32[4,320,128]{2,1,0:T(8,128)S(1)}, f32[4,320,128]{2,1,0:T(8,128)S(1)}, u32[]{:S(2)}, u32[]{:S(2)}) collective-permute-start(f32[4,320,128]{2,1,0:T(8,128)S(1)} %get-tuple-element.80), channel_id=1, source_target_pairs={{0,8},{8,0},{1,9},{9,1},{2,10},{10,2},{3,11},{11,3},{4,12},{12,4},... | collective-permute-start | bytes 1966088 | tf_op jit(solution)/shard_map/ppermute | solution.py:415
  12.6 1.7 %collective-permute-done.8.got = f32[4,320,128]{2,1,0:T(8,128)S(1)} collective-permute-done((f32[4,320,128]{2,1,0:T(8,128)S(1)}, f32[4,320,128]{2,1,0:T(8,128)S(1)}, u32[]{:S(2)}, u32[]{:S(2)}) %collective-permute-start.8) | collective-permute-done | bytes 655392 | tf_op jit(solution)/shard_map/ppermute | solution.py:415
  14.3 1.9 %collective-permute-start.9 = (f32[320,128]{1,0:T(8,128)S(1)}, f32[320,128]{1,0:T(8,128)S(1)}, u32[]{:S(2)}, u32[]{:S(2)}) collective-permute-start(f32[320,128]{1,0:T(8,128)S(1)} %get-tuple-element.82), channel_id=1, source_target_pairs={{0,128},{128,256},{256,384},{384,0},{1,129},{129,257},{257,385},{3... | collective-permute-start | bytes 491528 | tf_op jit(solution)/shard_map/ppermute | solution.py:422
  16.3 1.9 %collective-permute-start.10 = (f32[320,128]{1,0:T(8,128)S(1)}, f32[320,128]{1,0:T(8,128)S(1)}, u32[]{:S(2)}, u32[]{:S(2)}) collective-permute-start(f32[320,128]{1,0:T(8,128)S(1)} %get-tuple-element.83), channel_id=1, source_target_pairs={{0,256},{128,384},{256,0},{384,128},{1,257},{129,385},{257,1},{385... | collective-permute-start | bytes 491528 | tf_op jit(solution)/shard_map/ppermute | solution.py:422
  18.2 4.6 %collective-permute-start.11 = (f32[320,128]{1,0:T(8,128)S(1)}, f32[320,128]{1,0:T(8,128)S(1)}, u32[]{:S(2)}, u32[]{:S(2)}) collective-permute-start(f32[320,128]{1,0:T(8,128)S(1)} %get-tuple-element.84), channel_id=1, source_target_pairs={{0,384},{128,0},{256,128},{384,256},{1,385},{129,1},{257,129},{385... | collective-permute-start | bytes 491528 | tf_op jit(solution)/shard_map/ppermute | solution.py:422
  22.8 5.6 %plan.4 = (s32[256]{0:T(256)S(1)}, s32[256]{0:T(256)S(1)}, s32[2048]{0:T(1024)}, s32[264]{0:T(512)S(1)}, s32[9]{0:T(128)S(1)}, /*index=5*/s32[1]{0:T(128)}) custom-call(s32[256]{0:T(256)S(1)} %copy-done.8), custom_call_target="tpu_custom_call" | custom-call | bytes 16777216 | tf_op jit(solution)/shard_map/plan/pallas_call | solution.py:117
  28.5 2.3 %spread.3.after = f32[8,120,128]{2,1,0:T(8,128)} custom-call(s32[256]{0:T(256)S(1)} %get-tuple-element.75.filler, s32[256]{0:T(256)S(1)} %get-tuple-element.76.place, s32[264]{0:T(512)S(1)} %get-tuple-element.77.tops, s32[9]{0:T(128)S(1)} %get-tuple-element.78.count, f32[320,128]{1,0:T(8,128)S(1)} %get-tuple-element.81.refs_0_, ...), custom_call_target="tpu_custom_call" | custom-call | bytes 2097152 | tf_op jit(solution)/shard_map/spread/pallas_call | solution.py:367
  30.8 3.9 %all-to-all-start.3 = ((f32[8,120,128]{2,1,0:T(8,128)}), f32[8,120,128]{2,1,0:T(8,128)S(1)}, u32[]{:S(2)}, u32[]{:S(2)}) async-start(f32[8,120,128]{2,1,0:T(8,128)} %spread.3.after), calls=%async_computation.3 | async-start | bytes 983040 | tf_op jit(solution)/shard_map/all_to_all | solution.py:439
  34.7 1.1 %later.3.first = f32[32,512]{1,0:T(8,128)S(1)} custom-call(f32[32,512]{1,0:T(8,128)S(1)} %bitcast.3, f32[8,120,128]{2,1,0:T(8,128)} %spread.3.after), custom_call_target="tpu_custom_call" | custom-call | bytes 2097152 | tf_op jit(solution)/shard_map/later/pallas_call | solution.py:367
  35.8 7.4 %collective-permute-start.12 = (f32[32,512]{1,0:T(8,128)S(1)}, f32[32,512]{1,0:T(8,128)S(1)}, u32[]{:S(2)}, u32[]{:S(2)}) collective-permute-start(f32[32,512]{1,0:T(8,128)S(1)} %later.3.first), channel_id=1, source_target_pairs={{0,4},{1,5},{2,6},{3,7},{4,0},{5,1},{6,2},{7,3},{8,12},{9,13},{10,... | collective-permute-start | bytes 196616 | tf_op jit(solution)/shard_map/ppermute | solution.py:428
  43.2 1.7 %collective-permute-done.12.second = f32[32,512]{1,0:T(8,128)S(1)} collective-permute-done((f32[32,512]{1,0:T(8,128)S(1)}, f32[32,512]{1,0:T(8,128)S(1)}, u32[]{:S(2)}, u32[]{:S(2)}) %collective-permute-start.12) | collective-permute-done | bytes 65568 | tf_op jit(solution)/shard_map/ppermute | solution.py:428
  44.9 4.7 %collective-permute-start.13 = (f32[64,512]{1,0:T(8,128)S(1)}, f32[64,512]{1,0:T(8,128)S(1)}, u32[]{:S(2)}, u32[]{:S(2)}) collective-permute-start(f32[64,512]{1,0:T(8,128)S(1)} %double.9.first.slices), channel_id=1, source_target_pairs={{0,2},{1,3},{2,0},{3,1},{4,6},{5,7},{6,4},{7,5},{8,10},{9,11},{10,... | collective-permute-start | bytes 393224 | tf_op jit(solution)/shard_map/ppermute | solution.py:428
  49.7 6.1 %plan.5 = (s32[256]{0:T(256)}, s32[256]{0:T(256)S(1)}, s32[2048]{0:T(1024)}, s32[264]{0:T(512)S(1)}, s32[9]{0:T(128)S(1)}, /*index=5*/s32[1]{0:T(128)}) custom-call(s32[256]{0:T(256)S(1)} %copy-done.8, f32[8,120,128]{2,1,0:T(8,128)} %spread.3.after), custom_call_target="tpu_custom_call" | custom-call | bytes 16777216 | tf_op jit(solution)/shard_map/plan/pallas_call | solution.py:117
  55.8 1.2 %pieces.3 = f32[8,8,128]{2,1,0:T(8,128)} custom-call(s32[9]{0:T(128)S(1)} %get-tuple-element.122.count, f32[64,512]{1,0:T(8,128)S(1)} %double.9.first.slices, f32[8,120,128]{2,1,0:T(8,128)S(1)} %all-to-all-done.3.got), custom_call_target="tpu_custom_call" | custom-call | bytes 2097152 | tf_op jit(solution)/shard_map/pieces/pallas_call | solution.py:367
  56.9 4.8 %all-to-all-start.4 = ((f32[8,8,128]{2,1,0:T(8,128)}), f32[8,8,128]{2,1,0:T(8,128)S(1)}, u32[]{:S(2)}, u32[]{:S(2)}) async-start(f32[8,8,128]{2,1,0:T(8,128)} %pieces.3), calls=%async_computation.4 | async-start | bytes 65536 | tf_op jit(solution)/shard_map/all_to_all | solution.py:442
  61.8 6.8 %all-to-all-done.4.pieces = f32[8,8,128]{2,1,0:T(8,128)S(1)} async-done(((f32[8,8,128]{2,1,0:T(8,128)}), f32[8,8,128]{2,1,0:T(8,128)S(1)}, u32[]{:S(2)}, u32[]{:S(2)}) %all-to-all-start.4) | async-done | bytes 32800 | tf_op jit(solution)/shard_map/all_to_all | solution.py:442
  68.6 2.2 %collect.3 = f32[4,376,128]{2,1,0:T(8,128)} custom-call(s32[256]{0:T(256)S(1)} %get-tuple-element.123.place, s32[264]{0:T(512)S(1)} %get-tuple-element.124.tops, s32[9]{0:T(128)S(1)} %get-tuple-element.122.count, f32[128,512]{1,0:T(8,128)S(1)} %double.10.slices.first, f32[8,120,128]{2,1,0:T(8,128)S(1)} %all-to-all-done.3.got, ...), custom_call_target="tpu_custom_call" | custom-call | bytes 2097152 | tf_op jit(solution)/shard_map/collect/pallas_call | solution.py:367
  70.9 4.9 %all-to-all-start.5 = ((f32[4,376,128]{2,1,0:T(8,128)}), f32[4,376,128]{2,1,0:T(8,128)S(1)}, u32[]{:S(2)}, u32[]{:S(2)}) async-start(f32[4,376,128]{2,1,0:T(8,128)} %collect.3), calls=%async_computation.5 | async-start | bytes 1540096 | tf_op jit(solution)/shard_map/all_to_all | solution.py:445
  75.8 2.2 %collective-permute-start.14 = (f32[128,512]{1,0:T(8,128)S(1)}, f32[128,512]{1,0:T(8,128)S(1)}, u32[]{:S(2)}, u32[]{:S(2)}) collective-permute-start(f32[128,512]{1,0:T(8,128)S(1)} %double.10.slices.first), channel_id=1, source_target_pairs={{0,1},{1,0},{2,3},{3,2},{4,5},{5,4},{6,7},{7,6},{8,9},{9,8},{10,11... | collective-permute-start | bytes 786440 | tf_op jit(solution)/shard_map/ppermute | solution.py:428
  78.0 5.2 %collective-permute-done.14.second = f32[128,512]{1,0:T(8,128)S(1)} collective-permute-done((f32[128,512]{1,0:T(8,128)S(1)}, f32[128,512]{1,0:T(8,128)S(1)}, u32[]{:S(2)}, u32[]{:S(2)}) %collective-permute-start.14) | collective-permute-done | bytes 262176 | tf_op jit(solution)/shard_map/ppermute | solution.py:428
  84.0 7.0 %collective-permute-start.15 = (f32[4,376,128]{2,1,0:T(8,128)S(1)}, f32[4,376,128]{2,1,0:T(8,128)S(1)}, u32[]{:S(2)}, u32[]{:S(2)}) collective-permute-start(f32[4,376,128]{2,1,0:T(8,128)S(1)} %all-to-all-done.5.own), channel_id=1, source_target_pairs={{0,8},{8,0},{1,9},{9,1},{2,10},{10,2},{3,11},{11,3},{4,12},{12,4},... | collective-permute-start | bytes 2310152 | tf_op jit(solution)/shard_map/ppermute | solution.py:415
  91.7 1.2 %collective-permute-done.15.other = f32[4,376,128]{2,1,0:T(8,128)S(1)} collective-permute-done((f32[4,376,128]{2,1,0:T(8,128)S(1)}, f32[4,376,128]{2,1,0:T(8,128)S(1)}, u32[]{:S(2)}, u32[]{:S(2)}) %collective-permute-start.15) | collective-permute-done | bytes 770080 | tf_op jit(solution)/shard_map/ppermute | solution.py:415
  92.9 9.0 %finish.3 = f32[512,1024]{1,0:T(8,128)} custom-call(s32[264]{0:T(512)S(1)} %get-tuple-element.86.mine, f32[4,376,128]{2,1,0:T(8,128)S(1)} %all-to-all-done.5.own, f32[4,376,128]{2,1,0:T(8,128)S(1)} %collective-permute-done.15.other, f32[512,256]{1,0:T(8,128)S(1)} %turn.3.multipliers, f32[512,1024]{1,0:T(8,128)} %trailing.3), custom_call_target="tpu_custom_call" | custom-call | bytes 16777216 | tf_op jit(solution)/shard_map/finish/pallas_call | solution.py:367
  (18 shorter events, 1.3 us)
Async XLA Ops:
  0.0 22.8 %copy-start.8 = (s32[256]{0:T(256)S(1)}, s32[256]{0:T(256)}, u32[]{:S(2)}) copy-start(s32[256]{0:T(256)} %pivots.3) | copy-start | bytes 3076
  3.7 31.1 %copy-start.7 = (f32[512,32]{0,1:T(8,128)S(1)}, f32[512,32]{0,1:T(8,128)}, u32[]{:S(2)}) copy-start(f32[512,32]{0,1:T(8,128)} %param.5) | copy-start | bytes 196612
  3.7 10.6 %collective-permute-start.8 = (f32[4,320,128]{2,1,0:T(8,128)S(1)}, f32[4,320,128]{2,1,0:T(8,128)S(1)}, u32[]{:S(2)}, u32[]{:S(2)}) collective-permute-start(f32[4,320,128]{2,1,0:T(8,128)S(1)} %get-tuple-element.80), channel_id=1, source_target_pairs={{0,8},{8,0},{1,9},{9,1},{2,10},{10,2},{3,11},{11,3},{4,12},{12,4},... | collective-permute-start | bytes 1966088 | tf_op jit(solution)/shard_map/ppermute | solution.py:415
  14.3 14.1 %collective-permute-start.9 = (f32[320,128]{1,0:T(8,128)S(1)}, f32[320,128]{1,0:T(8,128)S(1)}, u32[]{:S(2)}, u32[]{:S(2)}) collective-permute-start(f32[320,128]{1,0:T(8,128)S(1)} %get-tuple-element.82), channel_id=1, source_target_pairs={{0,128},{128,256},{256,384},{384,0},{1,129},{129,257},{257,385},{3... | collective-permute-start | bytes 491528 | tf_op jit(solution)/shard_map/ppermute | solution.py:422
  16.3 12.1 %collective-permute-start.10 = (f32[320,128]{1,0:T(8,128)S(1)}, f32[320,128]{1,0:T(8,128)S(1)}, u32[]{:S(2)}, u32[]{:S(2)}) collective-permute-start(f32[320,128]{1,0:T(8,128)S(1)} %get-tuple-element.83), channel_id=1, source_target_pairs={{0,256},{128,384},{256,0},{384,128},{1,257},{129,385},{257,1},{385... | collective-permute-start | bytes 491528 | tf_op jit(solution)/shard_map/ppermute | solution.py:422
  18.2 10.3 %collective-permute-start.11 = (f32[320,128]{1,0:T(8,128)S(1)}, f32[320,128]{1,0:T(8,128)S(1)}, u32[]{:S(2)}, u32[]{:S(2)}) collective-permute-start(f32[320,128]{1,0:T(8,128)S(1)} %get-tuple-element.84), channel_id=1, source_target_pairs={{0,384},{128,0},{256,128},{384,256},{1,385},{129,1},{257,129},{385... | collective-permute-start | bytes 491528 | tf_op jit(solution)/shard_map/ppermute | solution.py:422
  30.8 25.0 %all-to-all-start.3 = ((f32[8,120,128]{2,1,0:T(8,128)}), f32[8,120,128]{2,1,0:T(8,128)S(1)}, u32[]{:S(2)}, u32[]{:S(2)}) async-start(f32[8,120,128]{2,1,0:T(8,128)} %spread.3.after), calls=%async_computation.3 | async-start | bytes 983040 | tf_op jit(solution)/shard_map/all_to_all | solution.py:439
  35.8 9.2 %collective-permute-start.12 = (f32[32,512]{1,0:T(8,128)S(1)}, f32[32,512]{1,0:T(8,128)S(1)}, u32[]{:S(2)}, u32[]{:S(2)}) collective-permute-start(f32[32,512]{1,0:T(8,128)S(1)} %later.3.first), channel_id=1, source_target_pairs={{0,4},{1,5},{2,6},{3,7},{4,0},{5,1},{6,2},{7,3},{8,12},{9,13},{10,... | collective-permute-start | bytes 196616 | tf_op jit(solution)/shard_map/ppermute | solution.py:428
  44.9 16.8 %collective-permute-start.13 = (f32[64,512]{1,0:T(8,128)S(1)}, f32[64,512]{1,0:T(8,128)S(1)}, u32[]{:S(2)}, u32[]{:S(2)}) collective-permute-start(f32[64,512]{1,0:T(8,128)S(1)} %double.9.first.slices), channel_id=1, source_target_pairs={{0,2},{1,3},{2,0},{3,1},{4,6},{5,7},{6,4},{7,5},{8,10},{9,11},{10,... | collective-permute-start | bytes 393224 | tf_op jit(solution)/shard_map/ppermute | solution.py:428
  55.8 15.1 %copy-start.9 = (s32[256]{0:T(256)}, s32[256]{0:T(256)S(1)}, u32[]{:S(2)}) copy-start(s32[256]{0:T(256)S(1)} %get-tuple-element.123.place) | copy-start | bytes 3076
  56.9 11.7 %all-to-all-start.4 = ((f32[8,8,128]{2,1,0:T(8,128)}), f32[8,8,128]{2,1,0:T(8,128)S(1)}, u32[]{:S(2)}, u32[]{:S(2)}) async-start(f32[8,8,128]{2,1,0:T(8,128)} %pieces.3), calls=%async_computation.4 | async-start | bytes 65536 | tf_op jit(solution)/shard_map/all_to_all | solution.py:442
  70.9 13.2 %all-to-all-start.5 = ((f32[4,376,128]{2,1,0:T(8,128)}), f32[4,376,128]{2,1,0:T(8,128)S(1)}, u32[]{:S(2)}, u32[]{:S(2)}) async-start(f32[4,376,128]{2,1,0:T(8,128)} %collect.3), calls=%async_computation.5 | async-start | bytes 1540096 | tf_op jit(solution)/shard_map/all_to_all | solution.py:445
  75.8 7.4 %collective-permute-start.14 = (f32[128,512]{1,0:T(8,128)S(1)}, f32[128,512]{1,0:T(8,128)S(1)}, u32[]{:S(2)}, u32[]{:S(2)}) collective-permute-start(f32[128,512]{1,0:T(8,128)S(1)} %double.10.slices.first), channel_id=1, source_target_pairs={{0,1},{1,0},{2,3},{3,2},{4,5},{5,4},{6,7},{7,6},{8,9},{9,8},{10,11... | collective-permute-start | bytes 786440 | tf_op jit(solution)/shard_map/ppermute | solution.py:428
  84.0 8.9 %collective-permute-start.15 = (f32[4,376,128]{2,1,0:T(8,128)S(1)}, f32[4,376,128]{2,1,0:T(8,128)S(1)}, u32[]{:S(2)}, u32[]{:S(2)}) collective-permute-start(f32[4,376,128]{2,1,0:T(8,128)S(1)} %all-to-all-done.5.own), channel_id=1, source_target_pairs={{0,8},{8,0},{1,9},{9,1},{2,10},{10,2},{3,11},{11,3},{4,12},{12,4},... | collective-permute-start | bytes 2310152 | tf_op jit(solution)/shard_map/ppermute | solution.py:415

commit v7 on v6

--- a/solution.py
+++ b/solution.py
@@ -17,6 +17,10 @@
 DIAG = NB // Y
 BATCH = 16
 DISTANCES = (4, 2, 1)
+FILLER, PLACE, TOPS = 0, NB, 2 * NB
+COUNT = TOPS + NB + 8
+MOST = COUNT + Z + 1
+TABLE = 1024
 BITS = NB.bit_length() - 1
 PLANE_BITS = (ROWS * C).bit_length() - 1
 NARROW = 56
@@ -62,43 +66,39 @@
     return ((lax.axis_index("x") * Z + lax.axis_index("z")) * C + lax.axis_index("c")) * ROWS
 
 
-def plan_kernel(pivots, filler, place, slot_of, tops, count, most, content):
+def plan_kernel(pivots, table, content):
     def start(i):
+        content[i] = i
         content[pivots[i]] = pivots[i]
 
-    def start_top(i):
-        content[i] = i
-
     loop(NB, start, 8)
-    loop(NB, start_top, 8)
+    for z in range(Z):
+        table[COUNT + z] = 0
 
     def exchange(i, found):
         at = pivots[i]
         left, right = content[i], content[at]
         content[i] = right
         content[at] = left
-        tops[found] = i * NB + right
+        table[TOPS + found] = i * NB + right
+        plane = plane_of(at)
+        have = table[COUNT + plane]
+        table[PLACE + i] = plane * NB + have
+        table[COUNT + plane] = have + 1
         return found + (right != at).astype(jnp.int32)
 
     found = lax.fori_loop(0, NB, exchange, jnp.int32(0), unroll=4)
-    for z in range(Z):
-        count[z] = 0
-
-    def rank(i):
+
+    def fill(i):
         row = pivots[i]
-        filler[i] = jnp.where(row < NB, 0, content[row])
-        plane = plane_of(row)
-        have = count[plane]
-        place[i] = plane * NB + have
-        slot_of[plane * NB + have] = i
-        count[plane] = have + 1
-
-    loop(NB, rank, 4)
-    count[Z] = found
-    peak = count[0]
+        table[FILLER + i] = jnp.where(row < NB, 0, content[row])
+
+    loop(NB, fill, 8)
+    table[COUNT + Z] = found
+    peak = table[COUNT]
     for z in range(1, Z):
-        peak = jnp.maximum(peak, count[z])
-    most[0] = peak + found
+        peak = jnp.maximum(peak, table[COUNT + z])
+    table[MOST] = peak + found
 
 
 def early_plan_kernel(*refs):
@@ -107,18 +107,17 @@
         plan_kernel(*refs)
 
 
-def late_plan_kernel(pivots, after, *refs):
-    plan_kernel(pivots, *refs)
+def late_plan_kernel(pivots, after, table, content):
+    plan_kernel(pivots, table, content)
 
 
 def make_plan(pivots, after=None):
-    sizes = (NB, NB, Z * NB, NB + 8, Z + 1, 1)
     early = after is None
     return pl.pallas_call(
         early_plan_kernel if early else late_plan_kernel,
-        out_shape=[jax.ShapeDtypeStruct((n,), jnp.int32) for n in sizes],
+        out_shape=jax.ShapeDtypeStruct((TABLE,), jnp.int32),
         in_specs=[SMEM] if early else [SMEM, VMEM],
-        out_specs=[SMEM] * len(sizes),
+        out_specs=SMEM,
         scratch_shapes=[pltpu.SMEM((ORDER,), jnp.int32)],
         compiler_params=PARAMS,
         cost_estimate=pl.CostEstimate(flops=0, bytes_accessed=16 * 1024 * 1024, transcendentals=0),
@@ -196,8 +195,8 @@
         out[cap:, :] = jnp.where(c == 0, keep[at, cap:, :], got[at, cap:, :])
 
 
-def spread_kernel(cap, room, filler, place, tops, count, *refs):
-    blocks, out, former = refs[:X], refs[-2], refs[-1]
+def spread_kernel(cap, room, table, *refs):
+    blocks, panel_t, out, panel_out, former = refs[:X], *refs[X:]
     x = lax.axis_index("x")
     rest = blocks[0][cap:, :]
     for s in range(1, X):
@@ -209,41 +208,44 @@
     for z in range(Z):
         out[z, :cap, :] = rows
         out[z, cap + room :, :] = former[NB:, :]
+    panel_out[...] = panel_t[...]
 
     @pl.when(lax.axis_index("z") == 0)
     def _():
         def put(k):
             moves = []
             for i in range(BATCH):
-                where = place[k * BATCH + i]
+                where = table[PLACE + k * BATCH + i]
                 rank = jnp.minimum(where & (NB - 1), cap - 1)
-                moves.append((where >> BITS, cap + rank, former[pl.ds(filler[k * BATCH + i], 1), :]))
+                filler = table[FILLER + k * BATCH + i]
+                moves.append((where >> BITS, cap + rank, former[pl.ds(filler, 1), :]))
             for plane, at, values in moves:
                 out[plane, pl.ds(at, 1), :] = values
 
         loop(NB // BATCH, put)
 
         def top(k):
-            values = former[pl.ds(tops[k] & (NB - 1), 1), :]
+            values = former[pl.ds(table[TOPS + k] & (NB - 1), 1), :]
             for z in range(Z):
-                out[z, pl.ds(cap + jnp.minimum(count[z] + k, room - 1), 1), :] = values
-
-        loop(count[Z], top)
-
-
-def pieces_kernel(count, slices, got, out):
+                at = cap + jnp.minimum(table[COUNT + z] + k, room - 1)
+                out[z, pl.ds(at, 1), :] = values
+
+        loop(table[COUNT + Z], top)
+
+
+def pieces_kernel(token, got, out):
     for y in range(Y):
         out[y] = got[0, got.shape[1] - 8 :, :]
 
 
-def collect_kernel(cap, room, place, tops, count, slices, got, pieces, out):
+def collect_kernel(cap, room, table, token, got, pieces, out):
     z = lax.axis_index("z")
 
     def take(k):
         base = pl.multiple_of(k * BATCH, BATCH)
         rows = []
         for i in range(BATCH):
-            where = place[base + i]
+            where = table[PLACE + base + i]
             rank = jnp.minimum(where & (NB - 1), cap - 1)
             rows.append(got[where >> BITS, pl.ds(rank, 1), :])
         for i in range(BATCH):
@@ -252,10 +254,10 @@
     loop(NB // BATCH, take)
 
     def top(k):
-        at = cap + jnp.minimum(count[z] + k, room - 1)
-        out[0, pl.ds(tops[k] >> BITS, 1), :] = got[0, pl.ds(at, 1), :]
-
-    loop(count[Z], top)
+        at = cap + jnp.minimum(table[COUNT + z] + k, room - 1)
+        out[0, pl.ds(table[TOPS + k] >> BITS, 1), :] = got[0, pl.ds(at, 1), :]
+
+    loop(table[COUNT + Z], top)
     out[0, NB : NB + cap, :] = got[0, cap : 2 * cap, :]
     for y in range(Y):
         out[0, NB + cap + 8 * y : NB + cap + 8 * y + 8, :] = pieces[y]
@@ -289,14 +291,11 @@
     return jnp.concatenate([left, right], axis=1)
 
 
-def later_kernel(values, after, out):
-    out[...] = values[...]
-
-
-def double_kernel(first, second, out):
+def double_kernel(first, second, out, token):
     half = first.shape[0]
     out[:half] = first[...]
     out[half:] = second[...]
+    token[...] = second[:8, :LANES]
 
 
 def turn_kernel(slices, out, ordered):
@@ -387,17 +386,14 @@
     return call(functools.partial(join_kernel, cap), [keep.shape[1:]] * X, (), (keep, got), name="join")
 
 
-def spread(cap, room, plan, blocks):
-    filler, place, _, tops, count = plan
-    return call(functools.partial(spread_kernel, cap, room), (Z, cap + room + 8, LANES),
-                (filler, place, tops, count), blocks,
-                [pltpu.VMEM((NB + 8, LANES), jnp.float32)], name="spread")
-
-
-def collect(cap, room, plan, planes, pieces, slices):
-    _, place, _, tops, count = plan
+def spread(cap, room, plan, blocks, panel_t):
+    return call(functools.partial(spread_kernel, cap, room), [(Z, cap + room + 8, LANES), panel_t.shape],
+                (plan,), (*blocks, panel_t), [pltpu.VMEM((NB + 8, LANES), jnp.float32)], name="spread")
+
+
+def collect(cap, room, plan, token, planes, pieces):
     return call(functools.partial(collect_kernel, cap, room), (X, NB + cap + 8 * Y, LANES),
-                (place, tops, count), (slices, planes, pieces), name="collect")
+                (plan,), (token, planes, pieces), name="collect")
 
 
 def finish(cap, mine, own, other, multipliers, trailing):
@@ -420,8 +416,7 @@
     blocks = join(cap, keep, other_core(send))
     for s in range(1, X):
         blocks[s] = lax.ppermute(blocks[s], "x", [(x, (x + s) % X) for x in range(X)])
-    plan = make_plan(pivots)
-    return spread(cap, room, plan[:-1], blocks), mine
+    return *spread(cap, room, make_plan(pivots), blocks, panel_t), mine
 
 
 def from_column(values, distance):
@@ -430,38 +425,38 @@
 
 def doubled(slices, distance):
     shape = (2 * slices.shape[0], ROWS)
-    return call(double_kernel, shape, (), (slices, from_column(slices, distance)), name="double")
-
-
-def later_phases(cap, room, planes, plan, panel_t):
-    slices = call(later_kernel, panel_t.shape, (), (panel_t, planes), name="later")
-    slices = doubled(slices, DISTANCES[0])
+    return call(double_kernel, [shape, (8, LANES)], (), (slices, from_column(slices, distance)), name="double")
+
+
+def later_phases(cap, room, planes, slices, pivots):
+    slices, token = doubled(slices, DISTANCES[0])
     planes = swap(planes, "z")
-    pieces = call(pieces_kernel, (Y, 8, LANES), (plan[-1],), (slices, planes), name="pieces")
-    slices = doubled(slices, DISTANCES[1])
-    blocks = collect(cap, room, plan, planes, swap(pieces, "y"), slices)
-    slices = doubled(slices, DISTANCES[2])
+    pieces = call(pieces_kernel, (Y, 8, LANES), (), (token, planes), name="pieces")
+    plan = make_plan(pivots, pieces)
+    slices, token = doubled(slices, DISTANCES[1])
+    blocks = collect(cap, room, plan, token, planes, swap(pieces, "y"))
+    slices, _ = doubled(slices, DISTANCES[2])
     multipliers = call(turn_kernel, (ROWS, NB), (), (slices,), [pltpu.VMEM((NB, ROWS), jnp.float32)], name="turn")
     own, multipliers = lax.optimization_barrier((swap(blocks, "x"), multipliers))
-    return own, other_core(own), multipliers
+    return plan[MOST], own, other_core(own), multipliers
 
 
 def shards(panel, trailing, pivots):
     panel_t = panel.T
-    planes, mine = first_phase(NARROW, NARROW, panel_t, trailing, pivots)
-    *plan, most = make_plan(pivots, planes)
-    ready = later_phases(NARROW, NARROW, planes, plan, panel_t)
-    result = finish(NARROW, mine, *ready, trailing)
+
+    def with_room(cap, room):
+        planes, slices, mine = first_phase(cap, room, panel_t, trailing, pivots)
+        most, *ready = later_phases(cap, room, planes, slices, pivots)
+        return most, finish(cap, mine, *ready, trailing)
 
     def pending(carry):
         return carry[0]
 
     def again(carry):
-        planes, mine = first_phase(NB, 2 * NB, panel_t, trailing, pivots)
-        ready = later_phases(NB, 2 * NB, planes, plan, panel_t)
-        return jnp.zeros_like(carry[0]), finish(NB, mine, *ready, trailing)
-
-    return lax.while_loop(pending, again, (most[0] > NARROW, result))[1]
+        return jnp.zeros_like(carry[0]), with_room(NB, 2 * NB)[1]
+
+    most, result = with_room(NARROW, NARROW)
+    return lax.while_loop(pending, again, (most > NARROW, result))[1]
 
 
 def solution(mesh):

time: 103 us -> 99.7 us (0.968)
  Pallas kernels: 31.4 us -> 28.4 us
  waiting for transfers between devices: 17.4 us -> 14.4 us
  starting transfers between devices: 52.3 us -> 54.5 us
    all_to_all x1, waiting for transfers between devices: 6.84 us -> 1.99 us  [later_phases(): blocks = collect(cap, room, plan, token, planes, swap(pieces, 'y'))]
    pallas_call x2, Pallas kernels: 11.7 us -> 9.42 us  [make_plan(): pl.pallas_call(early_plan_kernel if early else late_plan_kernel, out_shap...]
    all_to_all x1, starting transfers between devices: 4.92 us -> 7.06 us  [later_phases(): swap(blocks, 'x')]
    all_to_all x1, starting transfers between devices: 4.82 us -> 6.82 us  [later_phases(): blocks = collect(cap, room, plan, token, planes, swap(pieces, 'y'))]
    ppermute x2, starting transfers between devices: 15.9 us -> 14 us  [other_core(): return lax.ppermute(values, 'c', [(0, 1), (1, 0)])]
    pallas_call x11 -> x10, Pallas kernels: 19.7 us -> 19 us  [call(): pl.pallas_call(kernel, out_shape=shapes, in_specs=[SMEM] * len(smem) + [V...]
  transfers between devices with their start and end apart: 11 -> 11, of which waited for: 7 -> 8; matrix products, arithmetic and copies ran while one was open for 0% -> 1% of each run, Pallas kernels for 14% -> 11%
where the time goes in v7:
time: 99.7 us; the launch traced here: 99.1 us
  starting transfers between devices  54.5 us (55%)
  Pallas kernels  28.4 us (28%)
  waiting for transfers between devices  14.4 us (14%)
    pallas_call x10, Pallas kernels, call(): pl.pallas_call(kernel, out_shape=shapes, in_specs=[SMEM] * len(smem) + [V...  19 us
    ppermute x3, starting transfers between devices, from_column(): return lax.ppermute(values, 'y', [(y, y ^ distance) for y in range(Y)])  14.3 us
    ppermute x2, starting transfers between devices, other_core(): return lax.ppermute(values, 'c', [(0, 1), (1, 0)])  14 us
    pallas_call x2, Pallas kernels, make_plan(): pl.pallas_call(early_plan_kernel if early else late_plan_kernel, out_shap...  9.42 us
    ppermute x3, starting transfers between devices, first_phase(): lax.ppermute(blocks[s], 'x', [(x, (x + s) % X) for x in range(X)])  8.41 us
    all_to_all x1, starting transfers between devices, later_phases(): swap(blocks, 'x')  7.06 us
    ppermute x3, waiting for transfers between devices, from_column(): return lax.ppermute(values, 'y', [(y, y ^ distance) for y in range(Y)])  7 us
    all_to_all x1, starting transfers between devices, later_phases(): blocks = collect(cap, room, plan, token, planes, swap(pieces, 'y'))  6.82 us
  transfers between devices with their start and end apart: 11, of which 8 were waited for; matrix products, arithmetic and copies ran while one was open for 1% of the time, Pallas kernels for 11%

profile of v7, /device:TPU:1, one launch (start us, length us, event | category | flops | bytes accessed | tf_op | source)
XLA Modules:
  0.0 99.1 jit_solution(8384342657744441423)
XLA Ops:
  0.0 3.8 %pack.3 = (f32[4,320,128]{2,1,0:T(8,128)S(1)}, f32[4,320,128]{2,1,0:T(8,128)S(1)}, s32[264]{0:T(512)S(1)}) custom-call(s32[256]{0:T(256)} %pivots.3, f32[32,512]{1,0:T(8,128)} %bitcast.2, f32[512,1024]{1,0:T(8,128)} %trailing.3), custom_call_target="tpu_custom_call" | custom-call | bytes 2097152 | tf_op jit(solution)/shard_map/pack/pallas_call | solution.py:366
  3.8 8.7 %collective-permute-start.8 = (f32[4,320,128]{2,1,0:T(8,128)S(1)}, f32[4,320,128]{2,1,0:T(8,128)S(1)}, u32[]{:S(2)}, u32[]{:S(2)}) collective-permute-start(f32[4,320,128]{2,1,0:T(8,128)S(1)} %get-tuple-element.63), channel_id=1, source_target_pairs={{0,8},{8,0},{1,9},{9,1},{2,10},{10,2},{3,11},{11,3},{4,12},{12,4},... | collective-permute-start | bytes 1966088 | tf_op jit(solution)/shard_map/ppermute | solution.py:411
  12.5 1.7 %collective-permute-done.8.got = f32[4,320,128]{2,1,0:T(8,128)S(1)} collective-permute-done((f32[4,320,128]{2,1,0:T(8,128)S(1)}, f32[4,320,128]{2,1,0:T(8,128)S(1)}, u32[]{:S(2)}, u32[]{:S(2)}) %collective-permute-start.8) | collective-permute-done | bytes 655392 | tf_op jit(solution)/shard_map/ppermute | solution.py:411
  14.3 1.9 %collective-permute-start.9 = (f32[320,128]{1,0:T(8,128)S(1)}, f32[320,128]{1,0:T(8,128)S(1)}, u32[]{:S(2)}, u32[]{:S(2)}) collective-permute-start(f32[320,128]{1,0:T(8,128)S(1)} %get-tuple-element.65), channel_id=1, source_target_pairs={{0,128},{128,256},{256,384},{384,0},{1,129},{129,257},{257,385},{3... | collective-permute-start | bytes 491528 | tf_op jit(solution)/shard_map/ppermute | solution.py:418
  16.2 1.9 %collective-permute-start.10 = (f32[320,128]{1,0:T(8,128)S(1)}, f32[320,128]{1,0:T(8,128)S(1)}, u32[]{:S(2)}, u32[]{:S(2)}) collective-permute-start(f32[320,128]{1,0:T(8,128)S(1)} %get-tuple-element.66), channel_id=1, source_target_pairs={{0,256},{128,384},{256,0},{384,128},{1,257},{129,385},{257,1},{385... | collective-permute-start | bytes 491528 | tf_op jit(solution)/shard_map/ppermute | solution.py:418
  18.1 4.6 %collective-permute-start.11 = (f32[320,128]{1,0:T(8,128)S(1)}, f32[320,128]{1,0:T(8,128)S(1)}, u32[]{:S(2)}, u32[]{:S(2)}) collective-permute-start(f32[320,128]{1,0:T(8,128)S(1)} %get-tuple-element.67), channel_id=1, source_target_pairs={{0,384},{128,0},{256,128},{384,256},{1,385},{129,1},{257,129},{385... | collective-permute-start | bytes 491528 | tf_op jit(solution)/shard_map/ppermute | solution.py:418
  22.7 4.6 %plan.6.table = s32[1024]{0:T(1024)S(1)} custom-call(s32[256]{0:T(256)S(1)} %copy-done.7), custom_call_target="tpu_custom_call" | custom-call | bytes 16777216 | tf_op jit(solution)/shard_map/plan/pallas_call | solution.py:116
  27.3 1.1 %collective-permute-done.11.refs_3_ = f32[320,128]{1,0:T(8,128)S(1)} collective-permute-done((f32[320,128]{1,0:T(8,128)S(1)}, f32[320,128]{1,0:T(8,128)S(1)}, u32[]{:S(2)}, u32[]{:S(2)}) %collective-permute-start.11) | collective-permute-done | bytes 163872 | tf_op jit(solution)/shard_map/ppermute | solution.py:418
  28.5 2.3 %spread.3 = (f32[8,120,128]{2,1,0:T(8,128)}, f32[32,512]{1,0:T(8,128)S(1)}) custom-call(s32[1024]{0:T(1024)S(1)} %plan.6.table, f32[320,128]{1,0:T(8,128)S(1)} %get-tuple-element.64.refs_0_, f32[320,128]{1,0:T(8,128)S(1)} %collective-permute-done.9.refs_1_, f32[320,128]{1,0:T(8,128)S(1)} %collective-permute-done.10.refs_2_, ...), custom_call_target="tpu_custom_call" | custom-call | bytes 2097152 | tf_op jit(solution)/shard_map/spread/pallas_call | solution.py:366
  30.8 3.8 %all-to-all-start.3 = ((f32[8,120,128]{2,1,0:T(8,128)}), f32[8,120,128]{2,1,0:T(8,128)S(1)}, u32[]{:S(2)}, u32[]{:S(2)}) async-start(f32[8,120,128]{2,1,0:T(8,128)} %get-tuple-element.70), calls=%async_computation.3 | async-start | bytes 983040 | tf_op jit(solution)/shard_map/all_to_all | solution.py:433
  34.6 7.4 %collective-permute-start.12 = (f32[32,512]{1,0:T(8,128)S(1)}, f32[32,512]{1,0:T(8,128)S(1)}, u32[]{:S(2)}, u32[]{:S(2)}) collective-permute-start(f32[32,512]{1,0:T(8,128)S(1)} %get-tuple-element.68.first), channel_id=1, source_target_pairs={{0,4},{1,5},{2,6},{3,7},{4,0},{5,1},{6,2},{7,3},{8,12},{9,13},{10,... | collective-permute-start | bytes 196616 | tf_op jit(solution)/shard_map/ppermute | solution.py:423
  42.1 1.7 %collective-permute-done.12.second = f32[32,512]{1,0:T(8,128)S(1)} collective-permute-done((f32[32,512]{1,0:T(8,128)S(1)}, f32[32,512]{1,0:T(8,128)S(1)}, u32[]{:S(2)}, u32[]{:S(2)}) %collective-permute-start.12) | collective-permute-done | bytes 65568 | tf_op jit(solution)/shard_map/ppermute | solution.py:423
  43.8 4.7 %collective-permute-start.13 = (f32[64,512]{1,0:T(8,128)S(1)}, f32[64,512]{1,0:T(8,128)S(1)}, u32[]{:S(2)}, u32[]{:S(2)}) collective-permute-start(f32[64,512]{1,0:T(8,128)S(1)} %get-tuple-element.72.first), channel_id=1, source_target_pairs={{0,2},{1,3},{2,0},{3,1},{4,6},{5,7},{6,4},{7,5},{8,10},{9,11},{10,... | collective-permute-start | bytes 393224 | tf_op jit(solution)/shard_map/ppermute | solution.py:423
  48.5 0.7 all-to-all-done.3.got
  49.8 6.8 %all-to-all-start.4 = ((f32[8,8,128]{2,1,0:T(8,128)}), f32[8,8,128]{2,1,0:T(8,128)S(1)}, u32[]{:S(2)}, u32[]{:S(2)}) async-start(f32[8,8,128]{2,1,0:T(8,128)} %pieces.3.after), calls=%async_computation.4 | async-start | bytes 65536 | tf_op jit(solution)/shard_map/all_to_all | solution.py:437
  56.7 4.8 %plan.7.table = s32[1024]{0:T(1024)S(1)} custom-call(s32[256]{0:T(256)S(1)} %copy-done.7, f32[8,8,128]{2,1,0:T(8,128)} %pieces.3.after), custom_call_target="tpu_custom_call" | custom-call | bytes 16777216 | tf_op jit(solution)/shard_map/plan/pallas_call | solution.py:116
  61.5 2.0 %all-to-all-done.4.pieces = f32[8,8,128]{2,1,0:T(8,128)S(1)} async-done(((f32[8,8,128]{2,1,0:T(8,128)}), f32[8,8,128]{2,1,0:T(8,128)S(1)}, u32[]{:S(2)}, u32[]{:S(2)}) %all-to-all-start.4) | async-done | bytes 32800 | tf_op jit(solution)/shard_map/all_to_all | solution.py:437
  63.5 2.2 %collect.3 = f32[4,376,128]{2,1,0:T(8,128)} custom-call(s32[1024]{0:T(1024)S(1)} %plan.7.table, f32[8,128]{1,0:T(8,128)S(1)} %get-tuple-element.73.token, f32[8,120,128]{2,1,0:T(8,128)S(1)} %all-to-all-done.3.got, f32[8,8,128]{2,1,0:T(8,128)S(1)} %all-to-all-done.4.pieces), custom_call_target="tpu_custom_call" | custom-call | bytes 2097152 | tf_op jit(solution)/shard_map/collect/pallas_call | solution.py:366
  65.7 7.1 %all-to-all-start.5 = ((f32[4,376,128]{2,1,0:T(8,128)}), f32[4,376,128]{2,1,0:T(8,128)S(1)}, u32[]{:S(2)}, u32[]{:S(2)}) async-start(f32[4,376,128]{2,1,0:T(8,128)} %collect.3), calls=%async_computation.5 | async-start | bytes 1540096 | tf_op jit(solution)/shard_map/all_to_all | solution.py:440
  72.8 2.2 %collective-permute-start.14 = (f32[128,512]{1,0:T(8,128)S(1)}, f32[128,512]{1,0:T(8,128)S(1)}, u32[]{:S(2)}, u32[]{:S(2)}) collective-permute-start(f32[128,512]{1,0:T(8,128)S(1)} %get-tuple-element.74.first), channel_id=1, source_target_pairs={{0,1},{1,0},{2,3},{3,2},{4,5},{5,4},{6,7},{7,6},{8,9},{9,8},{10,11... | collective-permute-start | bytes 786440 | tf_op jit(solution)/shard_map/ppermute | solution.py:423
  75.0 5.3 %collective-permute-done.14.second = f32[128,512]{1,0:T(8,128)S(1)} collective-permute-done((f32[128,512]{1,0:T(8,128)S(1)}, f32[128,512]{1,0:T(8,128)S(1)}, u32[]{:S(2)}, u32[]{:S(2)}) %collective-permute-start.14) | collective-permute-done | bytes 262176 | tf_op jit(solution)/shard_map/ppermute | solution.py:423
  81.1 1.3 %all-to-all-done.5.own = f32[4,376,128]{2,1,0:T(8,128)S(1)} async-done(((f32[4,376,128]{2,1,0:T(8,128)}), f32[4,376,128]{2,1,0:T(8,128)S(1)}, u32[]{:S(2)}, u32[]{:S(2)}) %all-to-all-start.5) | async-done | bytes 770080 | tf_op jit(solution)/shard_map/all_to_all | solution.py:440
  82.4 5.3 %collective-permute-start.15 = (f32[4,376,128]{2,1,0:T(8,128)S(1)}, f32[4,376,128]{2,1,0:T(8,128)S(1)}, u32[]{:S(2)}, u32[]{:S(2)}) collective-permute-start(f32[4,376,128]{2,1,0:T(8,128)S(1)} %all-to-all-done.5.own), channel_id=1, source_target_pairs={{0,8},{8,0},{1,9},{9,1},{2,10},{10,2},{3,11},{11,3},{4,12},{12,4},... | collective-permute-start | bytes 2310152 | tf_op jit(solution)/shard_map/ppermute | solution.py:411
  89.6 9.1 %finish.3 = f32[512,1024]{1,0:T(8,128)} custom-call(s32[264]{0:T(512)S(1)} %get-tuple-element.71.mine, f32[4,376,128]{2,1,0:T(8,128)S(1)} %all-to-all-done.5.own, f32[4,376,128]{2,1,0:T(8,128)S(1)} %collective-permute-done.15.other, f32[512,256]{1,0:T(8,128)S(1)} %turn.3.multipliers, f32[512,1024]{1,0:T(8,128)} %trailing.3), custom_call_target="tpu_custom_call" | custom-call | bytes 16777216 | tf_op jit(solution)/shard_map/finish/pallas_call | solution.py:366
  (16 shorter events, 3.0 us)
Async XLA Ops:
  0.0 22.7 %copy-start.7 = (s32[256]{0:T(256)S(1)}, s32[256]{0:T(256)}, u32[]{:S(2)}) copy-start(s32[256]{0:T(256)} %pivots.3) | copy-start | bytes 3076
  0.0 28.5 %copy-start.6 = (f32[512,32]{0,1:T(8,128)S(1)}, f32[512,32]{0,1:T(8,128)}, u32[]{:S(2)}) copy-start(f32[512,32]{0,1:T(8,128)} %param.5) | copy-start | bytes 196612
  3.8 10.4 %collective-permute-start.8 = (f32[4,320,128]{2,1,0:T(8,128)S(1)}, f32[4,320,128]{2,1,0:T(8,128)S(1)}, u32[]{:S(2)}, u32[]{:S(2)}) collective-permute-start(f32[4,320,128]{2,1,0:T(8,128)S(1)} %get-tuple-element.63), channel_id=1, source_target_pairs={{0,8},{8,0},{1,9},{9,1},{2,10},{10,2},{3,11},{11,3},{4,12},{12,4},... | collective-permute-start | bytes 1966088 | tf_op jit(solution)/shard_map/ppermute | solution.py:411
  14.3 13.0 %collective-permute-start.9 = (f32[320,128]{1,0:T(8,128)S(1)}, f32[320,128]{1,0:T(8,128)S(1)}, u32[]{:S(2)}, u32[]{:S(2)}) collective-permute-start(f32[320,128]{1,0:T(8,128)S(1)} %get-tuple-element.65), channel_id=1, source_target_pairs={{0,128},{128,256},{256,384},{384,0},{1,129},{129,257},{257,385},{3... | collective-permute-start | bytes 491528 | tf_op jit(solution)/shard_map/ppermute | solution.py:418
  16.2 11.1 %collective-permute-start.10 = (f32[320,128]{1,0:T(8,128)S(1)}, f32[320,128]{1,0:T(8,128)S(1)}, u32[]{:S(2)}, u32[]{:S(2)}) collective-permute-start(f32[320,128]{1,0:T(8,128)S(1)} %get-tuple-element.66), channel_id=1, source_target_pairs={{0,256},{128,384},{256,0},{384,128},{1,257},{129,385},{257,1},{385... | collective-permute-start | bytes 491528 | tf_op jit(solution)/shard_map/ppermute | solution.py:418
  18.1 10.3 %collective-permute-start.11 = (f32[320,128]{1,0:T(8,128)S(1)}, f32[320,128]{1,0:T(8,128)S(1)}, u32[]{:S(2)}, u32[]{:S(2)}) collective-permute-start(f32[320,128]{1,0:T(8,128)S(1)} %get-tuple-element.67), channel_id=1, source_target_pairs={{0,384},{128,0},{256,128},{384,256},{1,385},{129,1},{257,129},{385... | collective-permute-start | bytes 491528 | tf_op jit(solution)/shard_map/ppermute | solution.py:418
  30.8 18.4 %all-to-all-start.3 = ((f32[8,120,128]{2,1,0:T(8,128)}), f32[8,120,128]{2,1,0:T(8,128)S(1)}, u32[]{:S(2)}, u32[]{:S(2)}) async-start(f32[8,120,128]{2,1,0:T(8,128)} %get-tuple-element.70), calls=%async_computation.3 | async-start | bytes 983040 | tf_op jit(solution)/shard_map/all_to_all | solution.py:433
  34.6 9.2 %collective-permute-start.12 = (f32[32,512]{1,0:T(8,128)S(1)}, f32[32,512]{1,0:T(8,128)S(1)}, u32[]{:S(2)}, u32[]{:S(2)}) collective-permute-start(f32[32,512]{1,0:T(8,128)S(1)} %get-tuple-element.68.first), channel_id=1, source_target_pairs={{0,4},{1,5},{2,6},{3,7},{4,0},{5,1},{6,2},{7,3},{8,12},{9,13},{10,... | collective-permute-start | bytes 196616 | tf_op jit(solution)/shard_map/ppermute | solution.py:423
  43.8 12.8 %collective-permute-start.13 = (f32[64,512]{1,0:T(8,128)S(1)}, f32[64,512]{1,0:T(8,128)S(1)}, u32[]{:S(2)}, u32[]{:S(2)}) collective-permute-start(f32[64,512]{1,0:T(8,128)S(1)} %get-tuple-element.72.first), channel_id=1, source_target_pairs={{0,2},{1,3},{2,0},{3,1},{4,6},{5,7},{6,4},{7,5},{8,10},{9,11},{10,... | collective-permute-start | bytes 393224 | tf_op jit(solution)/shard_map/ppermute | solution.py:423
  49.8 13.7 %all-to-all-start.4 = ((f32[8,8,128]{2,1,0:T(8,128)}), f32[8,8,128]{2,1,0:T(8,128)S(1)}, u32[]{:S(2)}, u32[]{:S(2)}) async-start(f32[8,8,128]{2,1,0:T(8,128)} %pieces.3.after), calls=%async_computation.4 | async-start | bytes 65536 | tf_op jit(solution)/shard_map/all_to_all | solution.py:437
  65.7 16.7 %all-to-all-start.5 = ((f32[4,376,128]{2,1,0:T(8,128)}), f32[4,376,128]{2,1,0:T(8,128)S(1)}, u32[]{:S(2)}, u32[]{:S(2)}) async-start(f32[4,376,128]{2,1,0:T(8,128)} %collect.3), calls=%async_computation.5 | async-start | bytes 1540096 | tf_op jit(solution)/shard_map/all_to_all | solution.py:440
  72.8 7.5 %collective-permute-start.14 = (f32[128,512]{1,0:T(8,128)S(1)}, f32[128,512]{1,0:T(8,128)S(1)}, u32[]{:S(2)}, u32[]{:S(2)}) collective-permute-start(f32[128,512]{1,0:T(8,128)S(1)} %get-tuple-element.74.first), channel_id=1, source_target_pairs={{0,1},{1,0},{2,3},{3,2},{4,5},{5,4},{6,7},{7,6},{8,9},{9,8},{10,11... | collective-permute-start | bytes 786440 | tf_op jit(solution)/shard_map/ppermute | solution.py:423
  82.4 7.2 %collective-permute-start.15 = (f32[4,376,128]{2,1,0:T(8,128)S(1)}, f32[4,376,128]{2,1,0:T(8,128)S(1)}, u32[]{:S(2)}, u32[]{:S(2)}) collective-permute-start(f32[4,376,128]{2,1,0:T(8,128)S(1)} %all-to-all-done.5.own), channel_id=1, source_target_pairs={{0,8},{8,0},{1,9},{9,1},{2,10},{10,2},{3,11},{11,3},{4,12},{12,4},... | collective-permute-start | bytes 2310152 | tf_op jit(solution)/shard_map/ppermute | solution.py:411

commit v8 on v7

--- a/solution.py
+++ b/solution.py
@@ -22,6 +22,7 @@
 MOST = COUNT + Z + 1
 TABLE = 1024
 BITS = NB.bit_length() - 1
+ROW_BITS = ROWS.bit_length() - 1
 PLANE_BITS = (ROWS * C).bit_length() - 1
 NARROW = 56
 HIGHEST = lax.Precision.HIGHEST
@@ -142,6 +143,10 @@
     at[:, lanes] = pltpu.roll(window, shift, axis=1)
 
 
+def local_entry(cap, entry):
+    return (entry >> BITS) & (ROWS - 1), jnp.minimum(entry & (NB - 1), cap - 1)
+
+
 def pack_kernel(cap, pivots, panel_t, trailing, keep, send, mine, triangle, rows, sem):
     copy = pltpu.make_async_copy(trailing, rows, sem)
     copy.start()
@@ -149,13 +154,14 @@
     c = lax.axis_index("c")
     first = first_row()
 
+    device = first >> ROW_BITS
+
     def find(i, carry):
         rank, found = carry
         row = pivots[i]
-        local = row - first
-        mine[found] = local * NB + jnp.minimum(rank, cap - 1)
-        hit = (local >= 0) & (local < ROWS)
-        return rank + (plane_of(row) == z).astype(jnp.int32), found + hit.astype(jnp.int32)
+        mine[found] = (row << BITS) + rank
+        rank = jnp.where(plane_of(row) == z, rank + 1, rank)
+        return rank, jnp.where(row >> ROW_BITS == device, found + 1, found)
 
     _, found = lax.fori_loop(0, NB, find, (jnp.int32(0), jnp.int32(0)), unroll=16)
     invert_diagonal(panel_t, triangle)
@@ -172,9 +178,8 @@
             out[x, cap : cap + NB, :] = rows[:NB, lanes]
 
     def put(k):
-        entry = mine[k]
-        row = entry >> BITS
-        at = pl.ds(entry & (NB - 1), 1)
+        row, rank = local_entry(cap, mine[k])
+        at = pl.ds(rank, 1)
         hit = picked(row, LANES)
         for out, side in sides:
             for x in range(X):
@@ -325,9 +330,8 @@
     copy.wait()
 
     def put(k):
-        entry = mine[k]
-        row = entry >> BITS
-        rank = pl.ds(NB + (entry & (NB - 1)), 1)
+        row, rank = local_entry(cap, mine[k])
+        rank = pl.ds(NB + rank, 1)
         at = tile_of(row)
         hit = picked(row, LANES)
         for x in range(X):
@@ -336,24 +340,50 @@
                 current[at, lanes] = jnp.where(hit, ref[x, rank, :], current[at, lanes])
 
     loop(mine[NB], put)
-    copies = []
     width = C * LANES
-    for x in range(X):
-        lanes = slice(x * width, (x + 1) * width)
+
+    def write(x):
+        lanes = pl.ds(pl.multiple_of(x * width, width), width)
+        return pltpu.make_async_copy(current.at[:, lanes], out.at[:, lanes], out_sem.at[x])
+
+    def solve(x):
+        slot = x & 1
         for lane, ref in sides:
-            block[x, :, pl.ds(lane, LANES)] = ref[x, :NB, :]
-        solved = dot(inverse[...], block[x])
-        block[x] = solved
-        current[:, lanes] = current[:, lanes] - dot(multipliers[...], solved)
+            block[slot, :, pl.ds(lane, LANES)] = ref[x, :NB, :]
+        block[slot] = dot(inverse[...], block[slot])
+
+    def update(x):
+        lanes = pl.ds(pl.multiple_of(x * width, width), width)
+        slot = x & 1
+        current[:, lanes] = current[:, lanes] - dot(multipliers[...], block[slot])
 
         @pl.when(first == 0)
         def _():
-            current[:NB, lanes] = block[x]
-
-        copies.append(pltpu.make_async_copy(current.at[:, lanes], out.at[:, lanes], out_sem.at[x]))
-        copies[-1].start()
-    for copy in copies:
-        copy.wait()
+            current[:NB, lanes] = block[slot]
+
+        write(x).start()
+
+    def both(x):
+        lanes = pl.ds(pl.multiple_of(x * width, width), width)
+        slot = x & 1
+        for lane, ref in sides:
+            block[1 - slot, :, pl.ds(lane, LANES)] = ref[x + 1, :NB, :]
+        solved = dot(inverse[...], block[1 - slot])
+        product = dot(multipliers[...], block[slot])
+        block[1 - slot] = solved
+        current[:, lanes] = current[:, lanes] - product
+
+        @pl.when(first == 0)
+        def _():
+            current[:NB, lanes] = block[slot]
+
+        write(x).start()
+
+    solve(0)
+    loop(X - 1, both)
+    update(X - 1)
+    for x in range(X):
+        write(x).wait()
 
 
 def call(kernel, shape, smem, vmem, scratch=(), name=None, last=VMEM, out=VMEM, busy=2, table=None):
@@ -397,7 +427,7 @@
 
 
 def finish(cap, mine, own, other, multipliers, trailing):
-    scratch = [pltpu.VMEM(s, jnp.float32) for s in ((NB, NB), (NB, NB), (X, NB, C * LANES), (ROWS, COLS))]
+    scratch = [pltpu.VMEM(s, jnp.float32) for s in ((NB, NB), (NB, NB), (2, NB, C * LANES), (ROWS, COLS))]
     scratch += [pltpu.SemaphoreType.DMA, pltpu.SemaphoreType.DMA((X,))]
     return call(functools.partial(finish_kernel, cap), (ROWS, COLS), (mine,),
                 (own, other, multipliers, trailing), scratch, name="finish",

time: 99.7 us -> 96.9 us (0.972)
  Pallas kernels: 28.4 us -> 25.6 us
    pallas_call x10, Pallas kernels: 19 us -> 16.2 us  [call(): pl.pallas_call(kernel, out_shape=shapes, in_specs=[SMEM] * len(smem) + [V...]
where the time goes in v8:
time: 96.9 us; the launch traced here: 96.2 us
  starting transfers between devices  54.7 us (56%)
  Pallas kernels  25.6 us (26%)
  waiting for transfers between devices  14.4 us (15%)
    pallas_call x10, Pallas kernels, call(): pl.pallas_call(kernel, out_shape=shapes, in_specs=[SMEM] * len(smem) + [V...  16.2 us
    ppermute x3, starting transfers between devices, from_column(): return lax.ppermute(values, 'y', [(y, y ^ distance) for y in range(Y)])  14.3 us
    ppermute x2, starting transfers between devices, other_core(): return lax.ppermute(values, 'c', [(0, 1), (1, 0)])  14.2 us
    pallas_call x2, Pallas kernels, make_plan(): pl.pallas_call(early_plan_kernel if early else late_plan_kernel, out_shap...  9.42 us
    ppermute x3, starting transfers between devices, first_phase(): lax.ppermute(blocks[s], 'x', [(x, (x + s) % X) for x in range(X)])  8.41 us
    all_to_all x1, starting transfers between devices, later_phases(): swap(blocks, 'x')  7.15 us
    ppermute x3, waiting for transfers between devices, from_column(): return lax.ppermute(values, 'y', [(y, y ^ distance) for y in range(Y)])  7 us
    all_to_all x1, starting transfers between devices, later_phases(): blocks = collect(cap, room, plan, token, planes, swap(pieces, 'y'))  6.82 us
  transfers between devices with their start and end apart: 11, of which 8 were waited for; matrix products, arithmetic and copies ran while one was open for 1% of the time, Pallas kernels for 11%

profile of v8, /device:TPU:1, one launch (start us, length us, event | category | flops | bytes accessed | tf_op | source)
XLA Modules:
  0.0 96.2 jit_solution(5559918345675058106)
XLA Ops:
  0.0 3.3 %pack.3 = (f32[4,320,128]{2,1,0:T(8,128)S(1)}, f32[4,320,128]{2,1,0:T(8,128)S(1)}, s32[264]{0:T(512)S(1)}) custom-call(s32[256]{0:T(256)} %pivots.3, f32[32,512]{1,0:T(8,128)} %bitcast.2, f32[512,1024]{1,0:T(8,128)} %trailing.3), custom_call_target="tpu_custom_call" | custom-call | bytes 2097152 | tf_op jit(solution)/shard_map/pack/pallas_call | solution.py:396
  3.3 8.8 %collective-permute-start.8 = (f32[4,320,128]{2,1,0:T(8,128)S(1)}, f32[4,320,128]{2,1,0:T(8,128)S(1)}, u32[]{:S(2)}, u32[]{:S(2)}) collective-permute-start(f32[4,320,128]{2,1,0:T(8,128)S(1)} %get-tuple-element.63), channel_id=1, source_target_pairs={{0,8},{8,0},{1,9},{9,1},{2,10},{10,2},{3,11},{11,3},{4,12},{12,4},... | collective-permute-start | bytes 1966088 | tf_op jit(solution)/shard_map/ppermute | solution.py:441
  12.2 1.7 %collective-permute-done.8.got = f32[4,320,128]{2,1,0:T(8,128)S(1)} collective-permute-done((f32[4,320,128]{2,1,0:T(8,128)S(1)}, f32[4,320,128]{2,1,0:T(8,128)S(1)}, u32[]{:S(2)}, u32[]{:S(2)}) %collective-permute-start.8) | collective-permute-done | bytes 655392 | tf_op jit(solution)/shard_map/ppermute | solution.py:441
  13.9 1.9 %collective-permute-start.9 = (f32[320,128]{1,0:T(8,128)S(1)}, f32[320,128]{1,0:T(8,128)S(1)}, u32[]{:S(2)}, u32[]{:S(2)}) collective-permute-start(f32[320,128]{1,0:T(8,128)S(1)} %get-tuple-element.65), channel_id=1, source_target_pairs={{0,128},{128,256},{256,384},{384,0},{1,129},{129,257},{257,385},{3... | collective-permute-start | bytes 491528 | tf_op jit(solution)/shard_map/ppermute | solution.py:448
  15.9 1.9 %collective-permute-start.10 = (f32[320,128]{1,0:T(8,128)S(1)}, f32[320,128]{1,0:T(8,128)S(1)}, u32[]{:S(2)}, u32[]{:S(2)}) collective-permute-start(f32[320,128]{1,0:T(8,128)S(1)} %get-tuple-element.66), channel_id=1, source_target_pairs={{0,256},{128,384},{256,0},{384,128},{1,257},{129,385},{257,1},{385... | collective-permute-start | bytes 491528 | tf_op jit(solution)/shard_map/ppermute | solution.py:448
  17.8 4.6 %collective-permute-start.11 = (f32[320,128]{1,0:T(8,128)S(1)}, f32[320,128]{1,0:T(8,128)S(1)}, u32[]{:S(2)}, u32[]{:S(2)}) collective-permute-start(f32[320,128]{1,0:T(8,128)S(1)} %get-tuple-element.67), channel_id=1, source_target_pairs={{0,384},{128,0},{256,128},{384,256},{1,385},{129,1},{257,129},{385... | collective-permute-start | bytes 491528 | tf_op jit(solution)/shard_map/ppermute | solution.py:448
  22.4 4.6 %plan.6.table = s32[1024]{0:T(1024)S(1)} custom-call(s32[256]{0:T(256)S(1)} %copy-done.7), custom_call_target="tpu_custom_call" | custom-call | bytes 16777216 | tf_op jit(solution)/shard_map/plan/pallas_call | solution.py:117
  27.0 1.1 %collective-permute-done.11.refs_3_ = f32[320,128]{1,0:T(8,128)S(1)} collective-permute-done((f32[320,128]{1,0:T(8,128)S(1)}, f32[320,128]{1,0:T(8,128)S(1)}, u32[]{:S(2)}, u32[]{:S(2)}) %collective-permute-start.11) | collective-permute-done | bytes 163872 | tf_op jit(solution)/shard_map/ppermute | solution.py:448
  28.1 2.3 %spread.3 = (f32[8,120,128]{2,1,0:T(8,128)}, f32[32,512]{1,0:T(8,128)S(1)}) custom-call(s32[1024]{0:T(1024)S(1)} %plan.6.table, f32[320,128]{1,0:T(8,128)S(1)} %get-tuple-element.64.refs_0_, f32[320,128]{1,0:T(8,128)S(1)} %collective-permute-done.9.refs_1_, f32[320,128]{1,0:T(8,128)S(1)} %collective-permute-done.10.refs_2_, ...), custom_call_target="tpu_custom_call" | custom-call | bytes 2097152 | tf_op jit(solution)/shard_map/spread/pallas_call | solution.py:396
  30.5 3.8 %all-to-all-start.3 = ((f32[8,120,128]{2,1,0:T(8,128)}), f32[8,120,128]{2,1,0:T(8,128)S(1)}, u32[]{:S(2)}, u32[]{:S(2)}) async-start(f32[8,120,128]{2,1,0:T(8,128)} %get-tuple-element.70), calls=%async_computation.3 | async-start | bytes 983040 | tf_op jit(solution)/shard_map/all_to_all | solution.py:463
  34.3 7.4 %collective-permute-start.12 = (f32[32,512]{1,0:T(8,128)S(1)}, f32[32,512]{1,0:T(8,128)S(1)}, u32[]{:S(2)}, u32[]{:S(2)}) collective-permute-start(f32[32,512]{1,0:T(8,128)S(1)} %get-tuple-element.68.first), channel_id=1, source_target_pairs={{0,4},{1,5},{2,6},{3,7},{4,0},{5,1},{6,2},{7,3},{8,12},{9,13},{10,... | collective-permute-start | bytes 196616 | tf_op jit(solution)/shard_map/ppermute | solution.py:453
  41.7 1.7 %collective-permute-done.12.second = f32[32,512]{1,0:T(8,128)S(1)} collective-permute-done((f32[32,512]{1,0:T(8,128)S(1)}, f32[32,512]{1,0:T(8,128)S(1)}, u32[]{:S(2)}, u32[]{:S(2)}) %collective-permute-start.12) | collective-permute-done | bytes 65568 | tf_op jit(solution)/shard_map/ppermute | solution.py:453
  43.4 4.7 %collective-permute-start.13 = (f32[64,512]{1,0:T(8,128)S(1)}, f32[64,512]{1,0:T(8,128)S(1)}, u32[]{:S(2)}, u32[]{:S(2)}) collective-permute-start(f32[64,512]{1,0:T(8,128)S(1)} %get-tuple-element.72.first), channel_id=1, source_target_pairs={{0,2},{1,3},{2,0},{3,1},{4,6},{5,7},{6,4},{7,5},{8,10},{9,11},{10,... | collective-permute-start | bytes 393224 | tf_op jit(solution)/shard_map/ppermute | solution.py:453
  48.2 0.7 all-to-all-done.3.got
  49.5 6.8 %all-to-all-start.4 = ((f32[8,8,128]{2,1,0:T(8,128)}), f32[8,8,128]{2,1,0:T(8,128)S(1)}, u32[]{:S(2)}, u32[]{:S(2)}) async-start(f32[8,8,128]{2,1,0:T(8,128)} %pieces.3.after), calls=%async_computation.4 | async-start | bytes 65536 | tf_op jit(solution)/shard_map/all_to_all | solution.py:467
  56.3 4.8 %plan.7.table = s32[1024]{0:T(1024)S(1)} custom-call(s32[256]{0:T(256)S(1)} %copy-done.7, f32[8,8,128]{2,1,0:T(8,128)} %pieces.3.after), custom_call_target="tpu_custom_call" | custom-call | bytes 16777216 | tf_op jit(solution)/shard_map/plan/pallas_call | solution.py:117
  61.2 2.0 %all-to-all-done.4.pieces = f32[8,8,128]{2,1,0:T(8,128)S(1)} async-done(((f32[8,8,128]{2,1,0:T(8,128)}), f32[8,8,128]{2,1,0:T(8,128)S(1)}, u32[]{:S(2)}, u32[]{:S(2)}) %all-to-all-start.4) | async-done | bytes 32800 | tf_op jit(solution)/shard_map/all_to_all | solution.py:467
  63.1 2.2 %collect.3 = f32[4,376,128]{2,1,0:T(8,128)} custom-call(s32[1024]{0:T(1024)S(1)} %plan.7.table, f32[8,128]{1,0:T(8,128)S(1)} %get-tuple-element.73.token, f32[8,120,128]{2,1,0:T(8,128)S(1)} %all-to-all-done.3.got, f32[8,8,128]{2,1,0:T(8,128)S(1)} %all-to-all-done.4.pieces), custom_call_target="tpu_custom_call" | custom-call | bytes 2097152 | tf_op jit(solution)/shard_map/collect/pallas_call | solution.py:396
  65.4 7.2 %all-to-all-start.5 = ((f32[4,376,128]{2,1,0:T(8,128)}), f32[4,376,128]{2,1,0:T(8,128)S(1)}, u32[]{:S(2)}, u32[]{:S(2)}) async-start(f32[4,376,128]{2,1,0:T(8,128)} %collect.3), calls=%async_computation.5 | async-start | bytes 1540096 | tf_op jit(solution)/shard_map/all_to_all | solution.py:470
  72.5 2.2 %collective-permute-start.14 = (f32[128,512]{1,0:T(8,128)S(1)}, f32[128,512]{1,0:T(8,128)S(1)}, u32[]{:S(2)}, u32[]{:S(2)}) collective-permute-start(f32[128,512]{1,0:T(8,128)S(1)} %get-tuple-element.74.first), channel_id=1, source_target_pairs={{0,1},{1,0},{2,3},{3,2},{4,5},{5,4},{6,7},{7,6},{8,9},{9,8},{10,11... | collective-permute-start | bytes 786440 | tf_op jit(solution)/shard_map/ppermute | solution.py:453
  74.7 5.3 %collective-permute-done.14.second = f32[128,512]{1,0:T(8,128)S(1)} collective-permute-done((f32[128,512]{1,0:T(8,128)S(1)}, f32[128,512]{1,0:T(8,128)S(1)}, u32[]{:S(2)}, u32[]{:S(2)}) %collective-permute-start.14) | collective-permute-done | bytes 262176 | tf_op jit(solution)/shard_map/ppermute | solution.py:453
  80.8 1.3 %all-to-all-done.5.own = f32[4,376,128]{2,1,0:T(8,128)S(1)} async-done(((f32[4,376,128]{2,1,0:T(8,128)}), f32[4,376,128]{2,1,0:T(8,128)S(1)}, u32[]{:S(2)}, u32[]{:S(2)}) %all-to-all-start.5) | async-done | bytes 770080 | tf_op jit(solution)/shard_map/all_to_all | solution.py:470
  82.2 5.3 %collective-permute-start.15 = (f32[4,376,128]{2,1,0:T(8,128)S(1)}, f32[4,376,128]{2,1,0:T(8,128)S(1)}, u32[]{:S(2)}, u32[]{:S(2)}) collective-permute-start(f32[4,376,128]{2,1,0:T(8,128)S(1)} %all-to-all-done.5.own), channel_id=1, source_target_pairs={{0,8},{8,0},{1,9},{9,1},{2,10},{10,2},{3,11},{11,3},{4,12},{12,4},... | collective-permute-start | bytes 2310152 | tf_op jit(solution)/shard_map/ppermute | solution.py:441
  89.3 6.8 %finish.3 = f32[512,1024]{1,0:T(8,128)} custom-call(s32[264]{0:T(512)S(1)} %get-tuple-element.71.mine, f32[4,376,128]{2,1,0:T(8,128)S(1)} %all-to-all-done.5.own, f32[4,376,128]{2,1,0:T(8,128)S(1)} %collective-permute-done.15.other, f32[512,256]{1,0:T(8,128)S(1)} %turn.3.multipliers, f32[512,1024]{1,0:T(8,128)} %trailing.3), custom_call_target="tpu_custom_call" | custom-call | bytes 16777216 | tf_op jit(solution)/shard_map/finish/pallas_call | solution.py:396
  (16 shorter events, 2.8 us)
Async XLA Ops:
  0.0 22.4 %copy-start.7 = (s32[256]{0:T(256)S(1)}, s32[256]{0:T(256)}, u32[]{:S(2)}) copy-start(s32[256]{0:T(256)} %pivots.3) | copy-start | bytes 3076
  0.0 28.1 %copy-start.6 = (f32[512,32]{0,1:T(8,128)S(1)}, f32[512,32]{0,1:T(8,128)}, u32[]{:S(2)}) copy-start(f32[512,32]{0,1:T(8,128)} %param.5) | copy-start | bytes 196612
  3.3 10.6 %collective-permute-start.8 = (f32[4,320,128]{2,1,0:T(8,128)S(1)}, f32[4,320,128]{2,1,0:T(8,128)S(1)}, u32[]{:S(2)}, u32[]{:S(2)}) collective-permute-start(f32[4,320,128]{2,1,0:T(8,128)S(1)} %get-tuple-element.63), channel_id=1, source_target_pairs={{0,8},{8,0},{1,9},{9,1},{2,10},{10,2},{3,11},{11,3},{4,12},{12,4},... | collective-permute-start | bytes 1966088 | tf_op jit(solution)/shard_map/ppermute | solution.py:441
  13.9 13.0 %collective-permute-start.9 = (f32[320,128]{1,0:T(8,128)S(1)}, f32[320,128]{1,0:T(8,128)S(1)}, u32[]{:S(2)}, u32[]{:S(2)}) collective-permute-start(f32[320,128]{1,0:T(8,128)S(1)} %get-tuple-element.65), channel_id=1, source_target_pairs={{0,128},{128,256},{256,384},{384,0},{1,129},{129,257},{257,385},{3... | collective-permute-start | bytes 491528 | tf_op jit(solution)/shard_map/ppermute | solution.py:448
  15.9 11.1 %collective-permute-start.10 = (f32[320,128]{1,0:T(8,128)S(1)}, f32[320,128]{1,0:T(8,128)S(1)}, u32[]{:S(2)}, u32[]{:S(2)}) collective-permute-start(f32[320,128]{1,0:T(8,128)S(1)} %get-tuple-element.66), channel_id=1, source_target_pairs={{0,256},{128,384},{256,0},{384,128},{1,257},{129,385},{257,1},{385... | collective-permute-start | bytes 491528 | tf_op jit(solution)/shard_map/ppermute | solution.py:448
  17.8 10.3 %collective-permute-start.11 = (f32[320,128]{1,0:T(8,128)S(1)}, f32[320,128]{1,0:T(8,128)S(1)}, u32[]{:S(2)}, u32[]{:S(2)}) collective-permute-start(f32[320,128]{1,0:T(8,128)S(1)} %get-tuple-element.67), channel_id=1, source_target_pairs={{0,384},{128,0},{256,128},{384,256},{1,385},{129,1},{257,129},{385... | collective-permute-start | bytes 491528 | tf_op jit(solution)/shard_map/ppermute | solution.py:448
  30.5 18.4 %all-to-all-start.3 = ((f32[8,120,128]{2,1,0:T(8,128)}), f32[8,120,128]{2,1,0:T(8,128)S(1)}, u32[]{:S(2)}, u32[]{:S(2)}) async-start(f32[8,120,128]{2,1,0:T(8,128)} %get-tuple-element.70), calls=%async_computation.3 | async-start | bytes 983040 | tf_op jit(solution)/shard_map/all_to_all | solution.py:463
  34.3 9.2 %collective-permute-start.12 = (f32[32,512]{1,0:T(8,128)S(1)}, f32[32,512]{1,0:T(8,128)S(1)}, u32[]{:S(2)}, u32[]{:S(2)}) collective-permute-start(f32[32,512]{1,0:T(8,128)S(1)} %get-tuple-element.68.first), channel_id=1, source_target_pairs={{0,4},{1,5},{2,6},{3,7},{4,0},{5,1},{6,2},{7,3},{8,12},{9,13},{10,... | collective-permute-start | bytes 196616 | tf_op jit(solution)/shard_map/ppermute | solution.py:453
  43.4 12.8 %collective-permute-start.13 = (f32[64,512]{1,0:T(8,128)S(1)}, f32[64,512]{1,0:T(8,128)S(1)}, u32[]{:S(2)}, u32[]{:S(2)}) collective-permute-start(f32[64,512]{1,0:T(8,128)S(1)} %get-tuple-element.72.first), channel_id=1, source_target_pairs={{0,2},{1,3},{2,0},{3,1},{4,6},{5,7},{6,4},{7,5},{8,10},{9,11},{10,... | collective-permute-start | bytes 393224 | tf_op jit(solution)/shard_map/ppermute | solution.py:453
  49.5 13.7 %all-to-all-start.4 = ((f32[8,8,128]{2,1,0:T(8,128)}), f32[8,8,128]{2,1,0:T(8,128)S(1)}, u32[]{:S(2)}, u32[]{:S(2)}) async-start(f32[8,8,128]{2,1,0:T(8,128)} %pieces.3.after), calls=%async_computation.4 | async-start | bytes 65536 | tf_op jit(solution)/shard_map/all_to_all | solution.py:467
  65.4 16.8 %all-to-all-start.5 = ((f32[4,376,128]{2,1,0:T(8,128)}), f32[4,376,128]{2,1,0:T(8,128)S(1)}, u32[]{:S(2)}, u32[]{:S(2)}) async-start(f32[4,376,128]{2,1,0:T(8,128)} %collect.3), calls=%async_computation.5 | async-start | bytes 1540096 | tf_op jit(solution)/shard_map/all_to_all | solution.py:470
  72.5 7.5 %collective-permute-start.14 = (f32[128,512]{1,0:T(8,128)S(1)}, f32[128,512]{1,0:T(8,128)S(1)}, u32[]{:S(2)}, u32[]{:S(2)}) collective-permute-start(f32[128,512]{1,0:T(8,128)S(1)} %get-tuple-element.74.first), channel_id=1, source_target_pairs={{0,1},{1,0},{2,3},{3,2},{4,5},{5,4},{6,7},{7,6},{8,9},{9,8},{10,11... | collective-permute-start | bytes 786440 | tf_op jit(solution)/shard_map/ppermute | solution.py:453
  82.2 7.2 %collective-permute-start.15 = (f32[4,376,128]{2,1,0:T(8,128)S(1)}, f32[4,376,128]{2,1,0:T(8,128)S(1)}, u32[]{:S(2)}, u32[]{:S(2)}) collective-permute-start(f32[4,376,128]{2,1,0:T(8,128)S(1)} %all-to-all-done.5.own), channel_id=1, source_target_pairs={{0,8},{8,0},{1,9},{9,1},{2,10},{10,2},{3,11},{11,3},{4,12},{12,4},... | collective-permute-start | bytes 2310152 | tf_op jit(solution)/shard_map/ppermute | solution.py:441

commit v9 on v8

--- a/solution.py
+++ b/solution.py
@@ -16,6 +16,7 @@
 COLS = BLOCKS * LANES
 DIAG = NB // Y
 BATCH = 16
+PIECE = DIAG // X * NB // LANES
 DISTANCES = (4, 2, 1)
 FILLER, PLACE, TOPS = 0, NB, 2 * NB
 COUNT = TOPS + NB + 8
@@ -102,28 +103,17 @@
     table[MOST] = peak + found
 
 
-def early_plan_kernel(*refs):
-    @pl.when(lax.axis_index("z") == 0)
-    def _():
-        plan_kernel(*refs)
-
-
-def late_plan_kernel(pivots, after, table, content):
-    plan_kernel(pivots, table, content)
-
-
-def make_plan(pivots, after=None):
-    early = after is None
+def make_plan(pivots):
     return pl.pallas_call(
-        early_plan_kernel if early else late_plan_kernel,
+        plan_kernel,
         out_shape=jax.ShapeDtypeStruct((TABLE,), jnp.int32),
-        in_specs=[SMEM] if early else [SMEM, VMEM],
+        in_specs=[SMEM],
         out_specs=SMEM,
         scratch_shapes=[pltpu.SMEM((ORDER,), jnp.int32)],
         compiler_params=PARAMS,
         cost_estimate=pl.CostEstimate(flops=0, bytes_accessed=16 * 1024 * 1024, transcendentals=0),
         name="plan",
-    )(*([pivots] if early else [pivots, after]))
+    )(pivots)
 
 
 def invert_diagonal(panel_t, at):
@@ -169,8 +159,9 @@
     for out, side in sides:
         for x in range(X):
             out[x, :cap, :] = jnp.zeros((cap, LANES), jnp.float32)
-            lanes = pl.ds(pl.multiple_of(side * LANES, LANES), LANES)
-            out[x, cap + NB :, :] = triangle[8 * x : 8 * x + 8, lanes]
+            for h in range(2):
+                at = cap + NB + 8 * h
+                out[x, at : at + 8, :] = triangle[8 * x : 8 * x + 8, h * LANES : (h + 1) * LANES]
     copy.wait()
     for out, side in sides:
         for x in range(X):
@@ -238,12 +229,13 @@
         loop(table[COUNT + Z], top)
 
 
-def pieces_kernel(token, got, out):
-    for y in range(Y):
-        out[y] = got[0, got.shape[1] - 8 :, :]
-
-
-def collect_kernel(cap, room, table, token, got, pieces, out):
+def slice_kernel(token, own, out):
+    for x in range(X):
+        for y in range(Y):
+            out[y, x * PIECE : (x + 1) * PIECE, :] = own[x, own.shape[1] - PIECE :, :]
+
+
+def collect_kernel(cap, room, table, token, got, out):
     z = lax.axis_index("z")
 
     def take(k):
@@ -264,8 +256,7 @@
 
     loop(table[COUNT + Z], top)
     out[0, NB : NB + cap, :] = got[0, cap : 2 * cap, :]
-    for y in range(Y):
-        out[0, NB + cap + 8 * y : NB + cap + 8 * y + 8, :] = pieces[y]
+    out[0, NB + cap :, :] = got[0, cap + room :, :]
     for x in range(1, X):
         out[x] = out[0]
 
@@ -314,18 +305,18 @@
     out[...] = ordered[...].T
 
 
-def finish_kernel(cap, mine, own, other, multipliers, trailing, out,
+def finish_kernel(cap, mine, whole, own, other, multipliers, trailing, out,
                   upper, inverse, block, current, in_sem, out_sem):
     copy = pltpu.make_async_copy(trailing, current, in_sem)
     copy.start()
     c = lax.axis_index("c")
     first = first_row()
     sides = ((pl.multiple_of(c * LANES, LANES), own), (pl.multiple_of((1 - c) * LANES, LANES), other))
-    for x in range(X):
-        for lane, ref in sides:
-            for y in range(Y):
-                at = DIAG * y + 8 * x
-                upper[at : at + 8, pl.ds(lane, LANES)] = ref[x, NB + cap + 8 * y : NB + cap + 8 * y + 8, :]
+    for y in range(Y):
+        for x in range(X):
+            for h in range(2):
+                at, start = DIAG * y + 8 * x, PIECE * x + 8 * h
+                upper[at : at + 8, h * LANES : (h + 1) * LANES] = whole[y, start : start + 8, :]
     inverse[...] = invert(upper)
     copy.wait()
 
@@ -408,7 +399,7 @@
 
 def pack(cap, pivots, trailing, panel_t):
     scratch = [pltpu.VMEM((DIAG, NB), jnp.float32), pltpu.VMEM((ROWS, COLS), jnp.float32), pltpu.SemaphoreType.DMA]
-    return call(functools.partial(pack_kernel, cap), [(X, cap + NB + 8, LANES)] * 2,
+    return call(functools.partial(pack_kernel, cap), [(X, cap + NB + PIECE, LANES)] * 2,
                 (pivots,), (panel_t, trailing), scratch, name="pack", last=ANY, table=NB + 8)
 
 
@@ -417,20 +408,20 @@
 
 
 def spread(cap, room, plan, blocks, panel_t):
-    return call(functools.partial(spread_kernel, cap, room), [(Z, cap + room + 8, LANES), panel_t.shape],
-                (plan,), (*blocks, panel_t), [pltpu.VMEM((NB + 8, LANES), jnp.float32)], name="spread")
-
-
-def collect(cap, room, plan, token, planes, pieces):
-    return call(functools.partial(collect_kernel, cap, room), (X, NB + cap + 8 * Y, LANES),
-                (plan,), (token, planes, pieces), name="collect")
-
-
-def finish(cap, mine, own, other, multipliers, trailing):
+    return call(functools.partial(spread_kernel, cap, room), [(Z, cap + room + PIECE, LANES), panel_t.shape],
+                (plan,), (*blocks, panel_t), [pltpu.VMEM((NB + PIECE, LANES), jnp.float32)], name="spread")
+
+
+def collect(cap, room, plan, token, planes):
+    return call(functools.partial(collect_kernel, cap, room), (X, NB + cap + PIECE, LANES),
+                (plan,), (token, planes), name="collect")
+
+
+def finish(cap, mine, whole, own, other, multipliers, trailing):
     scratch = [pltpu.VMEM(s, jnp.float32) for s in ((NB, NB), (NB, NB), (2, NB, C * LANES), (ROWS, COLS))]
     scratch += [pltpu.SemaphoreType.DMA, pltpu.SemaphoreType.DMA((X,))]
     return call(functools.partial(finish_kernel, cap), (ROWS, COLS), (mine,),
-                (own, other, multipliers, trailing), scratch, name="finish",
+                (whole, own, other, multipliers, trailing), scratch, name="finish",
                 last=ANY, out=pl.BlockSpec(memory_space=pltpu.HBM), busy=16)
 
 
@@ -446,7 +437,8 @@
     blocks = join(cap, keep, other_core(send))
     for s in range(1, X):
         blocks[s] = lax.ppermute(blocks[s], "x", [(x, (x + s) % X) for x in range(X)])
-    return *spread(cap, room, make_plan(pivots), blocks, panel_t), mine
+    plan = make_plan(pivots)
+    return *spread(cap, room, plan, blocks, panel_t), plan, mine
 
 
 def from_column(values, distance):
@@ -458,26 +450,25 @@
     return call(double_kernel, [shape, (8, LANES)], (), (slices, from_column(slices, distance)), name="double")
 
 
-def later_phases(cap, room, planes, slices, pivots):
+def later_phases(cap, room, planes, slices, plan):
     slices, token = doubled(slices, DISTANCES[0])
-    planes = swap(planes, "z")
-    pieces = call(pieces_kernel, (Y, 8, LANES), (), (token, planes), name="pieces")
-    plan = make_plan(pivots, pieces)
+    blocks = collect(cap, room, plan, token, swap(planes, "z"))
     slices, token = doubled(slices, DISTANCES[1])
-    blocks = collect(cap, room, plan, token, planes, swap(pieces, "y"))
+    own = swap(blocks, "x")
+    whole = swap(call(slice_kernel, (Y, X * PIECE, LANES), (), (token, own), name="slice"), "y")
+    other = other_core(own)
     slices, _ = doubled(slices, DISTANCES[2])
     multipliers = call(turn_kernel, (ROWS, NB), (), (slices,), [pltpu.VMEM((NB, ROWS), jnp.float32)], name="turn")
-    own, multipliers = lax.optimization_barrier((swap(blocks, "x"), multipliers))
-    return plan[MOST], own, other_core(own), multipliers
+    return whole, own, other, multipliers
 
 
 def shards(panel, trailing, pivots):
     panel_t = panel.T
 
     def with_room(cap, room):
-        planes, slices, mine = first_phase(cap, room, panel_t, trailing, pivots)
-        most, *ready = later_phases(cap, room, planes, slices, pivots)
-        return most, finish(cap, mine, *ready, trailing)
+        planes, slices, plan, mine = first_phase(cap, room, panel_t, trailing, pivots)
+        ready = later_phases(cap, room, planes, slices, plan)
+        return plan[MOST], finish(cap, mine, *ready, trailing)
 
     def pending(carry):
         return carry[0]

time: 96.9 us -> 112 us (1.16)
  blocking collectives: 0 us -> 15 us
  waiting for transfers between devices: 14.4 us -> 26.7 us
  starting transfers between devices: 54.7 us -> 47.6 us
  Pallas kernels: 25.6 us -> 21 us
    all_to_all x0 -> x1, blocking collectives: none -> 15 us  [later_phases(): own = swap(blocks, 'x')]
    ppermute x3, waiting for transfers between devices: 7 us -> 16.4 us  [from_column(): return lax.ppermute(values, 'y', [(y, y ^ distance) for y in range(Y)])]
    all_to_all x3 -> x2, starting transfers between devices: 17.8 us -> 11.6 us  [the longest x1 7.01 us: later_phases(): swap(call(slice_kernel, (Y, X * PIECE, LANES), (), (token, own), name='sl...]
    pallas_call x2 -> x1, Pallas kernels: 9.42 us -> 4.59 us  [make_plan(): pl.pallas_call(plan_kernel, out_shape=jax.ShapeDtypeStruct((TABLE,), jnp....]
    all_to_all x3 -> x2, waiting for transfers between devices: 3.96 us -> 7.25 us  [the longest x1 7.25 us: later_phases(): blocks = collect(cap, room, plan, token, swap(planes, 'z'))]
    ppermute x2, starting transfers between devices: 14.2 us -> 12.6 us  [other_core(): return lax.ppermute(values, 'c', [(0, 1), (1, 0)])]
  transfers between devices with their start and end apart: 11 -> 10, of which waited for: 8 -> 6; matrix products, arithmetic and copies ran while one was open for 1% -> 1% of each run, Pallas kernels for 11% -> 6%
where the time goes in v9:
time: 112 us
  starting transfers between devices  47.6 us (42%)
  waiting for transfers between devices  26.7 us (24%)
  Pallas kernels  21 us (19%)
  blocking collectives  15 us (13%)
    pallas_call x10, Pallas kernels, call(): pl.pallas_call(kernel, out_shape=shapes, in_specs=[SMEM] * len(smem) + [V...  16.4 us
    ppermute x3, waiting for transfers between devices, from_column(): return lax.ppermute(values, 'y', [(y, y ^ distance) for y in range(Y)])  16.4 us
    ppermute x3, starting transfers between devices, from_column(): return lax.ppermute(values, 'y', [(y, y ^ distance) for y in range(Y)])  15 us
    all_to_all x1, blocking collectives, later_phases(): own = swap(blocks, 'x')  15 us
    ppermute x2, starting transfers between devices, other_core(): return lax.ppermute(values, 'c', [(0, 1), (1, 0)])  12.6 us
    ppermute x3, starting transfers between devices, first_phase(): lax.ppermute(blocks[s], 'x', [(x, (x + s) % X) for x in range(X)])  8.41 us
    all_to_all x1, waiting for transfers between devices, later_phases(): blocks = collect(cap, room, plan, token, swap(planes, 'z'))  7.25 us
    all_to_all x1, starting transfers between devices, later_phases(): swap(call(slice_kernel, (Y, X * PIECE, LANES), (), (token, own), name='sl...  7.01 us
  transfers between devices with their start and end apart: 10, of which 6 were waited for; matrix products, arithmetic and copies ran while one was open for 1% of the time, Pallas kernels for 6%

profile of v9, /device:TPU:1, one launch (start us, length us, event | category | flops | bytes accessed | tf_op | source)
XLA Modules:
  0.0 111.7 jit_solution(8601288337967751993)
XLA Ops:
  0.0 3.4 %pack.3 = (f32[4,328,128]{2,1,0:T(8,128)S(1)}, f32[4,328,128]{2,1,0:T(8,128)S(1)}, s32[264]{0:T(512)S(1)}) custom-call(s32[256]{0:T(256)} %pivots.3, f32[32,512]{1,0:T(8,128)} %bitcast.2, f32[512,1024]{1,0:T(8,128)} %trailing.3), custom_call_target="tpu_custom_call" | custom-call | bytes 2097152 | tf_op jit(solution)/shard_map/pack/pallas_call | solution.py:387
  3.4 8.7 %collective-permute-start.8 = (f32[4,328,128]{2,1,0:T(8,128)S(1)}, f32[4,328,128]{2,1,0:T(8,128)S(1)}, u32[]{:S(2)}, u32[]{:S(2)}) collective-permute-start(f32[4,328,128]{2,1,0:T(8,128)S(1)} %get-tuple-element.60), channel_id=1, source_target_pairs={{0,8},{8,0},{1,9},{9,1},{2,10},{10,2},{3,11},{11,3},{4,12},{12,4},... | collective-permute-start | bytes 2015240 | tf_op jit(solution)/shard_map/ppermute | solution.py:432
  12.1 1.7 %collective-permute-done.8.got = f32[4,328,128]{2,1,0:T(8,128)S(1)} collective-permute-done((f32[4,328,128]{2,1,0:T(8,128)S(1)}, f32[4,328,128]{2,1,0:T(8,128)S(1)}, u32[]{:S(2)}, u32[]{:S(2)}) %collective-permute-start.8) | collective-permute-done | bytes 671776 | tf_op jit(solution)/shard_map/ppermute | solution.py:432
  13.9 1.9 %collective-permute-start.9 = (f32[328,128]{1,0:T(8,128)S(1)}, f32[328,128]{1,0:T(8,128)S(1)}, u32[]{:S(2)}, u32[]{:S(2)}) collective-permute-start(f32[328,128]{1,0:T(8,128)S(1)} %get-tuple-element.62), channel_id=1, source_target_pairs={{0,128},{128,256},{256,384},{384,0},{1,129},{129,257},{257,385},{3... | collective-permute-start | bytes 503816 | tf_op jit(solution)/shard_map/ppermute | solution.py:439
  15.9 1.9 %collective-permute-start.10 = (f32[328,128]{1,0:T(8,128)S(1)}, f32[328,128]{1,0:T(8,128)S(1)}, u32[]{:S(2)}, u32[]{:S(2)}) collective-permute-start(f32[328,128]{1,0:T(8,128)S(1)} %get-tuple-element.63), channel_id=1, source_target_pairs={{0,256},{128,384},{256,0},{384,128},{1,257},{129,385},{257,1},{385... | collective-permute-start | bytes 503816 | tf_op jit(solution)/shard_map/ppermute | solution.py:439
  17.8 4.6 %collective-permute-start.11 = (f32[328,128]{1,0:T(8,128)S(1)}, f32[328,128]{1,0:T(8,128)S(1)}, u32[]{:S(2)}, u32[]{:S(2)}) collective-permute-start(f32[328,128]{1,0:T(8,128)S(1)} %get-tuple-element.64), channel_id=1, source_target_pairs={{0,384},{128,0},{256,128},{384,256},{1,385},{129,1},{257,129},{385... | collective-permute-start | bytes 503816 | tf_op jit(solution)/shard_map/ppermute | solution.py:439
  22.4 4.6 %plan.3.table = s32[1024]{0:T(1024)S(1)} custom-call(s32[256]{0:T(256)S(1)} %copy-done.4), custom_call_target="tpu_custom_call" | custom-call | bytes 16777216 | tf_op jit(solution)/shard_map/plan/pallas_call | solution.py:107
  27.0 1.3 %collective-permute-done.11.refs_3_ = f32[328,128]{1,0:T(8,128)S(1)} collective-permute-done((f32[328,128]{1,0:T(8,128)S(1)}, f32[328,128]{1,0:T(8,128)S(1)}, u32[]{:S(2)}, u32[]{:S(2)}) %collective-permute-start.11) | collective-permute-done | bytes 167968 | tf_op jit(solution)/shard_map/ppermute | solution.py:439
  28.3 2.4 %spread.3 = (f32[8,128,128]{2,1,0:T(8,128)}, f32[32,512]{1,0:T(8,128)S(1)}) custom-call(s32[1024]{0:T(1024)S(1)} %plan.3.table, f32[328,128]{1,0:T(8,128)S(1)} %get-tuple-element.61.refs_0_, f32[328,128]{1,0:T(8,128)S(1)} %collective-permute-done.9.refs_1_, f32[328,128]{1,0:T(8,128)S(1)} %collective-permute-done.10.refs_2_, ...), custom_call_target="tpu_custom_call" | custom-call | bytes 2097152 | tf_op jit(solution)/shard_map/spread/pallas_call | solution.py:387
  30.7 4.6 %all-to-all-start.3 = ((f32[8,128,128]{2,1,0:T(8,128)}), f32[8,128,128]{2,1,0:T(8,128)S(1)}, u32[]{:S(2)}, u32[]{:S(2)}) async-start(f32[8,128,128]{2,1,0:T(8,128)} %get-tuple-element.69), calls=%async_computation.3 | async-start | bytes 1048576 | tf_op jit(solution)/shard_map/all_to_all | solution.py:455
  35.3 7.4 %collective-permute-start.12 = (f32[32,512]{1,0:T(8,128)S(1)}, f32[32,512]{1,0:T(8,128)S(1)}, u32[]{:S(2)}, u32[]{:S(2)}) collective-permute-start(f32[32,512]{1,0:T(8,128)S(1)} %get-tuple-element.65.first), channel_id=1, source_target_pairs={{0,4},{1,5},{2,6},{3,7},{4,0},{5,1},{6,2},{7,3},{8,12},{9,13},{10,... | collective-permute-start | bytes 196616 | tf_op jit(solution)/shard_map/ppermute | solution.py:445
  42.8 1.7 %collective-permute-done.12.second = f32[32,512]{1,0:T(8,128)S(1)} collective-permute-done((f32[32,512]{1,0:T(8,128)S(1)}, f32[32,512]{1,0:T(8,128)S(1)}, u32[]{:S(2)}, u32[]{:S(2)}) %collective-permute-start.12) | collective-permute-done | bytes 65568 | tf_op jit(solution)/shard_map/ppermute | solution.py:445
  44.5 7.2 %all-to-all-done.3.got = f32[8,128,128]{2,1,0:T(8,128)S(1)} async-done(((f32[8,128,128]{2,1,0:T(8,128)}), f32[8,128,128]{2,1,0:T(8,128)S(1)}, u32[]{:S(2)}, u32[]{:S(2)}) %all-to-all-start.3) | async-done | bytes 524320 | tf_op jit(solution)/shard_map/all_to_all | solution.py:455
  51.7 1.3 %collect.3 = f32[4,328,128]{2,1,0:T(8,128)S(1)} custom-call(s32[1024]{0:T(1024)S(1)} %plan.3.table, f32[8,128]{1,0:T(8,128)S(1)} %get-tuple-element.68.token, f32[8,128,128]{2,1,0:T(8,128)S(1)} %all-to-all-done.3.got), custom_call_target="tpu_custom_call" | custom-call | bytes 2097152 | tf_op jit(solution)/shard_map/collect/pallas_call | solution.py:387
  53.1 15.0 %all_to_all.28.own = f32[4,328,128]{2,1,0:T(8,128)S(1)} all-to-all(f32[4,328,128]{2,1,0:T(8,128)S(1)} %collect.3), channel_id=1, replica_groups=mesh['x'=4,'z'=8,'c'=2,'y'=8] {'x'}, dimensions={0} | all-to-all | bytes 1343488 | tf_op jit(solution)/shard_map/all_to_all | solution.py:457
  68.1 3.9 %collective-permute-start.14 = (f32[4,328,128]{2,1,0:T(8,128)S(1)}, f32[4,328,128]{2,1,0:T(8,128)S(1)}, u32[]{:S(2)}, u32[]{:S(2)}) collective-permute-start(f32[4,328,128]{2,1,0:T(8,128)S(1)} %all_to_all.28.own), channel_id=1, source_target_pairs={{0,8},{8,0},{1,9},{9,1},{2,10},{10,2},{3,11},{11,3},{4,12},{12,4},... | collective-permute-start | bytes 2015240 | tf_op jit(solution)/shard_map/ppermute | solution.py:432
  71.9 4.2 %collective-permute-start.13 = (f32[64,512]{1,0:T(8,128)S(1)}, f32[64,512]{1,0:T(8,128)S(1)}, u32[]{:S(2)}, u32[]{:S(2)}) collective-permute-start(f32[64,512]{1,0:T(8,128)S(1)} %get-tuple-element.66.first), channel_id=1, source_target_pairs={{0,2},{1,3},{2,0},{3,1},{4,6},{5,7},{6,4},{7,5},{8,10},{9,11},{10,... | collective-permute-start | bytes 393224 | tf_op jit(solution)/shard_map/ppermute | solution.py:445
  76.1 6.5 %collective-permute-done.13.second = f32[64,512]{1,0:T(8,128)S(1)} collective-permute-done((f32[64,512]{1,0:T(8,128)S(1)}, f32[64,512]{1,0:T(8,128)S(1)}, u32[]{:S(2)}, u32[]{:S(2)}) %collective-permute-start.13) | collective-permute-done | bytes 131104 | tf_op jit(solution)/shard_map/ppermute | solution.py:445
  82.7 0.7 slice.7
  83.4 7.0 %all-to-all-start.5 = ((f32[8,64,128]{2,1,0:T(8,128)}), f32[8,64,128]{2,1,0:T(8,128)S(1)}, u32[]{:S(2)}, u32[]{:S(2)}) async-start(f32[8,64,128]{2,1,0:T(8,128)} %slice.7), calls=%async_computation.5 | async-start | bytes 524288 | tf_op jit(solution)/shard_map/all_to_all | solution.py:458
  90.4 3.4 %collective-permute-start.15 = (f32[128,512]{1,0:T(8,128)S(1)}, f32[128,512]{1,0:T(8,128)S(1)}, u32[]{:S(2)}, u32[]{:S(2)}) collective-permute-start(f32[128,512]{1,0:T(8,128)S(1)} %get-tuple-element.70.first), channel_id=1, source_target_pairs={{0,1},{1,0},{2,3},{3,2},{4,5},{5,4},{6,7},{7,6},{8,9},{9,8},{10,11... | collective-permute-start | bytes 786440 | tf_op jit(solution)/shard_map/ppermute | solution.py:445
  95.0 8.2 %collective-permute-done.15.second = f32[128,512]{1,0:T(8,128)S(1)} collective-permute-done((f32[128,512]{1,0:T(8,128)S(1)}, f32[128,512]{1,0:T(8,128)S(1)}, u32[]{:S(2)}, u32[]{:S(2)}) %collective-permute-start.15) | collective-permute-done | bytes 262176 | tf_op jit(solution)/shard_map/ppermute | solution.py:445
  103.2 0.6 double.11
  104.1 7.7 %finish.3 = f32[512,1024]{1,0:T(8,128)} custom-call(s32[264]{0:T(512)S(1)} %get-tuple-element.58.mine, f32[8,64,128]{2,1,0:T(8,128)S(1)} %all-to-all-done.5.whole, f32[4,328,128]{2,1,0:T(8,128)S(1)} %all_to_all.28.own, f32[4,328,128]{2,1,0:T(8,128)S(1)} %collective-permute-done.14.other, f32[512,256]{1,0:T(8,128)S(1)} %turn.3.multipliers, f32[512,1024]{1,0:T(8,128)} %trailing.3), custom_call_target="tpu_custom_call" | custom-call | bytes 16777216 | tf_op jit(solution)/shard_map/finish/pallas_call | solution.py:387
  (16 shorter events, 1.0 us)
Async XLA Ops:
  0.0 22.4 %copy-start.4 = (s32[256]{0:T(256)S(1)}, s32[256]{0:T(256)}, u32[]{:S(2)}) copy-start(s32[256]{0:T(256)} %pivots.3) | copy-start | bytes 3076
  0.0 28.3 %copy-start.3 = (f32[512,32]{0,1:T(8,128)S(1)}, f32[512,32]{0,1:T(8,128)}, u32[]{:S(2)}) copy-start(f32[512,32]{0,1:T(8,128)} %param.5) | copy-start | bytes 196612
  3.4 10.5 %collective-permute-start.8 = (f32[4,328,128]{2,1,0:T(8,128)S(1)}, f32[4,328,128]{2,1,0:T(8,128)S(1)}, u32[]{:S(2)}, u32[]{:S(2)}) collective-permute-start(f32[4,328,128]{2,1,0:T(8,128)S(1)} %get-tuple-element.60), channel_id=1, source_target_pairs={{0,8},{8,0},{1,9},{9,1},{2,10},{10,2},{3,11},{11,3},{4,12},{12,4},... | collective-permute-start | bytes 2015240 | tf_op jit(solution)/shard_map/ppermute | solution.py:432
  13.9 13.0 %collective-permute-start.9 = (f32[328,128]{1,0:T(8,128)S(1)}, f32[328,128]{1,0:T(8,128)S(1)}, u32[]{:S(2)}, u32[]{:S(2)}) collective-permute-start(f32[328,128]{1,0:T(8,128)S(1)} %get-tuple-element.62), channel_id=1, source_target_pairs={{0,128},{128,256},{256,384},{384,0},{1,129},{129,257},{257,385},{3... | collective-permute-start | bytes 503816 | tf_op jit(solution)/shard_map/ppermute | solution.py:439
  15.9 11.1 %collective-permute-start.10 = (f32[328,128]{1,0:T(8,128)S(1)}, f32[328,128]{1,0:T(8,128)S(1)}, u32[]{:S(2)}, u32[]{:S(2)}) collective-permute-start(f32[328,128]{1,0:T(8,128)S(1)} %get-tuple-element.63), channel_id=1, source_target_pairs={{0,256},{128,384},{256,0},{384,128},{1,257},{129,385},{257,1},{385... | collective-permute-start | bytes 503816 | tf_op jit(solution)/shard_map/ppermute | solution.py:439
  17.8 10.5 %collective-permute-start.11 = (f32[328,128]{1,0:T(8,128)S(1)}, f32[328,128]{1,0:T(8,128)S(1)}, u32[]{:S(2)}, u32[]{:S(2)}) collective-permute-start(f32[328,128]{1,0:T(8,128)S(1)} %get-tuple-element.64), channel_id=1, source_target_pairs={{0,384},{128,0},{256,128},{384,256},{1,385},{129,1},{257,129},{385... | collective-permute-start | bytes 503816 | tf_op jit(solution)/shard_map/ppermute | solution.py:439
  30.7 21.1 %all-to-all-start.3 = ((f32[8,128,128]{2,1,0:T(8,128)}), f32[8,128,128]{2,1,0:T(8,128)S(1)}, u32[]{:S(2)}, u32[]{:S(2)}) async-start(f32[8,128,128]{2,1,0:T(8,128)} %get-tuple-element.69), calls=%async_computation.3 | async-start | bytes 1048576 | tf_op jit(solution)/shard_map/all_to_all | solution.py:455
  35.3 9.2 %collective-permute-start.12 = (f32[32,512]{1,0:T(8,128)S(1)}, f32[32,512]{1,0:T(8,128)S(1)}, u32[]{:S(2)}, u32[]{:S(2)}) collective-permute-start(f32[32,512]{1,0:T(8,128)S(1)} %get-tuple-element.65.first), channel_id=1, source_target_pairs={{0,4},{1,5},{2,6},{3,7},{4,0},{5,1},{6,2},{7,3},{8,12},{9,13},{10,... | collective-permute-start | bytes 196616 | tf_op jit(solution)/shard_map/ppermute | solution.py:445
  68.1 36.0 %collective-permute-start.14 = (f32[4,328,128]{2,1,0:T(8,128)S(1)}, f32[4,328,128]{2,1,0:T(8,128)S(1)}, u32[]{:S(2)}, u32[]{:S(2)}) collective-permute-start(f32[4,328,128]{2,1,0:T(8,128)S(1)} %all_to_all.28.own), channel_id=1, source_target_pairs={{0,8},{8,0},{1,9},{9,1},{2,10},{10,2},{3,11},{11,3},{4,12},{12,4},... | collective-permute-start | bytes 2015240 | tf_op jit(solution)/shard_map/ppermute | solution.py:432
  71.9 10.7 %collective-permute-start.13 = (f32[64,512]{1,0:T(8,128)S(1)}, f32[64,512]{1,0:T(8,128)S(1)}, u32[]{:S(2)}, u32[]{:S(2)}) collective-permute-start(f32[64,512]{1,0:T(8,128)S(1)} %get-tuple-element.66.first), channel_id=1, source_target_pairs={{0,2},{1,3},{2,0},{3,1},{4,6},{5,7},{6,4},{7,5},{8,10},{9,11},{10,... | collective-permute-start | bytes 393224 | tf_op jit(solution)/shard_map/ppermute | solution.py:445
  83.4 20.7 %all-to-all-start.5 = ((f32[8,64,128]{2,1,0:T(8,128)}), f32[8,64,128]{2,1,0:T(8,128)S(1)}, u32[]{:S(2)}, u32[]{:S(2)}) async-start(f32[8,64,128]{2,1,0:T(8,128)} %slice.7), calls=%async_computation.5 | async-start | bytes 524288 | tf_op jit(solution)/shard_map/all_to_all | solution.py:458
  90.4 12.8 %collective-permute-start.15 = (f32[128,512]{1,0:T(8,128)S(1)}, f32[128,512]{1,0:T(8,128)S(1)}, u32[]{:S(2)}, u32[]{:S(2)}) collective-permute-start(f32[128,512]{1,0:T(8,128)S(1)} %get-tuple-element.70.first), channel_id=1, source_target_pairs={{0,1},{1,0},{2,3},{3,2},{4,5},{5,4},{6,7},{7,6},{8,9},{9,8},{10,11... | collective-permute-start | bytes 786440 | tf_op jit(solution)/shard_map/ppermute | solution.py:445
  104.0 7.7 %copy-start.1 = (f32[512,1024]{1,0:T(8,128)S(1)}, f32[512,1024]{1,0:T(8,128)}, u32[]{:S(2)}) copy-start(f32[512,1024]{1,0:T(8,128)} %trailing.3) | copy-start | bytes 6291460

commit v10 on v8

--- a/solution.py
+++ b/solution.py
@@ -29,6 +29,7 @@
 VMEM = pl.BlockSpec(memory_space=pltpu.VMEM)
 SMEM = pl.BlockSpec(memory_space=pltpu.SMEM)
 ANY = pl.BlockSpec(memory_space=pl.ANY)
+HBM = pl.BlockSpec(memory_space=pltpu.HBM)
 PARAMS = pltpu.CompilerParams(vmem_limit_bytes=48 * 1024 * 1024)
 
 
@@ -203,20 +204,22 @@
 def spread_kernel(cap, room, table, *refs):
     blocks, panel_t, out, panel_out, former = refs[:X], *refs[X:]
     x = lax.axis_index("x")
-    rest = blocks[0][cap:, :]
-    for s in range(1, X):
-        rest = jnp.where(x == s, blocks[s][cap:, :], rest)
-    former[...] = rest
     rows = blocks[0][:cap, :]
     for s in range(1, X):
         rows = rows + blocks[s][:cap, :]
     for z in range(Z):
         out[z, :cap, :] = rows
-        out[z, cap + room :, :] = former[NB:, :]
     panel_out[...] = panel_t[...]
 
     @pl.when(lax.axis_index("z") == 0)
     def _():
+        rest = blocks[0][cap:, :]
+        for s in range(1, X):
+            rest = jnp.where(x == s, blocks[s][cap:, :], rest)
+        former[...] = rest
+        for z in range(Z):
+            out[z, cap + room :, :] = former[NB:, :]
+
         def put(k):
             moves = []
             for i in range(BATCH):
@@ -243,7 +246,7 @@
         out[y] = got[0, got.shape[1] - 8 :, :]
 
 
-def collect_kernel(cap, room, table, token, got, pieces, out):
+def collect_kernel(cap, room, table, token, got, out, block, sem):
     z = lax.axis_index("z")
 
     def take(k):
@@ -254,20 +257,31 @@
             rank = jnp.minimum(where & (NB - 1), cap - 1)
             rows.append(got[where >> BITS, pl.ds(rank, 1), :])
         for i in range(BATCH):
-            out[0, pl.ds(base + i, 1), :] = rows[i]
+            block[pl.ds(base + i, 1), :] = rows[i]
 
     loop(NB // BATCH, take)
 
     def top(k):
         at = cap + jnp.minimum(table[COUNT + z] + k, room - 1)
-        out[0, pl.ds(table[TOPS + k] >> BITS, 1), :] = got[0, pl.ds(at, 1), :]
+        block[pl.ds(table[TOPS + k] >> BITS, 1), :] = got[0, pl.ds(at, 1), :]
 
     loop(table[COUNT + Z], top)
-    out[0, NB : NB + cap, :] = got[0, cap : 2 * cap, :]
+    block[NB:, :] = got[0, cap : 2 * cap, :]
+    copies = [pltpu.make_async_copy(block, out.at[x, pl.ds(0, NB + cap), :], sem.at[x]) for x in range(X)]
+    for copy in copies:
+        copy.start()
+    for copy in copies:
+        copy.wait()
+
+
+def append_kernel(cap, pieces, blocks, out, rows, sem):
     for y in range(Y):
-        out[0, NB + cap + 8 * y : NB + cap + 8 * y + 8, :] = pieces[y]
-    for x in range(1, X):
-        out[x] = out[0]
+        rows[8 * y : 8 * y + 8, :] = pieces[y]
+    copies = [pltpu.make_async_copy(rows, out.at[x, pl.ds(NB + cap, 8 * Y), :], sem.at[x]) for x in range(X)]
+    for copy in copies:
+        copy.start()
+    for copy in copies:
+        copy.wait()
 
 
 def dot(a, b):
@@ -386,7 +400,7 @@
         write(x).wait()
 
 
-def call(kernel, shape, smem, vmem, scratch=(), name=None, last=VMEM, out=VMEM, busy=2, table=None):
+def call(kernel, shape, smem, vmem, scratch=(), name=None, last=VMEM, out=VMEM, busy=2, table=None, aliases={}):
     many = isinstance(shape, list)
     shapes = [jax.ShapeDtypeStruct(s, jnp.float32) for s in (shape if many else [shape])]
     specs = [out] * len(shapes)
@@ -400,6 +414,7 @@
         out_specs=specs,
         scratch_shapes=list(scratch),
         compiler_params=PARAMS,
+        input_output_aliases=aliases,
         cost_estimate=pl.CostEstimate(flops=0, bytes_accessed=busy * 2**20, transcendentals=0),
         name=name,
     )(*smem, *vmem)
@@ -421,9 +436,16 @@
                 (plan,), (*blocks, panel_t), [pltpu.VMEM((NB + 8, LANES), jnp.float32)], name="spread")
 
 
-def collect(cap, room, plan, token, planes, pieces):
+def collect(cap, room, plan, token, planes):
+    scratch = [pltpu.VMEM((NB + cap, LANES), jnp.float32), pltpu.SemaphoreType.DMA((X,))]
     return call(functools.partial(collect_kernel, cap, room), (X, NB + cap + 8 * Y, LANES),
-                (plan,), (token, planes, pieces), name="collect")
+                (plan,), (token, planes), scratch, name="collect", out=HBM)
+
+
+def append(cap, pieces, blocks):
+    scratch = [pltpu.VMEM((8 * Y, LANES), jnp.float32), pltpu.SemaphoreType.DMA((X,))]
+    return call(functools.partial(append_kernel, cap), blocks.shape, (), (pieces, blocks), scratch,
+                name="append", last=HBM, out=HBM, aliases={1: 0})
 
 
 def finish(cap, mine, own, other, multipliers, trailing):
@@ -431,7 +453,7 @@
     scratch += [pltpu.SemaphoreType.DMA, pltpu.SemaphoreType.DMA((X,))]
     return call(functools.partial(finish_kernel, cap), (ROWS, COLS), (mine,),
                 (own, other, multipliers, trailing), scratch, name="finish",
-                last=ANY, out=pl.BlockSpec(memory_space=pltpu.HBM), busy=16)
+                last=ANY, out=HBM, busy=16)
 
 
 swap = functools.partial(lax.all_to_all, split_axis=0, concat_axis=0, tiled=True)
@@ -464,7 +486,7 @@
     pieces = call(pieces_kernel, (Y, 8, LANES), (), (token, planes), name="pieces")
     plan = make_plan(pivots, pieces)
     slices, token = doubled(slices, DISTANCES[1])
-    blocks = collect(cap, room, plan, token, planes, swap(pieces, "y"))
+    blocks = append(cap, swap(pieces, "y"), collect(cap, room, plan, token, planes))
     slices, _ = doubled(slices, DISTANCES[2])
     multipliers = call(turn_kernel, (ROWS, NB), (), (slices,), [pltpu.VMEM((NB, ROWS), jnp.float32)], name="turn")
     own, multipliers = lax.optimization_barrier((swap(blocks, "x"), multipliers))

time: 96.9 us -> 95.6 us (0.987)
  waiting for transfers between devices: 14.4 us -> 11.5 us
    all_to_all x1, waiting for transfers between devices: 1.99 us -> 0.01 us  [later_phases(): swap(pieces, 'y')]
    ppermute x3, starting transfers between devices: 14.3 us -> 15.5 us  [from_column(): return lax.ppermute(values, 'y', [(y, y ^ distance) for y in range(Y)])]
    pallas_call x10 -> x11, Pallas kernels: 16.2 us -> 16.9 us  [call(): pl.pallas_call(kernel, out_shape=shapes, in_specs=[SMEM] * len(smem) + [V...]
  transfers between devices with their start and end apart: 11 -> 11, of which waited for: 8 -> 7; matrix products, arithmetic and copies ran while one was open for 1% -> 1% of each run, Pallas kernels for 11% -> 14%
where the time goes in v10:
time: 95.6 us; the launch traced here: 94.9 us
  starting transfers between devices  55.6 us (58%)
  Pallas kernels  26.3 us (28%)
  waiting for transfers between devices  11.5 us (12%)
    pallas_call x11, Pallas kernels, call(): pl.pallas_call(kernel, out_shape=shapes, in_specs=[SMEM] * len(smem) + [V...  16.9 us
    ppermute x3, starting transfers between devices, from_column(): return lax.ppermute(values, 'y', [(y, y ^ distance) for y in range(Y)])  15.5 us
    ppermute x2, starting transfers between devices, other_core(): return lax.ppermute(values, 'c', [(0, 1), (1, 0)])  14 us
    pallas_call x2, Pallas kernels, make_plan(): pl.pallas_call(early_plan_kernel if early else late_plan_kernel, out_shap...  9.42 us
    ppermute x3, starting transfers between devices, first_phase(): lax.ppermute(blocks[s], 'x', [(x, (x + s) % X) for x in range(X)])  8.41 us
    all_to_all x1, starting transfers between devices, later_phases(): swap(blocks, 'x')  7.27 us
    all_to_all x1, starting transfers between devices, later_phases(): swap(pieces, 'y')  6.82 us
    ppermute x3, waiting for transfers between devices, from_column(): return lax.ppermute(values, 'y', [(y, y ^ distance) for y in range(Y)])  6.06 us
  transfers between devices with their start and end apart: 11, of which 7 were waited for; matrix products, arithmetic and copies ran while one was open for 1% of the time, Pallas kernels for 14%

profile of v10, /device:TPU:1, one launch (start us, length us, event | category | flops | bytes accessed | tf_op | source)
XLA Modules:
  0.0 94.9 jit_solution(15568697896921787855)
XLA Ops:
  0.0 3.3 %pack.3 = (f32[4,320,128]{2,1,0:T(8,128)S(1)}, f32[4,320,128]{2,1,0:T(8,128)S(1)}, s32[264]{0:T(512)S(1)}) custom-call(s32[256]{0:T(256)} %pivots.3, f32[32,512]{1,0:T(8,128)} %bitcast.2, f32[512,1024]{1,0:T(8,128)} %trailing.3), custom_call_target="tpu_custom_call" | custom-call | bytes 2097152 | tf_op jit(solution)/shard_map/pack/pallas_call | solution.py:410
  3.3 8.9 %collective-permute-start.8 = (f32[4,320,128]{2,1,0:T(8,128)S(1)}, f32[4,320,128]{2,1,0:T(8,128)S(1)}, u32[]{:S(2)}, u32[]{:S(2)}) collective-permute-start(f32[4,320,128]{2,1,0:T(8,128)S(1)} %get-tuple-element.63), channel_id=1, source_target_pairs={{0,8},{8,0},{1,9},{9,1},{2,10},{10,2},{3,11},{11,3},{4,12},{12,4},... | collective-permute-start | bytes 1966088 | tf_op jit(solution)/shard_map/ppermute | solution.py:463
  12.2 1.7 %collective-permute-done.8.got = f32[4,320,128]{2,1,0:T(8,128)S(1)} collective-permute-done((f32[4,320,128]{2,1,0:T(8,128)S(1)}, f32[4,320,128]{2,1,0:T(8,128)S(1)}, u32[]{:S(2)}, u32[]{:S(2)}) %collective-permute-start.8) | collective-permute-done | bytes 655392 | tf_op jit(solution)/shard_map/ppermute | solution.py:463
  14.0 1.9 %collective-permute-start.9 = (f32[320,128]{1,0:T(8,128)S(1)}, f32[320,128]{1,0:T(8,128)S(1)}, u32[]{:S(2)}, u32[]{:S(2)}) collective-permute-start(f32[320,128]{1,0:T(8,128)S(1)} %get-tuple-element.65), channel_id=1, source_target_pairs={{0,128},{128,256},{256,384},{384,0},{1,129},{129,257},{257,385},{3... | collective-permute-start | bytes 491528 | tf_op jit(solution)/shard_map/ppermute | solution.py:470
  15.9 1.9 %collective-permute-start.10 = (f32[320,128]{1,0:T(8,128)S(1)}, f32[320,128]{1,0:T(8,128)S(1)}, u32[]{:S(2)}, u32[]{:S(2)}) collective-permute-start(f32[320,128]{1,0:T(8,128)S(1)} %get-tuple-element.66), channel_id=1, source_target_pairs={{0,256},{128,384},{256,0},{384,128},{1,257},{129,385},{257,1},{385... | collective-permute-start | bytes 491528 | tf_op jit(solution)/shard_map/ppermute | solution.py:470
  17.8 4.6 %collective-permute-start.11 = (f32[320,128]{1,0:T(8,128)S(1)}, f32[320,128]{1,0:T(8,128)S(1)}, u32[]{:S(2)}, u32[]{:S(2)}) collective-permute-start(f32[320,128]{1,0:T(8,128)S(1)} %get-tuple-element.67), channel_id=1, source_target_pairs={{0,384},{128,0},{256,128},{384,256},{1,385},{129,1},{257,129},{385... | collective-permute-start | bytes 491528 | tf_op jit(solution)/shard_map/ppermute | solution.py:470
  22.4 4.6 %plan.6.table = s32[1024]{0:T(1024)S(1)} custom-call(s32[256]{0:T(256)S(1)} %copy-done.9), custom_call_target="tpu_custom_call" | custom-call | bytes 16777216 | tf_op jit(solution)/shard_map/plan/pallas_call | solution.py:118
  27.0 1.1 %collective-permute-done.11.refs_3_ = f32[320,128]{1,0:T(8,128)S(1)} collective-permute-done((f32[320,128]{1,0:T(8,128)S(1)}, f32[320,128]{1,0:T(8,128)S(1)}, u32[]{:S(2)}, u32[]{:S(2)}) %collective-permute-start.11) | collective-permute-done | bytes 163872 | tf_op jit(solution)/shard_map/ppermute | solution.py:470
  28.2 2.4 %spread.3 = (f32[8,120,128]{2,1,0:T(8,128)}, f32[32,512]{1,0:T(8,128)S(1)}) custom-call(s32[1024]{0:T(1024)S(1)} %plan.6.table, f32[320,128]{1,0:T(8,128)S(1)} %get-tuple-element.64.refs_0_, f32[320,128]{1,0:T(8,128)S(1)} %collective-permute-done.9.refs_1_, f32[320,128]{1,0:T(8,128)S(1)} %collective-permute-done.10.refs_2_, ...), custom_call_target="tpu_custom_call" | custom-call | bytes 2097152 | tf_op jit(solution)/shard_map/spread/pallas_call | solution.py:410
  30.5 3.6 %all-to-all-start.3 = ((f32[8,120,128]{2,1,0:T(8,128)}), f32[8,120,128]{2,1,0:T(8,128)S(1)}, u32[]{:S(2)}, u32[]{:S(2)}) async-start(f32[8,120,128]{2,1,0:T(8,128)} %get-tuple-element.70), calls=%async_computation.3 | async-start | bytes 983040 | tf_op jit(solution)/shard_map/all_to_all | solution.py:485
  34.1 7.4 %collective-permute-start.12 = (f32[32,512]{1,0:T(8,128)S(1)}, f32[32,512]{1,0:T(8,128)S(1)}, u32[]{:S(2)}, u32[]{:S(2)}) collective-permute-start(f32[32,512]{1,0:T(8,128)S(1)} %get-tuple-element.68.first), channel_id=1, source_target_pairs={{0,4},{1,5},{2,6},{3,7},{4,0},{5,1},{6,2},{7,3},{8,12},{9,13},{10,... | collective-permute-start | bytes 196616 | tf_op jit(solution)/shard_map/ppermute | solution.py:475
  41.6 1.7 %collective-permute-done.12.second = f32[32,512]{1,0:T(8,128)S(1)} collective-permute-done((f32[32,512]{1,0:T(8,128)S(1)}, f32[32,512]{1,0:T(8,128)S(1)}, u32[]{:S(2)}, u32[]{:S(2)}) %collective-permute-start.12) | collective-permute-done | bytes 65568 | tf_op jit(solution)/shard_map/ppermute | solution.py:475
  43.3 4.7 %collective-permute-start.13 = (f32[64,512]{1,0:T(8,128)S(1)}, f32[64,512]{1,0:T(8,128)S(1)}, u32[]{:S(2)}, u32[]{:S(2)}) collective-permute-start(f32[64,512]{1,0:T(8,128)S(1)} %get-tuple-element.72.first), channel_id=1, source_target_pairs={{0,2},{1,3},{2,0},{3,1},{4,6},{5,7},{6,4},{7,5},{8,10},{9,11},{10,... | collective-permute-start | bytes 393224 | tf_op jit(solution)/shard_map/ppermute | solution.py:475
  48.1 0.7 all-to-all-done.3.got
  49.3 6.8 %all-to-all-start.4 = ((f32[8,8,128]{2,1,0:T(8,128)}), f32[8,8,128]{2,1,0:T(8,128)S(1)}, u32[]{:S(2)}, u32[]{:S(2)}) async-start(f32[8,8,128]{2,1,0:T(8,128)} %pieces.3.after), calls=%async_computation.4 | async-start | bytes 65536 | tf_op jit(solution)/shard_map/all_to_all | solution.py:489
  56.2 4.8 %plan.7.table = s32[1024]{0:T(1024)S(1)} custom-call(s32[256]{0:T(256)S(1)} %copy-done.9, f32[8,8,128]{2,1,0:T(8,128)} %pieces.3.after), custom_call_target="tpu_custom_call" | custom-call | bytes 16777216 | tf_op jit(solution)/shard_map/plan/pallas_call | solution.py:118
  61.0 2.2 %collect.3.blocks = f32[4,376,128]{2,1,0:T(8,128)} custom-call(s32[1024]{0:T(1024)S(1)} %plan.7.table, f32[8,128]{1,0:T(8,128)S(1)} %get-tuple-element.73.token, f32[8,120,128]{2,1,0:T(8,128)S(1)} %all-to-all-done.3.got), custom_call_target="tpu_custom_call" | custom-call | bytes 2097152 | tf_op jit(solution)/shard_map/collect/pallas_call | solution.py:410
  63.2 0.7 append.3
  63.9 7.3 %all-to-all-start.5 = ((f32[4,376,128]{2,1,0:T(8,128)}), f32[4,376,128]{2,1,0:T(8,128)S(1)}, u32[]{:S(2)}, u32[]{:S(2)}) async-start(f32[4,376,128]{2,1,0:T(8,128)} %append.3), calls=%async_computation.5 | async-start | bytes 1540096 | tf_op jit(solution)/shard_map/all_to_all | solution.py:492
  71.2 3.3 %collective-permute-start.14 = (f32[128,512]{1,0:T(8,128)S(1)}, f32[128,512]{1,0:T(8,128)S(1)}, u32[]{:S(2)}, u32[]{:S(2)}) collective-permute-start(f32[128,512]{1,0:T(8,128)S(1)} %get-tuple-element.74.first), channel_id=1, source_target_pairs={{0,1},{1,0},{2,3},{3,2},{4,5},{5,4},{6,7},{7,6},{8,9},{9,8},{10,11... | collective-permute-start | bytes 786440 | tf_op jit(solution)/shard_map/ppermute | solution.py:475
  74.5 4.3 %collective-permute-done.14.second = f32[128,512]{1,0:T(8,128)S(1)} collective-permute-done((f32[128,512]{1,0:T(8,128)S(1)}, f32[128,512]{1,0:T(8,128)S(1)}, u32[]{:S(2)}, u32[]{:S(2)}) %collective-permute-start.14) | collective-permute-done | bytes 262176 | tf_op jit(solution)/shard_map/ppermute | solution.py:475
  79.7 1.3 %all-to-all-done.5.own = f32[4,376,128]{2,1,0:T(8,128)S(1)} async-done(((f32[4,376,128]{2,1,0:T(8,128)}), f32[4,376,128]{2,1,0:T(8,128)S(1)}, u32[]{:S(2)}, u32[]{:S(2)}) %all-to-all-start.5) | async-done | bytes 770080 | tf_op jit(solution)/shard_map/all_to_all | solution.py:492
  81.0 5.1 %collective-permute-start.15 = (f32[4,376,128]{2,1,0:T(8,128)S(1)}, f32[4,376,128]{2,1,0:T(8,128)S(1)}, u32[]{:S(2)}, u32[]{:S(2)}) collective-permute-start(f32[4,376,128]{2,1,0:T(8,128)S(1)} %all-to-all-done.5.own), channel_id=1, source_target_pairs={{0,8},{8,0},{1,9},{9,1},{2,10},{10,2},{3,11},{11,3},{4,12},{12,4},... | collective-permute-start | bytes 2310152 | tf_op jit(solution)/shard_map/ppermute | solution.py:463
  88.0 6.8 %finish.3 = f32[512,1024]{1,0:T(8,128)} custom-call(s32[264]{0:T(512)S(1)} %get-tuple-element.71.mine, f32[4,376,128]{2,1,0:T(8,128)S(1)} %all-to-all-done.5.own, f32[4,376,128]{2,1,0:T(8,128)S(1)} %collective-permute-done.15.other, f32[512,256]{1,0:T(8,128)S(1)} %turn.3.multipliers, f32[512,1024]{1,0:T(8,128)} %trailing.3), custom_call_target="tpu_custom_call" | custom-call | bytes 16777216 | tf_op jit(solution)/shard_map/finish/pallas_call | solution.py:410
  (17 shorter events, 2.8 us)
Async XLA Ops:
  0.0 22.4 %copy-start.9 = (s32[256]{0:T(256)S(1)}, s32[256]{0:T(256)}, u32[]{:S(2)}) copy-start(s32[256]{0:T(256)} %pivots.3) | copy-start | bytes 3076
  0.0 28.2 %copy-start.8 = (f32[512,32]{0,1:T(8,128)S(1)}, f32[512,32]{0,1:T(8,128)}, u32[]{:S(2)}) copy-start(f32[512,32]{0,1:T(8,128)} %param.5) | copy-start | bytes 196612
  3.3 10.6 %collective-permute-start.8 = (f32[4,320,128]{2,1,0:T(8,128)S(1)}, f32[4,320,128]{2,1,0:T(8,128)S(1)}, u32[]{:S(2)}, u32[]{:S(2)}) collective-permute-start(f32[4,320,128]{2,1,0:T(8,128)S(1)} %get-tuple-element.63), channel_id=1, source_target_pairs={{0,8},{8,0},{1,9},{9,1},{2,10},{10,2},{3,11},{11,3},{4,12},{12,4},... | collective-permute-start | bytes 1966088 | tf_op jit(solution)/shard_map/ppermute | solution.py:463
  14.0 13.0 %collective-permute-start.9 = (f32[320,128]{1,0:T(8,128)S(1)}, f32[320,128]{1,0:T(8,128)S(1)}, u32[]{:S(2)}, u32[]{:S(2)}) collective-permute-start(f32[320,128]{1,0:T(8,128)S(1)} %get-tuple-element.65), channel_id=1, source_target_pairs={{0,128},{128,256},{256,384},{384,0},{1,129},{129,257},{257,385},{3... | collective-permute-start | bytes 491528 | tf_op jit(solution)/shard_map/ppermute | solution.py:470
  15.9 11.1 %collective-permute-start.10 = (f32[320,128]{1,0:T(8,128)S(1)}, f32[320,128]{1,0:T(8,128)S(1)}, u32[]{:S(2)}, u32[]{:S(2)}) collective-permute-start(f32[320,128]{1,0:T(8,128)S(1)} %get-tuple-element.66), channel_id=1, source_target_pairs={{0,256},{128,384},{256,0},{384,128},{1,257},{129,385},{257,1},{385... | collective-permute-start | bytes 491528 | tf_op jit(solution)/shard_map/ppermute | solution.py:470
  17.8 10.3 %collective-permute-start.11 = (f32[320,128]{1,0:T(8,128)S(1)}, f32[320,128]{1,0:T(8,128)S(1)}, u32[]{:S(2)}, u32[]{:S(2)}) collective-permute-start(f32[320,128]{1,0:T(8,128)S(1)} %get-tuple-element.67), channel_id=1, source_target_pairs={{0,384},{128,0},{256,128},{384,256},{1,385},{129,1},{257,129},{385... | collective-permute-start | bytes 491528 | tf_op jit(solution)/shard_map/ppermute | solution.py:470
  30.5 18.2 %all-to-all-start.3 = ((f32[8,120,128]{2,1,0:T(8,128)}), f32[8,120,128]{2,1,0:T(8,128)S(1)}, u32[]{:S(2)}, u32[]{:S(2)}) async-start(f32[8,120,128]{2,1,0:T(8,128)} %get-tuple-element.70), calls=%async_computation.3 | async-start | bytes 983040 | tf_op jit(solution)/shard_map/all_to_all | solution.py:485
  34.1 9.2 %collective-permute-start.12 = (f32[32,512]{1,0:T(8,128)S(1)}, f32[32,512]{1,0:T(8,128)S(1)}, u32[]{:S(2)}, u32[]{:S(2)}) collective-permute-start(f32[32,512]{1,0:T(8,128)S(1)} %get-tuple-element.68.first), channel_id=1, source_target_pairs={{0,4},{1,5},{2,6},{3,7},{4,0},{5,1},{6,2},{7,3},{8,12},{9,13},{10,... | collective-permute-start | bytes 196616 | tf_op jit(solution)/shard_map/ppermute | solution.py:475
  43.3 12.8 %collective-permute-start.13 = (f32[64,512]{1,0:T(8,128)S(1)}, f32[64,512]{1,0:T(8,128)S(1)}, u32[]{:S(2)}, u32[]{:S(2)}) collective-permute-start(f32[64,512]{1,0:T(8,128)S(1)} %get-tuple-element.72.first), channel_id=1, source_target_pairs={{0,2},{1,3},{2,0},{3,1},{4,6},{5,7},{6,4},{7,5},{8,10},{9,11},{10,... | collective-permute-start | bytes 393224 | tf_op jit(solution)/shard_map/ppermute | solution.py:475
  49.3 13.9 %all-to-all-start.4 = ((f32[8,8,128]{2,1,0:T(8,128)}), f32[8,8,128]{2,1,0:T(8,128)S(1)}, u32[]{:S(2)}, u32[]{:S(2)}) async-start(f32[8,8,128]{2,1,0:T(8,128)} %pieces.3.after), calls=%async_computation.4 | async-start | bytes 65536 | tf_op jit(solution)/shard_map/all_to_all | solution.py:489
  63.9 17.1 %all-to-all-start.5 = ((f32[4,376,128]{2,1,0:T(8,128)}), f32[4,376,128]{2,1,0:T(8,128)S(1)}, u32[]{:S(2)}, u32[]{:S(2)}) async-start(f32[4,376,128]{2,1,0:T(8,128)} %append.3), calls=%async_computation.5 | async-start | bytes 1540096 | tf_op jit(solution)/shard_map/all_to_all | solution.py:492
  71.2 7.7 %collective-permute-start.14 = (f32[128,512]{1,0:T(8,128)S(1)}, f32[128,512]{1,0:T(8,128)S(1)}, u32[]{:S(2)}, u32[]{:S(2)}) collective-permute-start(f32[128,512]{1,0:T(8,128)S(1)} %get-tuple-element.74.first), channel_id=1, source_target_pairs={{0,1},{1,0},{2,3},{3,2},{4,5},{5,4},{6,7},{7,6},{8,9},{9,8},{10,11... | collective-permute-start | bytes 786440 | tf_op jit(solution)/shard_map/ppermute | solution.py:475
  81.0 7.0 %collective-permute-start.15 = (f32[4,376,128]{2,1,0:T(8,128)S(1)}, f32[4,376,128]{2,1,0:T(8,128)S(1)}, u32[]{:S(2)}, u32[]{:S(2)}) collective-permute-start(f32[4,376,128]{2,1,0:T(8,128)S(1)} %all-to-all-done.5.own), channel_id=1, source_target_pairs={{0,8},{8,0},{1,9},{9,1},{2,10},{10,2},{3,11},{11,3},{4,12},{12,4},... | collective-permute-start | bytes 2310152 | tf_op jit(solution)/shard_map/ppermute | solution.py:463

commit v11 on v10

--- a/solution.py
+++ b/solution.py
@@ -103,28 +103,17 @@
     table[MOST] = peak + found
 
 
-def early_plan_kernel(*refs):
-    @pl.when(lax.axis_index("z") == 0)
-    def _():
-        plan_kernel(*refs)
-
-
-def late_plan_kernel(pivots, after, table, content):
-    plan_kernel(pivots, table, content)
-
-
-def make_plan(pivots, after=None):
-    early = after is None
+def make_plan(pivots):
     return pl.pallas_call(
-        early_plan_kernel if early else late_plan_kernel,
+        plan_kernel,
         out_shape=jax.ShapeDtypeStruct((TABLE,), jnp.int32),
-        in_specs=[SMEM] if early else [SMEM, VMEM],
+        in_specs=[SMEM],
         out_specs=SMEM,
         scratch_shapes=[pltpu.SMEM((ORDER,), jnp.int32)],
         compiler_params=PARAMS,
         cost_estimate=pl.CostEstimate(flops=0, bytes_accessed=16 * 1024 * 1024, transcendentals=0),
         name="plan",
-    )(*([pivots] if early else [pivots, after]))
+    )(pivots)
 
 
 def invert_diagonal(panel_t, at):
@@ -165,18 +154,25 @@
         return rank, jnp.where(row >> ROW_BITS == device, found + 1, found)
 
     _, found = lax.fori_loop(0, NB, find, (jnp.int32(0), jnp.int32(0)), unroll=16)
-    invert_diagonal(panel_t, triangle)
     sides = ((keep, c), (send, 1 - c))
     for out, side in sides:
         for x in range(X):
             out[x, :cap, :] = jnp.zeros((cap, LANES), jnp.float32)
-            lanes = pl.ds(pl.multiple_of(side * LANES, LANES), LANES)
-            out[x, cap + NB :, :] = triangle[8 * x : 8 * x + 8, lanes]
+
+    @pl.when(first == 0)
+    def _():
+        invert_diagonal(panel_t, triangle)
+
     copy.wait()
-    for out, side in sides:
-        for x in range(X):
-            lanes = pl.ds(pl.multiple_of((x * C + side) * LANES, LANES), LANES)
-            out[x, cap : cap + NB, :] = rows[:NB, lanes]
+
+    @pl.when(first == 0)
+    def _():
+        for out, side in sides:
+            for x in range(X):
+                lanes = pl.ds(pl.multiple_of(side * LANES, LANES), LANES)
+                out[x, cap + NB :, :] = triangle[8 * x : 8 * x + 8, lanes]
+                lanes = pl.ds(pl.multiple_of((x * C + side) * LANES, LANES), LANES)
+                out[x, cap : cap + NB, :] = rows[:NB, lanes]
 
     def put(k):
         row, rank = local_entry(cap, mine[k])
@@ -468,7 +464,8 @@
     blocks = join(cap, keep, other_core(send))
     for s in range(1, X):
         blocks[s] = lax.ppermute(blocks[s], "x", [(x, (x + s) % X) for x in range(X)])
-    return *spread(cap, room, make_plan(pivots), blocks, panel_t), mine
+    plan = make_plan(pivots)
+    return *spread(cap, room, plan, blocks, panel_t), plan, mine
 
 
 def from_column(values, distance):
@@ -480,26 +477,25 @@
     return call(double_kernel, [shape, (8, LANES)], (), (slices, from_column(slices, distance)), name="double")
 
 
-def later_phases(cap, room, planes, slices, pivots):
+def later_phases(cap, room, planes, slices, plan):
     slices, token = doubled(slices, DISTANCES[0])
     planes = swap(planes, "z")
     pieces = call(pieces_kernel, (Y, 8, LANES), (), (token, planes), name="pieces")
-    plan = make_plan(pivots, pieces)
     slices, token = doubled(slices, DISTANCES[1])
     blocks = append(cap, swap(pieces, "y"), collect(cap, room, plan, token, planes))
     slices, _ = doubled(slices, DISTANCES[2])
     multipliers = call(turn_kernel, (ROWS, NB), (), (slices,), [pltpu.VMEM((NB, ROWS), jnp.float32)], name="turn")
     own, multipliers = lax.optimization_barrier((swap(blocks, "x"), multipliers))
-    return plan[MOST], own, other_core(own), multipliers
+    return own, other_core(own), multipliers
 
 
 def shards(panel, trailing, pivots):
     panel_t = panel.T
 
     def with_room(cap, room):
-        planes, slices, mine = first_phase(cap, room, panel_t, trailing, pivots)
-        most, *ready = later_phases(cap, room, planes, slices, pivots)
-        return most, finish(cap, mine, *ready, trailing)
+        planes, slices, plan, mine = first_phase(cap, room, panel_t, trailing, pivots)
+        ready = later_phases(cap, room, planes, slices, plan)
+        return plan[MOST], finish(cap, mine, *ready, trailing)
 
     def pending(carry):
         return carry[0]

time: 95.6 us -> 95.2 us (level)
  waiting for transfers between devices: 11.5 us -> 18 us
  Pallas kernels: 26.3 us -> 21.4 us
  starting transfers between devices: 55.6 us -> 53.7 us
    pallas_call x2 -> x1, Pallas kernels: 9.42 us -> 4.59 us  [make_plan(): pl.pallas_call(plan_kernel, out_shape=jax.ShapeDtypeStruct((TABLE,), jnp....]
    all_to_all x1, waiting for transfers between devices: 0.01 us -> 4.69 us  [later_phases(): swap(pieces, 'y')]
    all_to_all x1, starting transfers between devices: 7.27 us -> 5.28 us  [later_phases(): swap(blocks, 'x')]
    ppermute x3, starting transfers between devices: 15.5 us -> 14.3 us  [from_column(): return lax.ppermute(values, 'y', [(y, y ^ distance) for y in range(Y)])]
    all_to_all x1, starting transfers between devices: 3.62 us -> 4.6 us  [later_phases(): planes = swap(planes, 'z')]
  transfers between devices with their start and end apart: 11 -> 11, of which waited for: 7 -> 8; matrix products, arithmetic and copies ran while one was open for 1% -> 1% of each run, Pallas kernels for 14% -> 9%
where the time goes in v11:
time: 95.2 us; the launch traced here: 94.5 us
  starting transfers between devices  53.7 us (56%)
  Pallas kernels  21.4 us (22%)
  waiting for transfers between devices  18 us (19%)
    pallas_call x11, Pallas kernels, call(): pl.pallas_call(kernel, out_shape=shapes, in_specs=[SMEM] * len(smem) + [V...  16.9 us
    ppermute x3, starting transfers between devices, from_column(): return lax.ppermute(values, 'y', [(y, y ^ distance) for y in range(Y)])  14.3 us
    ppermute x2, starting transfers between devices, other_core(): return lax.ppermute(values, 'c', [(0, 1), (1, 0)])  14.3 us
    ppermute x3, starting transfers between devices, first_phase(): lax.ppermute(blocks[s], 'x', [(x, (x + s) % X) for x in range(X)])  8.41 us
    ppermute x3, waiting for transfers between devices, from_column(): return lax.ppermute(values, 'y', [(y, y ^ distance) for y in range(Y)])  7 us
    all_to_all x1, starting transfers between devices, later_phases(): swap(pieces, 'y')  6.82 us
    all_to_all x1, starting transfers between devices, later_phases(): swap(blocks, 'x')  5.28 us
    all_to_all x1, waiting for transfers between devices, later_phases(): swap(pieces, 'y')  4.69 us
  transfers between devices with their start and end apart: 11, of which 8 were waited for; matrix products, arithmetic and copies ran while one was open for 1% of the time, Pallas kernels for 9%

profile of v11, /device:TPU:1, one launch (start us, length us, event | category | flops | bytes accessed | tf_op | source)
XLA Modules:
  0.0 94.5 jit_solution(15757202482856131162)
XLA Ops:
  0.0 3.2 %pack.3 = (f32[4,320,128]{2,1,0:T(8,128)S(1)}, f32[4,320,128]{2,1,0:T(8,128)S(1)}, s32[264]{0:T(512)S(1)}) custom-call(s32[256]{0:T(256)} %pivots.3, f32[32,512]{1,0:T(8,128)} %bitcast.2, f32[512,1024]{1,0:T(8,128)} %trailing.3), custom_call_target="tpu_custom_call" | custom-call | bytes 2097152 | tf_op jit(solution)/shard_map/pack/pallas_call | solution.py:406
  3.2 8.9 %collective-permute-start.8 = (f32[4,320,128]{2,1,0:T(8,128)S(1)}, f32[4,320,128]{2,1,0:T(8,128)S(1)}, u32[]{:S(2)}, u32[]{:S(2)}) collective-permute-start(f32[4,320,128]{2,1,0:T(8,128)S(1)} %get-tuple-element.64), channel_id=1, source_target_pairs={{0,8},{8,0},{1,9},{9,1},{2,10},{10,2},{3,11},{11,3},{4,12},{12,4},... | collective-permute-start | bytes 1966088 | tf_op jit(solution)/shard_map/ppermute | solution.py:459
  12.2 1.7 %collective-permute-done.8.got = f32[4,320,128]{2,1,0:T(8,128)S(1)} collective-permute-done((f32[4,320,128]{2,1,0:T(8,128)S(1)}, f32[4,320,128]{2,1,0:T(8,128)S(1)}, u32[]{:S(2)}, u32[]{:S(2)}) %collective-permute-start.8) | collective-permute-done | bytes 655392 | tf_op jit(solution)/shard_map/ppermute | solution.py:459
  14.0 1.9 %collective-permute-start.9 = (f32[320,128]{1,0:T(8,128)S(1)}, f32[320,128]{1,0:T(8,128)S(1)}, u32[]{:S(2)}, u32[]{:S(2)}) collective-permute-start(f32[320,128]{1,0:T(8,128)S(1)} %get-tuple-element.66), channel_id=1, source_target_pairs={{0,128},{128,256},{256,384},{384,0},{1,129},{129,257},{257,385},{3... | collective-permute-start | bytes 491528 | tf_op jit(solution)/shard_map/ppermute | solution.py:466
  15.9 1.9 %collective-permute-start.10 = (f32[320,128]{1,0:T(8,128)S(1)}, f32[320,128]{1,0:T(8,128)S(1)}, u32[]{:S(2)}, u32[]{:S(2)}) collective-permute-start(f32[320,128]{1,0:T(8,128)S(1)} %get-tuple-element.67), channel_id=1, source_target_pairs={{0,256},{128,384},{256,0},{384,128},{1,257},{129,385},{257,1},{385... | collective-permute-start | bytes 491528 | tf_op jit(solution)/shard_map/ppermute | solution.py:466
  17.8 4.6 %collective-permute-start.11 = (f32[320,128]{1,0:T(8,128)S(1)}, f32[320,128]{1,0:T(8,128)S(1)}, u32[]{:S(2)}, u32[]{:S(2)}) collective-permute-start(f32[320,128]{1,0:T(8,128)S(1)} %get-tuple-element.68), channel_id=1, source_target_pairs={{0,384},{128,0},{256,128},{384,256},{1,385},{129,1},{257,129},{385... | collective-permute-start | bytes 491528 | tf_op jit(solution)/shard_map/ppermute | solution.py:466
  22.4 4.6 %plan.3.table = s32[1024]{0:T(1024)S(1)} custom-call(s32[256]{0:T(256)S(1)} %copy-done.9), custom_call_target="tpu_custom_call" | custom-call | bytes 16777216 | tf_op jit(solution)/shard_map/plan/pallas_call | solution.py:107
  27.0 1.1 %collective-permute-done.11.refs_3_ = f32[320,128]{1,0:T(8,128)S(1)} collective-permute-done((f32[320,128]{1,0:T(8,128)S(1)}, f32[320,128]{1,0:T(8,128)S(1)}, u32[]{:S(2)}, u32[]{:S(2)}) %collective-permute-start.11) | collective-permute-done | bytes 163872 | tf_op jit(solution)/shard_map/ppermute | solution.py:466
  28.2 2.3 %spread.3 = (f32[8,120,128]{2,1,0:T(8,128)}, f32[32,512]{1,0:T(8,128)S(1)}) custom-call(s32[1024]{0:T(1024)S(1)} %plan.3.table, f32[320,128]{1,0:T(8,128)S(1)} %get-tuple-element.65.refs_0_, f32[320,128]{1,0:T(8,128)S(1)} %collective-permute-done.9.refs_1_, f32[320,128]{1,0:T(8,128)S(1)} %collective-permute-done.10.refs_2_, ...), custom_call_target="tpu_custom_call" | custom-call | bytes 2097152 | tf_op jit(solution)/shard_map/spread/pallas_call | solution.py:406
  30.5 4.6 %all-to-all-start.3 = ((f32[8,120,128]{2,1,0:T(8,128)}), f32[8,120,128]{2,1,0:T(8,128)S(1)}, u32[]{:S(2)}, u32[]{:S(2)}) async-start(f32[8,120,128]{2,1,0:T(8,128)} %get-tuple-element.71), calls=%async_computation.3 | async-start | bytes 983040 | tf_op jit(solution)/shard_map/all_to_all | solution.py:482
  35.1 7.4 %collective-permute-start.12 = (f32[32,512]{1,0:T(8,128)S(1)}, f32[32,512]{1,0:T(8,128)S(1)}, u32[]{:S(2)}, u32[]{:S(2)}) collective-permute-start(f32[32,512]{1,0:T(8,128)S(1)} %get-tuple-element.69.first), channel_id=1, source_target_pairs={{0,4},{1,5},{2,6},{3,7},{4,0},{5,1},{6,2},{7,3},{8,12},{9,13},{10,... | collective-permute-start | bytes 196616 | tf_op jit(solution)/shard_map/ppermute | solution.py:472
  42.5 1.7 %collective-permute-done.12.second = f32[32,512]{1,0:T(8,128)S(1)} collective-permute-done((f32[32,512]{1,0:T(8,128)S(1)}, f32[32,512]{1,0:T(8,128)S(1)}, u32[]{:S(2)}, u32[]{:S(2)}) %collective-permute-start.12) | collective-permute-done | bytes 65568 | tf_op jit(solution)/shard_map/ppermute | solution.py:472
  44.3 4.7 %collective-permute-start.13 = (f32[64,512]{1,0:T(8,128)S(1)}, f32[64,512]{1,0:T(8,128)S(1)}, u32[]{:S(2)}, u32[]{:S(2)}) collective-permute-start(f32[64,512]{1,0:T(8,128)S(1)} %get-tuple-element.72.first), channel_id=1, source_target_pairs={{0,2},{1,3},{2,0},{3,1},{4,6},{5,7},{6,4},{7,5},{8,10},{9,11},{10,... | collective-permute-start | bytes 393224 | tf_op jit(solution)/shard_map/ppermute | solution.py:472
  49.0 1.5 %all-to-all-done.3.got = f32[8,120,128]{2,1,0:T(8,128)S(1)} async-done(((f32[8,120,128]{2,1,0:T(8,128)}), f32[8,120,128]{2,1,0:T(8,128)S(1)}, u32[]{:S(2)}, u32[]{:S(2)}) %all-to-all-start.3) | async-done | bytes 491552 | tf_op jit(solution)/shard_map/all_to_all | solution.py:482
  51.1 6.8 %all-to-all-start.4 = ((f32[8,8,128]{2,1,0:T(8,128)}), f32[8,8,128]{2,1,0:T(8,128)S(1)}, u32[]{:S(2)}, u32[]{:S(2)}) async-start(f32[8,8,128]{2,1,0:T(8,128)} %pieces.3), calls=%async_computation.4 | async-start | bytes 65536 | tf_op jit(solution)/shard_map/all_to_all | solution.py:485
  58.0 2.1 %collect.3.blocks = f32[4,376,128]{2,1,0:T(8,128)} custom-call(s32[1024]{0:T(1024)S(1)} %plan.3.table, f32[8,128]{1,0:T(8,128)S(1)} %get-tuple-element.73.token, f32[8,120,128]{2,1,0:T(8,128)S(1)} %all-to-all-done.3.got), custom_call_target="tpu_custom_call" | custom-call | bytes 2097152 | tf_op jit(solution)/shard_map/collect/pallas_call | solution.py:406
  60.1 4.7 %all-to-all-done.4.pieces = f32[8,8,128]{2,1,0:T(8,128)S(1)} async-done(((f32[8,8,128]{2,1,0:T(8,128)}), f32[8,8,128]{2,1,0:T(8,128)S(1)}, u32[]{:S(2)}, u32[]{:S(2)}) %all-to-all-start.4) | async-done | bytes 32800 | tf_op jit(solution)/shard_map/all_to_all | solution.py:485
  64.8 0.7 append.3
  65.5 5.3 %all-to-all-start.5 = ((f32[4,376,128]{2,1,0:T(8,128)}), f32[4,376,128]{2,1,0:T(8,128)S(1)}, u32[]{:S(2)}, u32[]{:S(2)}) async-start(f32[4,376,128]{2,1,0:T(8,128)} %append.3), calls=%async_computation.5 | async-start | bytes 1540096 | tf_op jit(solution)/shard_map/all_to_all | solution.py:488
  70.8 2.2 %collective-permute-start.14 = (f32[128,512]{1,0:T(8,128)S(1)}, f32[128,512]{1,0:T(8,128)S(1)}, u32[]{:S(2)}, u32[]{:S(2)}) collective-permute-start(f32[128,512]{1,0:T(8,128)S(1)} %get-tuple-element.74.first), channel_id=1, source_target_pairs={{0,1},{1,0},{2,3},{3,2},{4,5},{5,4},{6,7},{7,6},{8,9},{9,8},{10,11... | collective-permute-start | bytes 786440 | tf_op jit(solution)/shard_map/ppermute | solution.py:472
  73.0 5.3 %collective-permute-done.14.second = f32[128,512]{1,0:T(8,128)S(1)} collective-permute-done((f32[128,512]{1,0:T(8,128)S(1)}, f32[128,512]{1,0:T(8,128)S(1)}, u32[]{:S(2)}, u32[]{:S(2)}) %collective-permute-start.14) | collective-permute-done | bytes 262176 | tf_op jit(solution)/shard_map/ppermute | solution.py:472
  79.1 1.3 %all-to-all-done.5.own = f32[4,376,128]{2,1,0:T(8,128)S(1)} async-done(((f32[4,376,128]{2,1,0:T(8,128)}), f32[4,376,128]{2,1,0:T(8,128)S(1)}, u32[]{:S(2)}, u32[]{:S(2)}) %all-to-all-start.5) | async-done | bytes 770080 | tf_op jit(solution)/shard_map/all_to_all | solution.py:488
  80.4 5.3 %collective-permute-start.15 = (f32[4,376,128]{2,1,0:T(8,128)S(1)}, f32[4,376,128]{2,1,0:T(8,128)S(1)}, u32[]{:S(2)}, u32[]{:S(2)}) collective-permute-start(f32[4,376,128]{2,1,0:T(8,128)S(1)} %all-to-all-done.5.own), channel_id=1, source_target_pairs={{0,8},{8,0},{1,9},{9,1},{2,10},{10,2},{3,11},{11,3},{4,12},{12,4},... | collective-permute-start | bytes 2310152 | tf_op jit(solution)/shard_map/ppermute | solution.py:459
  87.6 6.9 %finish.3 = f32[512,1024]{1,0:T(8,128)} custom-call(s32[264]{0:T(512)S(1)} %get-tuple-element.62.mine, f32[4,376,128]{2,1,0:T(8,128)S(1)} %all-to-all-done.5.own, f32[4,376,128]{2,1,0:T(8,128)S(1)} %collective-permute-done.15.other, f32[512,256]{1,0:T(8,128)S(1)} %turn.3.multipliers, f32[512,1024]{1,0:T(8,128)} %trailing.3), custom_call_target="tpu_custom_call" | custom-call | bytes 16777216 | tf_op jit(solution)/shard_map/finish/pallas_call | solution.py:406
  (16 shorter events, 2.8 us)
Async XLA Ops:
  0.0 22.4 %copy-start.9 = (s32[256]{0:T(256)S(1)}, s32[256]{0:T(256)}, u32[]{:S(2)}) copy-start(s32[256]{0:T(256)} %pivots.3) | copy-start | bytes 3076
  0.0 28.2 %copy-start.8 = (f32[512,32]{0,1:T(8,128)S(1)}, f32[512,32]{0,1:T(8,128)}, u32[]{:S(2)}) copy-start(f32[512,32]{0,1:T(8,128)} %param.5) | copy-start | bytes 196612
  3.2 10.6 %collective-permute-start.8 = (f32[4,320,128]{2,1,0:T(8,128)S(1)}, f32[4,320,128]{2,1,0:T(8,128)S(1)}, u32[]{:S(2)}, u32[]{:S(2)}) collective-permute-start(f32[4,320,128]{2,1,0:T(8,128)S(1)} %get-tuple-element.64), channel_id=1, source_target_pairs={{0,8},{8,0},{1,9},{9,1},{2,10},{10,2},{3,11},{11,3},{4,12},{12,4},... | collective-permute-start | bytes 1966088 | tf_op jit(solution)/shard_map/ppermute | solution.py:459
  14.0 13.0 %collective-permute-start.9 = (f32[320,128]{1,0:T(8,128)S(1)}, f32[320,128]{1,0:T(8,128)S(1)}, u32[]{:S(2)}, u32[]{:S(2)}) collective-permute-start(f32[320,128]{1,0:T(8,128)S(1)} %get-tuple-element.66), channel_id=1, source_target_pairs={{0,128},{128,256},{256,384},{384,0},{1,129},{129,257},{257,385},{3... | collective-permute-start | bytes 491528 | tf_op jit(solution)/shard_map/ppermute | solution.py:466
  15.9 11.1 %collective-permute-start.10 = (f32[320,128]{1,0:T(8,128)S(1)}, f32[320,128]{1,0:T(8,128)S(1)}, u32[]{:S(2)}, u32[]{:S(2)}) collective-permute-start(f32[320,128]{1,0:T(8,128)S(1)} %get-tuple-element.67), channel_id=1, source_target_pairs={{0,256},{128,384},{256,0},{384,128},{1,257},{129,385},{257,1},{385... | collective-permute-start | bytes 491528 | tf_op jit(solution)/shard_map/ppermute | solution.py:466
  17.8 10.3 %collective-permute-start.11 = (f32[320,128]{1,0:T(8,128)S(1)}, f32[320,128]{1,0:T(8,128)S(1)}, u32[]{:S(2)}, u32[]{:S(2)}) collective-permute-start(f32[320,128]{1,0:T(8,128)S(1)} %get-tuple-element.68), channel_id=1, source_target_pairs={{0,384},{128,0},{256,128},{384,256},{1,385},{129,1},{257,129},{385... | collective-permute-start | bytes 491528 | tf_op jit(solution)/shard_map/ppermute | solution.py:466
  30.5 20.0 %all-to-all-start.3 = ((f32[8,120,128]{2,1,0:T(8,128)}), f32[8,120,128]{2,1,0:T(8,128)S(1)}, u32[]{:S(2)}, u32[]{:S(2)}) async-start(f32[8,120,128]{2,1,0:T(8,128)} %get-tuple-element.71), calls=%async_computation.3 | async-start | bytes 983040 | tf_op jit(solution)/shard_map/all_to_all | solution.py:482
  35.1 9.2 %collective-permute-start.12 = (f32[32,512]{1,0:T(8,128)S(1)}, f32[32,512]{1,0:T(8,128)S(1)}, u32[]{:S(2)}, u32[]{:S(2)}) collective-permute-start(f32[32,512]{1,0:T(8,128)S(1)} %get-tuple-element.69.first), channel_id=1, source_target_pairs={{0,4},{1,5},{2,6},{3,7},{4,0},{5,1},{6,2},{7,3},{8,12},{9,13},{10,... | collective-permute-start | bytes 196616 | tf_op jit(solution)/shard_map/ppermute | solution.py:472
  44.3 13.7 %collective-permute-start.13 = (f32[64,512]{1,0:T(8,128)S(1)}, f32[64,512]{1,0:T(8,128)S(1)}, u32[]{:S(2)}, u32[]{:S(2)}) collective-permute-start(f32[64,512]{1,0:T(8,128)S(1)} %get-tuple-element.72.first), channel_id=1, source_target_pairs={{0,2},{1,3},{2,0},{3,1},{4,6},{5,7},{6,4},{7,5},{8,10},{9,11},{10,... | collective-permute-start | bytes 393224 | tf_op jit(solution)/shard_map/ppermute | solution.py:472
  51.1 13.7 %all-to-all-start.4 = ((f32[8,8,128]{2,1,0:T(8,128)}), f32[8,8,128]{2,1,0:T(8,128)S(1)}, u32[]{:S(2)}, u32[]{:S(2)}) async-start(f32[8,8,128]{2,1,0:T(8,128)} %pieces.3), calls=%async_computation.4 | async-start | bytes 65536 | tf_op jit(solution)/shard_map/all_to_all | solution.py:485
  65.5 14.9 %all-to-all-start.5 = ((f32[4,376,128]{2,1,0:T(8,128)}), f32[4,376,128]{2,1,0:T(8,128)S(1)}, u32[]{:S(2)}, u32[]{:S(2)}) async-start(f32[4,376,128]{2,1,0:T(8,128)} %append.3), calls=%async_computation.5 | async-start | bytes 1540096 | tf_op jit(solution)/shard_map/all_to_all | solution.py:488
  70.8 7.5 %collective-permute-start.14 = (f32[128,512]{1,0:T(8,128)S(1)}, f32[128,512]{1,0:T(8,128)S(1)}, u32[]{:S(2)}, u32[]{:S(2)}) collective-permute-start(f32[128,512]{1,0:T(8,128)S(1)} %get-tuple-element.74.first), channel_id=1, source_target_pairs={{0,1},{1,0},{2,3},{3,2},{4,5},{5,4},{6,7},{7,6},{8,9},{9,8},{10,11... | collective-permute-start | bytes 786440 | tf_op jit(solution)/shard_map/ppermute | solution.py:472
  80.4 7.2 %collective-permute-start.15 = (f32[4,376,128]{2,1,0:T(8,128)S(1)}, f32[4,376,128]{2,1,0:T(8,128)S(1)}, u32[]{:S(2)}, u32[]{:S(2)}) collective-permute-start(f32[4,376,128]{2,1,0:T(8,128)S(1)} %all-to-all-done.5.own), channel_id=1, source_target_pairs={{0,8},{8,0},{1,9},{9,1},{2,10},{10,2},{3,11},{11,3},{4,12},{12,4},... | collective-permute-start | bytes 2310152 | tf_op jit(solution)/shard_map/ppermute | solution.py:459

commit v12 on v11

--- a/solution.py
+++ b/solution.py
@@ -103,17 +103,35 @@
     table[MOST] = peak + found
 
 
-def make_plan(pivots):
+def early_plan_kernel(pivots, table, content):
+    @pl.when(lax.axis_index("z") == 0)
+    def _():
+        plan_kernel(pivots, table, content)
+
+
+def late_plan_kernel(pivots, early, after, table, content):
+    z = lax.axis_index("z")
+
+    @pl.when(z == 0)
+    def _():
+        table[MOST] = early[MOST]
+
+    @pl.when(z != 0)
+    def _():
+        plan_kernel(pivots, table, content)
+
+
+def make_plan(kernel, *args):
     return pl.pallas_call(
-        plan_kernel,
+        kernel,
         out_shape=jax.ShapeDtypeStruct((TABLE,), jnp.int32),
-        in_specs=[SMEM],
+        in_specs=[SMEM, SMEM, VMEM][: len(args)],
         out_specs=SMEM,
         scratch_shapes=[pltpu.SMEM((ORDER,), jnp.int32)],
         compiler_params=PARAMS,
         cost_estimate=pl.CostEstimate(flops=0, bytes_accessed=16 * 1024 * 1024, transcendentals=0),
         name="plan",
-    )(pivots)
+    )(*args)
 
 
 def invert_diagonal(panel_t, at):
@@ -242,26 +260,30 @@
         out[y] = got[0, got.shape[1] - 8 :, :]
 
 
-def collect_kernel(cap, room, table, token, got, out, block, sem):
+def collect_kernel(cap, room, early, late, token, got, out, block, sem):
     z = lax.axis_index("z")
 
-    def take(k):
-        base = pl.multiple_of(k * BATCH, BATCH)
-        rows = []
-        for i in range(BATCH):
-            where = table[PLACE + base + i]
-            rank = jnp.minimum(where & (NB - 1), cap - 1)
-            rows.append(got[where >> BITS, pl.ds(rank, 1), :])
-        for i in range(BATCH):
-            block[pl.ds(base + i, 1), :] = rows[i]
-
-    loop(NB // BATCH, take)
-
-    def top(k):
-        at = cap + jnp.minimum(table[COUNT + z] + k, room - 1)
-        block[pl.ds(table[TOPS + k] >> BITS, 1), :] = got[0, pl.ds(at, 1), :]
-
-    loop(table[COUNT + Z], top)
+    def assemble(table):
+        def take(k):
+            base = pl.multiple_of(k * BATCH, BATCH)
+            rows = []
+            for i in range(BATCH):
+                where = table[PLACE + base + i]
+                rank = jnp.minimum(where & (NB - 1), cap - 1)
+                rows.append(got[where >> BITS, pl.ds(rank, 1), :])
+            for i in range(BATCH):
+                block[pl.ds(base + i, 1), :] = rows[i]
+
+        loop(NB // BATCH, take)
+
+        def top(k):
+            at = cap + jnp.minimum(table[COUNT + z] + k, room - 1)
+            block[pl.ds(table[TOPS + k] >> BITS, 1), :] = got[0, pl.ds(at, 1), :]
+
+        loop(table[COUNT + Z], top)
+
+    pl.when(z == 0)(lambda: assemble(early))
+    pl.when(z != 0)(lambda: assemble(late))
     block[NB:, :] = got[0, cap : 2 * cap, :]
     copies = [pltpu.make_async_copy(block, out.at[x, pl.ds(0, NB + cap), :], sem.at[x]) for x in range(X)]
     for copy in copies:
@@ -432,10 +454,10 @@
                 (plan,), (*blocks, panel_t), [pltpu.VMEM((NB + 8, LANES), jnp.float32)], name="spread")
 
 
-def collect(cap, room, plan, token, planes):
+def collect(cap, room, plans, token, planes):
     scratch = [pltpu.VMEM((NB + cap, LANES), jnp.float32), pltpu.SemaphoreType.DMA((X,))]
     return call(functools.partial(collect_kernel, cap, room), (X, NB + cap + 8 * Y, LANES),
-                (plan,), (token, planes), scratch, name="collect", out=HBM)
+                plans, (token, planes), scratch, name="collect", out=HBM)
 
 
 def append(cap, pieces, blocks):
@@ -464,7 +486,7 @@
     blocks = join(cap, keep, other_core(send))
     for s in range(1, X):
         blocks[s] = lax.ppermute(blocks[s], "x", [(x, (x + s) % X) for x in range(X)])
-    plan = make_plan(pivots)
+    plan = make_plan(early_plan_kernel, pivots)
     return *spread(cap, room, plan, blocks, panel_t), plan, mine
 
 
@@ -477,16 +499,17 @@
     return call(double_kernel, [shape, (8, LANES)], (), (slices, from_column(slices, distance)), name="double")
 
 
-def later_phases(cap, room, planes, slices, plan):
+def later_phases(cap, room, planes, slices, pivots, early):
     slices, token = doubled(slices, DISTANCES[0])
     planes = swap(planes, "z")
     pieces = call(pieces_kernel, (Y, 8, LANES), (), (token, planes), name="pieces")
+    late = make_plan(late_plan_kernel, pivots, early, pieces)
     slices, token = doubled(slices, DISTANCES[1])
-    blocks = append(cap, swap(pieces, "y"), collect(cap, room, plan, token, planes))
+    blocks = append(cap, swap(pieces, "y"), collect(cap, room, (early, late), token, planes))
     slices, _ = doubled(slices, DISTANCES[2])
     multipliers = call(turn_kernel, (ROWS, NB), (), (slices,), [pltpu.VMEM((NB, ROWS), jnp.float32)], name="turn")
     own, multipliers = lax.optimization_barrier((swap(blocks, "x"), multipliers))
-    return own, other_core(own), multipliers
+    return late[MOST], own, other_core(own), multipliers
 
 
 def shards(panel, trailing, pivots):
@@ -494,8 +517,8 @@
 
     def with_room(cap, room):
         planes, slices, plan, mine = first_phase(cap, room, panel_t, trailing, pivots)
-        ready = later_phases(cap, room, planes, slices, plan)
-        return plan[MOST], finish(cap, mine, *ready, trailing)
+        most, *ready = later_phases(cap, room, planes, slices, pivots, plan)
+        return most, finish(cap, mine, *ready, trailing)
 
     def pending(carry):
         return carry[0]

time: 95.2 us -> 95.2 us (level)
  waiting for transfers between devices: 18 us -> 15.6 us
  Pallas kernels: 21.4 us -> 23 us
    all_to_all x1, starting transfers between devices: 5.28 us -> 7.21 us  [later_phases(): swap(blocks, 'x')]
    all_to_all x1, waiting for transfers between devices: 4.69 us -> 3.14 us  [later_phases(): swap(pieces, 'y')]
    pallas_call x1 -> x2, Pallas kernels: 4.59 us -> 6.05 us  [make_plan(): pl.pallas_call(kernel, out_shape=jax.ShapeDtypeStruct((TABLE,), jnp.int32...]
    all_to_all x1, starting transfers between devices: 4.6 us -> 3.59 us  [later_phases(): planes = swap(planes, 'z')]
  transfers between devices with their start and end apart: 11 -> 11, of which waited for: 8 -> 8; matrix products, arithmetic and copies ran while one was open for 1% -> 1% of each run, Pallas kernels for 9% -> 10%
where the time goes in v12:
time: 95.2 us; the launch traced here: 94.6 us
  starting transfers between devices  54.6 us (57%)
  Pallas kernels  23 us (24%)
  waiting for transfers between devices  15.6 us (16%)
    pallas_call x11, Pallas kernels, call(): pl.pallas_call(kernel, out_shape=shapes, in_specs=[SMEM] * len(smem) + [V...  17 us
    ppermute x3, starting transfers between devices, from_column(): return lax.ppermute(values, 'y', [(y, y ^ distance) for y in range(Y)])  14.3 us
    ppermute x2, starting transfers between devices, other_core(): return lax.ppermute(values, 'c', [(0, 1), (1, 0)])  14.2 us
    ppermute x3, starting transfers between devices, first_phase(): lax.ppermute(blocks[s], 'x', [(x, (x + s) % X) for x in range(X)])  8.41 us
    all_to_all x1, starting transfers between devices, later_phases(): swap(blocks, 'x')  7.21 us
    ppermute x3, waiting for transfers between devices, from_column(): return lax.ppermute(values, 'y', [(y, y ^ distance) for y in range(Y)])  7 us
    all_to_all x1, starting transfers between devices, later_phases(): swap(pieces, 'y')  6.82 us
    pallas_call x2, Pallas kernels, make_plan(): pl.pallas_call(kernel, out_shape=jax.ShapeDtypeStruct((TABLE,), jnp.int32...  6.05 us
  transfers between devices with their start and end apart: 11, of which 8 were waited for; matrix products, arithmetic and copies ran while one was open for 1% of the time, Pallas kernels for 10%

profile of v12, /device:TPU:1, one launch (start us, length us, event | category | flops | bytes accessed | tf_op | source)
XLA Modules:
  0.0 94.6 jit_solution(8009472603337699805)
XLA Ops:
  0.0 3.3 %pack.3 = (f32[4,320,128]{2,1,0:T(8,128)S(1)}, f32[4,320,128]{2,1,0:T(8,128)S(1)}, s32[264]{0:T(512)S(1)}) custom-call(s32[256]{0:T(256)} %pivots.5, f32[32,512]{1,0:T(8,128)} %bitcast.2, f32[512,1024]{1,0:T(8,128)} %trailing.3), custom_call_target="tpu_custom_call" | custom-call | bytes 2097152 | tf_op jit(solution)/shard_map/pack/pallas_call | solution.py:428
  3.3 8.9 %collective-permute-start.8 = (f32[4,320,128]{2,1,0:T(8,128)S(1)}, f32[4,320,128]{2,1,0:T(8,128)S(1)}, u32[]{:S(2)}, u32[]{:S(2)}) collective-permute-start(f32[4,320,128]{2,1,0:T(8,128)S(1)} %get-tuple-element.63), channel_id=1, source_target_pairs={{0,8},{8,0},{1,9},{9,1},{2,10},{10,2},{3,11},{11,3},{4,12},{12,4},... | collective-permute-start | bytes 1966088 | tf_op jit(solution)/shard_map/ppermute | solution.py:481
  12.1 1.7 %collective-permute-done.8.got = f32[4,320,128]{2,1,0:T(8,128)S(1)} collective-permute-done((f32[4,320,128]{2,1,0:T(8,128)S(1)}, f32[4,320,128]{2,1,0:T(8,128)S(1)}, u32[]{:S(2)}, u32[]{:S(2)}) %collective-permute-start.8) | collective-permute-done | bytes 655392 | tf_op jit(solution)/shard_map/ppermute | solution.py:481
  13.9 1.9 %collective-permute-start.9 = (f32[320,128]{1,0:T(8,128)S(1)}, f32[320,128]{1,0:T(8,128)S(1)}, u32[]{:S(2)}, u32[]{:S(2)}) collective-permute-start(f32[320,128]{1,0:T(8,128)S(1)} %get-tuple-element.65), channel_id=1, source_target_pairs={{0,128},{128,256},{256,384},{384,0},{1,129},{129,257},{257,385},{3... | collective-permute-start | bytes 491528 | tf_op jit(solution)/shard_map/ppermute | solution.py:488
  15.8 1.9 %collective-permute-start.10 = (f32[320,128]{1,0:T(8,128)S(1)}, f32[320,128]{1,0:T(8,128)S(1)}, u32[]{:S(2)}, u32[]{:S(2)}) collective-permute-start(f32[320,128]{1,0:T(8,128)S(1)} %get-tuple-element.66), channel_id=1, source_target_pairs={{0,256},{128,384},{256,0},{384,128},{1,257},{129,385},{257,1},{385... | collective-permute-start | bytes 491528 | tf_op jit(solution)/shard_map/ppermute | solution.py:488
  17.8 4.6 %collective-permute-start.11 = (f32[320,128]{1,0:T(8,128)S(1)}, f32[320,128]{1,0:T(8,128)S(1)}, u32[]{:S(2)}, u32[]{:S(2)}) collective-permute-start(f32[320,128]{1,0:T(8,128)S(1)} %get-tuple-element.67), channel_id=1, source_target_pairs={{0,384},{128,0},{256,128},{384,256},{1,385},{129,1},{257,129},{385... | collective-permute-start | bytes 491528 | tf_op jit(solution)/shard_map/ppermute | solution.py:488
  22.4 4.6 %plan.6.table.early = s32[1024]{0:T(1024)S(1)} custom-call(s32[256]{0:T(256)S(1)} %copy-done.9), custom_call_target="tpu_custom_call" | custom-call | bytes 16777216 | tf_op jit(solution)/shard_map/plan/pallas_call | solution.py:125
  27.0 1.1 %collective-permute-done.11.refs_3_ = f32[320,128]{1,0:T(8,128)S(1)} collective-permute-done((f32[320,128]{1,0:T(8,128)S(1)}, f32[320,128]{1,0:T(8,128)S(1)}, u32[]{:S(2)}, u32[]{:S(2)}) %collective-permute-start.11) | collective-permute-done | bytes 163872 | tf_op jit(solution)/shard_map/ppermute | solution.py:488
  28.1 2.3 %spread.3 = (f32[8,120,128]{2,1,0:T(8,128)}, f32[32,512]{1,0:T(8,128)S(1)}) custom-call(s32[1024]{0:T(1024)S(1)} %plan.6.table.early, f32[320,128]{1,0:T(8,128)S(1)} %get-tuple-element.64.refs_0_, f32[320,128]{1,0:T(8,128)S(1)} %collective-permute-done.9.refs_1_, f32[320,128]{1,0:T(8,128)S(1)} %collective-permute-done.10.refs_2_, ...), custom_call_target="tpu_custom_call" | custom-call | bytes 2097152 | tf_op jit(solution)/shard_map/spread/pallas_call | solution.py:428
  30.4 3.6 %all-to-all-start.3 = ((f32[8,120,128]{2,1,0:T(8,128)}), f32[8,120,128]{2,1,0:T(8,128)S(1)}, u32[]{:S(2)}, u32[]{:S(2)}) async-start(f32[8,120,128]{2,1,0:T(8,128)} %get-tuple-element.70), calls=%async_computation.3 | async-start | bytes 983040 | tf_op jit(solution)/shard_map/all_to_all | solution.py:504
  34.0 7.4 %collective-permute-start.12 = (f32[32,512]{1,0:T(8,128)S(1)}, f32[32,512]{1,0:T(8,128)S(1)}, u32[]{:S(2)}, u32[]{:S(2)}) collective-permute-start(f32[32,512]{1,0:T(8,128)S(1)} %get-tuple-element.68.first), channel_id=1, source_target_pairs={{0,4},{1,5},{2,6},{3,7},{4,0},{5,1},{6,2},{7,3},{8,12},{9,13},{10,... | collective-permute-start | bytes 196616 | tf_op jit(solution)/shard_map/ppermute | solution.py:494
  41.5 1.7 %collective-permute-done.12.second = f32[32,512]{1,0:T(8,128)S(1)} collective-permute-done((f32[32,512]{1,0:T(8,128)S(1)}, f32[32,512]{1,0:T(8,128)S(1)}, u32[]{:S(2)}, u32[]{:S(2)}) %collective-permute-start.12) | collective-permute-done | bytes 65568 | tf_op jit(solution)/shard_map/ppermute | solution.py:494
  43.2 4.7 %collective-permute-start.13 = (f32[64,512]{1,0:T(8,128)S(1)}, f32[64,512]{1,0:T(8,128)S(1)}, u32[]{:S(2)}, u32[]{:S(2)}) collective-permute-start(f32[64,512]{1,0:T(8,128)S(1)} %get-tuple-element.72.first), channel_id=1, source_target_pairs={{0,2},{1,3},{2,0},{3,1},{4,6},{5,7},{6,4},{7,5},{8,10},{9,11},{10,... | collective-permute-start | bytes 393224 | tf_op jit(solution)/shard_map/ppermute | solution.py:494
  49.2 6.8 %all-to-all-start.4 = ((f32[8,8,128]{2,1,0:T(8,128)}), f32[8,8,128]{2,1,0:T(8,128)S(1)}, u32[]{:S(2)}, u32[]{:S(2)}) async-start(f32[8,8,128]{2,1,0:T(8,128)} %pieces.3.after), calls=%async_computation.4 | async-start | bytes 65536 | tf_op jit(solution)/shard_map/all_to_all | solution.py:508
  56.1 1.5 %plan.7.late = s32[1024]{0:T(1024)S(1)} custom-call(s32[256]{0:T(256)S(1)} %copy-done.9, s32[1024]{0:T(1024)S(1)} %plan.6.table.early, f32[8,8,128]{2,1,0:T(8,128)} %pieces.3.after), custom_call_target="tpu_custom_call" | custom-call | bytes 16777216 | tf_op jit(solution)/shard_map/plan/pallas_call | solution.py:125
  57.5 2.2 %collect.3.blocks = f32[4,376,128]{2,1,0:T(8,128)} custom-call(s32[1024]{0:T(1024)S(1)} %plan.6.table.early, s32[1024]{0:T(1024)S(1)} %plan.7.late, f32[8,128]{1,0:T(8,128)S(1)} %get-tuple-element.73.token, f32[8,120,128]{2,1,0:T(8,128)S(1)} %all-to-all-done.3.got), custom_call_target="tpu_custom_call" | custom-call | bytes 2097152 | tf_op jit(solution)/shard_map/collect/pallas_call | solution.py:428
  59.8 3.1 %all-to-all-done.4.pieces = f32[8,8,128]{2,1,0:T(8,128)S(1)} async-done(((f32[8,8,128]{2,1,0:T(8,128)}), f32[8,8,128]{2,1,0:T(8,128)S(1)}, u32[]{:S(2)}, u32[]{:S(2)}) %all-to-all-start.4) | async-done | bytes 32800 | tf_op jit(solution)/shard_map/all_to_all | solution.py:508
  62.9 0.7 append.3
  63.6 7.2 %all-to-all-start.5 = ((f32[4,376,128]{2,1,0:T(8,128)}), f32[4,376,128]{2,1,0:T(8,128)S(1)}, u32[]{:S(2)}, u32[]{:S(2)}) async-start(f32[4,376,128]{2,1,0:T(8,128)} %append.3), calls=%async_computation.5 | async-start | bytes 1540096 | tf_op jit(solution)/shard_map/all_to_all | solution.py:511
  70.8 2.2 %collective-permute-start.14 = (f32[128,512]{1,0:T(8,128)S(1)}, f32[128,512]{1,0:T(8,128)S(1)}, u32[]{:S(2)}, u32[]{:S(2)}) collective-permute-start(f32[128,512]{1,0:T(8,128)S(1)} %get-tuple-element.74.first), channel_id=1, source_target_pairs={{0,1},{1,0},{2,3},{3,2},{4,5},{5,4},{6,7},{7,6},{8,9},{9,8},{10,11... | collective-permute-start | bytes 786440 | tf_op jit(solution)/shard_map/ppermute | solution.py:494
  73.0 5.3 %collective-permute-done.14.second = f32[128,512]{1,0:T(8,128)S(1)} collective-permute-done((f32[128,512]{1,0:T(8,128)S(1)}, f32[128,512]{1,0:T(8,128)S(1)}, u32[]{:S(2)}, u32[]{:S(2)}) %collective-permute-start.14) | collective-permute-done | bytes 262176 | tf_op jit(solution)/shard_map/ppermute | solution.py:494
  79.1 1.3 %all-to-all-done.5.own = f32[4,376,128]{2,1,0:T(8,128)S(1)} async-done(((f32[4,376,128]{2,1,0:T(8,128)}), f32[4,376,128]{2,1,0:T(8,128)S(1)}, u32[]{:S(2)}, u32[]{:S(2)}) %all-to-all-start.5) | async-done | bytes 770080 | tf_op jit(solution)/shard_map/all_to_all | solution.py:511
  80.5 5.3 %collective-permute-start.15 = (f32[4,376,128]{2,1,0:T(8,128)S(1)}, f32[4,376,128]{2,1,0:T(8,128)S(1)}, u32[]{:S(2)}, u32[]{:S(2)}) collective-permute-start(f32[4,376,128]{2,1,0:T(8,128)S(1)} %all-to-all-done.5.own), channel_id=1, source_target_pairs={{0,8},{8,0},{1,9},{9,1},{2,10},{10,2},{3,11},{11,3},{4,12},{12,4},... | collective-permute-start | bytes 2310152 | tf_op jit(solution)/shard_map/ppermute | solution.py:481
  87.6 6.9 %finish.3 = f32[512,1024]{1,0:T(8,128)} custom-call(s32[264]{0:T(512)S(1)} %get-tuple-element.71.mine, f32[4,376,128]{2,1,0:T(8,128)S(1)} %all-to-all-done.5.own, f32[4,376,128]{2,1,0:T(8,128)S(1)} %collective-permute-done.15.other, f32[512,256]{1,0:T(8,128)S(1)} %turn.3.multipliers, f32[512,1024]{1,0:T(8,128)} %trailing.3), custom_call_target="tpu_custom_call" | custom-call | bytes 16777216 | tf_op jit(solution)/shard_map/finish/pallas_call | solution.py:428
  (17 shorter events, 3.5 us)
Async XLA Ops:
  0.0 22.4 %copy-start.9 = (s32[256]{0:T(256)S(1)}, s32[256]{0:T(256)}, u32[]{:S(2)}) copy-start(s32[256]{0:T(256)} %pivots.5) | copy-start | bytes 3076
  0.0 28.1 %copy-start.8 = (f32[512,32]{0,1:T(8,128)S(1)}, f32[512,32]{0,1:T(8,128)}, u32[]{:S(2)}) copy-start(f32[512,32]{0,1:T(8,128)} %param.5) | copy-start | bytes 196612
  3.3 10.6 %collective-permute-start.8 = (f32[4,320,128]{2,1,0:T(8,128)S(1)}, f32[4,320,128]{2,1,0:T(8,128)S(1)}, u32[]{:S(2)}, u32[]{:S(2)}) collective-permute-start(f32[4,320,128]{2,1,0:T(8,128)S(1)} %get-tuple-element.63), channel_id=1, source_target_pairs={{0,8},{8,0},{1,9},{9,1},{2,10},{10,2},{3,11},{11,3},{4,12},{12,4},... | collective-permute-start | bytes 1966088 | tf_op jit(solution)/shard_map/ppermute | solution.py:481
  13.9 13.0 %collective-permute-start.9 = (f32[320,128]{1,0:T(8,128)S(1)}, f32[320,128]{1,0:T(8,128)S(1)}, u32[]{:S(2)}, u32[]{:S(2)}) collective-permute-start(f32[320,128]{1,0:T(8,128)S(1)} %get-tuple-element.65), channel_id=1, source_target_pairs={{0,128},{128,256},{256,384},{384,0},{1,129},{129,257},{257,385},{3... | collective-permute-start | bytes 491528 | tf_op jit(solution)/shard_map/ppermute | solution.py:488
  15.8 11.1 %collective-permute-start.10 = (f32[320,128]{1,0:T(8,128)S(1)}, f32[320,128]{1,0:T(8,128)S(1)}, u32[]{:S(2)}, u32[]{:S(2)}) collective-permute-start(f32[320,128]{1,0:T(8,128)S(1)} %get-tuple-element.66), channel_id=1, source_target_pairs={{0,256},{128,384},{256,0},{384,128},{1,257},{129,385},{257,1},{385... | collective-permute-start | bytes 491528 | tf_op jit(solution)/shard_map/ppermute | solution.py:488
  17.8 10.3 %collective-permute-start.11 = (f32[320,128]{1,0:T(8,128)S(1)}, f32[320,128]{1,0:T(8,128)S(1)}, u32[]{:S(2)}, u32[]{:S(2)}) collective-permute-start(f32[320,128]{1,0:T(8,128)S(1)} %get-tuple-element.67), channel_id=1, source_target_pairs={{0,384},{128,0},{256,128},{384,256},{1,385},{129,1},{257,129},{385... | collective-permute-start | bytes 491528 | tf_op jit(solution)/shard_map/ppermute | solution.py:488
  30.4 18.2 %all-to-all-start.3 = ((f32[8,120,128]{2,1,0:T(8,128)}), f32[8,120,128]{2,1,0:T(8,128)S(1)}, u32[]{:S(2)}, u32[]{:S(2)}) async-start(f32[8,120,128]{2,1,0:T(8,128)} %get-tuple-element.70), calls=%async_computation.3 | async-start | bytes 983040 | tf_op jit(solution)/shard_map/all_to_all | solution.py:504
  34.0 9.2 %collective-permute-start.12 = (f32[32,512]{1,0:T(8,128)S(1)}, f32[32,512]{1,0:T(8,128)S(1)}, u32[]{:S(2)}, u32[]{:S(2)}) collective-permute-start(f32[32,512]{1,0:T(8,128)S(1)} %get-tuple-element.68.first), channel_id=1, source_target_pairs={{0,4},{1,5},{2,6},{3,7},{4,0},{5,1},{6,2},{7,3},{8,12},{9,13},{10,... | collective-permute-start | bytes 196616 | tf_op jit(solution)/shard_map/ppermute | solution.py:494
  43.2 12.8 %collective-permute-start.13 = (f32[64,512]{1,0:T(8,128)S(1)}, f32[64,512]{1,0:T(8,128)S(1)}, u32[]{:S(2)}, u32[]{:S(2)}) collective-permute-start(f32[64,512]{1,0:T(8,128)S(1)} %get-tuple-element.72.first), channel_id=1, source_target_pairs={{0,2},{1,3},{2,0},{3,1},{4,6},{5,7},{6,4},{7,5},{8,10},{9,11},{10,... | collective-permute-start | bytes 393224 | tf_op jit(solution)/shard_map/ppermute | solution.py:494
  49.2 13.7 %all-to-all-start.4 = ((f32[8,8,128]{2,1,0:T(8,128)}), f32[8,8,128]{2,1,0:T(8,128)S(1)}, u32[]{:S(2)}, u32[]{:S(2)}) async-start(f32[8,8,128]{2,1,0:T(8,128)} %pieces.3.after), calls=%async_computation.4 | async-start | bytes 65536 | tf_op jit(solution)/shard_map/all_to_all | solution.py:508
  63.6 16.9 %all-to-all-start.5 = ((f32[4,376,128]{2,1,0:T(8,128)}), f32[4,376,128]{2,1,0:T(8,128)S(1)}, u32[]{:S(2)}, u32[]{:S(2)}) async-start(f32[4,376,128]{2,1,0:T(8,128)} %append.3), calls=%async_computation.5 | async-start | bytes 1540096 | tf_op jit(solution)/shard_map/all_to_all | solution.py:511
  70.8 7.5 %collective-permute-start.14 = (f32[128,512]{1,0:T(8,128)S(1)}, f32[128,512]{1,0:T(8,128)S(1)}, u32[]{:S(2)}, u32[]{:S(2)}) collective-permute-start(f32[128,512]{1,0:T(8,128)S(1)} %get-tuple-element.74.first), channel_id=1, source_target_pairs={{0,1},{1,0},{2,3},{3,2},{4,5},{5,4},{6,7},{7,6},{8,9},{9,8},{10,11... | collective-permute-start | bytes 786440 | tf_op jit(solution)/shard_map/ppermute | solution.py:494
  80.5 7.2 %collective-permute-start.15 = (f32[4,376,128]{2,1,0:T(8,128)S(1)}, f32[4,376,128]{2,1,0:T(8,128)S(1)}, u32[]{:S(2)}, u32[]{:S(2)}) collective-permute-start(f32[4,376,128]{2,1,0:T(8,128)S(1)} %all-to-all-done.5.own), channel_id=1, source_target_pairs={{0,8},{8,0},{1,9},{9,1},{2,10},{10,2},{3,11},{11,3},{4,12},{12,4},... | collective-permute-start | bytes 2310152 | tf_op jit(solution)/shard_map/ppermute | solution.py:481

commit v13 on v12

--- a/solution.py
+++ b/solution.py
@@ -68,7 +68,7 @@
     return ((lax.axis_index("x") * Z + lax.axis_index("z")) * C + lax.axis_index("c")) * ROWS
 
 
-def plan_kernel(pivots, table, content):
+def plan_kernel(pivots, table, content, fillers):
     def start(i):
         content[i] = i
         content[pivots[i]] = pivots[i]
@@ -95,7 +95,8 @@
         row = pivots[i]
         table[FILLER + i] = jnp.where(row < NB, 0, content[row])
 
-    loop(NB, fill, 8)
+    if fillers:
+        loop(NB, fill, 8)
     table[COUNT + Z] = found
     peak = table[COUNT]
     for z in range(1, Z):
@@ -106,7 +107,7 @@
 def early_plan_kernel(pivots, table, content):
     @pl.when(lax.axis_index("z") == 0)
     def _():
-        plan_kernel(pivots, table, content)
+        plan_kernel(pivots, table, content, True)
 
 
 def late_plan_kernel(pivots, early, after, table, content):
@@ -118,7 +119,7 @@
 
     @pl.when(z != 0)
     def _():
-        plan_kernel(pivots, table, content)
+        plan_kernel(pivots, table, content, False)
 
 
 def make_plan(kernel, *args):
@@ -401,9 +402,11 @@
         for lane, ref in sides:
             block[1 - slot, :, pl.ds(lane, LANES)] = ref[x + 1, :NB, :]
         solved = dot(inverse[...], block[1 - slot])
-        product = dot(multipliers[...], block[slot])
+        half = ROWS // 2
+        product = [dot(multipliers[k * half : (k + 1) * half], block[slot]) for k in range(2)]
         block[1 - slot] = solved
-        current[:, lanes] = current[:, lanes] - product
+        for k in range(2):
+            current[k * half : (k + 1) * half, lanes] -= product[k]
 
         @pl.when(first == 0)
         def _():

time: 95.2 us -> 95.1 us (level)
  no operation moved by 1% of the time
where the time goes in v13:
time: 95.1 us; the launch traced here: 94.4 us
  starting transfers between devices  54.5 us (57%)
  Pallas kernels  22.9 us (24%)
  waiting for transfers between devices  15.6 us (16%)
    pallas_call x11, Pallas kernels, call(): pl.pallas_call(kernel, out_shape=shapes, in_specs=[SMEM] * len(smem) + [V...  16.8 us
    ppermute x3, starting transfers between devices, from_column(): return lax.ppermute(values, 'y', [(y, y ^ distance) for y in range(Y)])  14.3 us
    ppermute x2, starting transfers between devices, other_core(): return lax.ppermute(values, 'c', [(0, 1), (1, 0)])  14.2 us
    ppermute x3, starting transfers between devices, first_phase(): lax.ppermute(blocks[s], 'x', [(x, (x + s) % X) for x in range(X)])  8.41 us
    all_to_all x1, starting transfers between devices, later_phases(): swap(blocks, 'x')  7.09 us
    ppermute x3, waiting for transfers between devices, from_column(): return lax.ppermute(values, 'y', [(y, y ^ distance) for y in range(Y)])  7 us
    all_to_all x1, starting transfers between devices, later_phases(): swap(pieces, 'y')  6.82 us
    pallas_call x2, Pallas kernels, make_plan(): pl.pallas_call(kernel, out_shape=jax.ShapeDtypeStruct((TABLE,), jnp.int32...  6.05 us
  transfers between devices with their start and end apart: 11, of which 8 were waited for; matrix products, arithmetic and copies ran while one was open for 1% of the time, Pallas kernels for 10%

profile of v13, /device:TPU:1, one launch (start us, length us, event | category | flops | bytes accessed | tf_op | source)
XLA Modules:
  0.0 94.4 jit_solution(5882101890240507440)
XLA Ops:
  0.0 3.3 %pack.3 = (f32[4,320,128]{2,1,0:T(8,128)S(1)}, f32[4,320,128]{2,1,0:T(8,128)S(1)}, s32[264]{0:T(512)S(1)}) custom-call(s32[256]{0:T(256)} %pivots.5, f32[32,512]{1,0:T(8,128)} %bitcast.2, f32[512,1024]{1,0:T(8,128)} %trailing.3), custom_call_target="tpu_custom_call" | custom-call | bytes 2097152 | tf_op jit(solution)/shard_map/pack/pallas_call | solution.py:431
  3.3 8.9 %collective-permute-start.8 = (f32[4,320,128]{2,1,0:T(8,128)S(1)}, f32[4,320,128]{2,1,0:T(8,128)S(1)}, u32[]{:S(2)}, u32[]{:S(2)}) collective-permute-start(f32[4,320,128]{2,1,0:T(8,128)S(1)} %get-tuple-element.63), channel_id=1, source_target_pairs={{0,8},{8,0},{1,9},{9,1},{2,10},{10,2},{3,11},{11,3},{4,12},{12,4},... | collective-permute-start | bytes 1966088 | tf_op jit(solution)/shard_map/ppermute | solution.py:484
  12.1 1.7 %collective-permute-done.8.got = f32[4,320,128]{2,1,0:T(8,128)S(1)} collective-permute-done((f32[4,320,128]{2,1,0:T(8,128)S(1)}, f32[4,320,128]{2,1,0:T(8,128)S(1)}, u32[]{:S(2)}, u32[]{:S(2)}) %collective-permute-start.8) | collective-permute-done | bytes 655392 | tf_op jit(solution)/shard_map/ppermute | solution.py:484
  13.9 1.9 %collective-permute-start.9 = (f32[320,128]{1,0:T(8,128)S(1)}, f32[320,128]{1,0:T(8,128)S(1)}, u32[]{:S(2)}, u32[]{:S(2)}) collective-permute-start(f32[320,128]{1,0:T(8,128)S(1)} %get-tuple-element.65), channel_id=1, source_target_pairs={{0,128},{128,256},{256,384},{384,0},{1,129},{129,257},{257,385},{3... | collective-permute-start | bytes 491528 | tf_op jit(solution)/shard_map/ppermute | solution.py:491
  15.8 1.9 %collective-permute-start.10 = (f32[320,128]{1,0:T(8,128)S(1)}, f32[320,128]{1,0:T(8,128)S(1)}, u32[]{:S(2)}, u32[]{:S(2)}) collective-permute-start(f32[320,128]{1,0:T(8,128)S(1)} %get-tuple-element.66), channel_id=1, source_target_pairs={{0,256},{128,384},{256,0},{384,128},{1,257},{129,385},{257,1},{385... | collective-permute-start | bytes 491528 | tf_op jit(solution)/shard_map/ppermute | solution.py:491
  17.8 4.6 %collective-permute-start.11 = (f32[320,128]{1,0:T(8,128)S(1)}, f32[320,128]{1,0:T(8,128)S(1)}, u32[]{:S(2)}, u32[]{:S(2)}) collective-permute-start(f32[320,128]{1,0:T(8,128)S(1)} %get-tuple-element.67), channel_id=1, source_target_pairs={{0,384},{128,0},{256,128},{384,256},{1,385},{129,1},{257,129},{385... | collective-permute-start | bytes 491528 | tf_op jit(solution)/shard_map/ppermute | solution.py:491
  22.4 4.6 %plan.6.table.early = s32[1024]{0:T(1024)S(1)} custom-call(s32[256]{0:T(256)S(1)} %copy-done.9), custom_call_target="tpu_custom_call" | custom-call | bytes 16777216 | tf_op jit(solution)/shard_map/plan/pallas_call | solution.py:126
  27.0 1.1 %collective-permute-done.11.refs_3_ = f32[320,128]{1,0:T(8,128)S(1)} collective-permute-done((f32[320,128]{1,0:T(8,128)S(1)}, f32[320,128]{1,0:T(8,128)S(1)}, u32[]{:S(2)}, u32[]{:S(2)}) %collective-permute-start.11) | collective-permute-done | bytes 163872 | tf_op jit(solution)/shard_map/ppermute | solution.py:491
  28.1 2.3 %spread.3 = (f32[8,120,128]{2,1,0:T(8,128)}, f32[32,512]{1,0:T(8,128)S(1)}) custom-call(s32[1024]{0:T(1024)S(1)} %plan.6.table.early, f32[320,128]{1,0:T(8,128)S(1)} %get-tuple-element.64.refs_0_, f32[320,128]{1,0:T(8,128)S(1)} %collective-permute-done.9.refs_1_, f32[320,128]{1,0:T(8,128)S(1)} %collective-permute-done.10.refs_2_, ...), custom_call_target="tpu_custom_call" | custom-call | bytes 2097152 | tf_op jit(solution)/shard_map/spread/pallas_call | solution.py:431
  30.4 3.6 %all-to-all-start.3 = ((f32[8,120,128]{2,1,0:T(8,128)}), f32[8,120,128]{2,1,0:T(8,128)S(1)}, u32[]{:S(2)}, u32[]{:S(2)}) async-start(f32[8,120,128]{2,1,0:T(8,128)} %get-tuple-element.70), calls=%async_computation.3 | async-start | bytes 983040 | tf_op jit(solution)/shard_map/all_to_all | solution.py:507
  34.1 7.4 %collective-permute-start.12 = (f32[32,512]{1,0:T(8,128)S(1)}, f32[32,512]{1,0:T(8,128)S(1)}, u32[]{:S(2)}, u32[]{:S(2)}) collective-permute-start(f32[32,512]{1,0:T(8,128)S(1)} %get-tuple-element.68.first), channel_id=1, source_target_pairs={{0,4},{1,5},{2,6},{3,7},{4,0},{5,1},{6,2},{7,3},{8,12},{9,13},{10,... | collective-permute-start | bytes 196616 | tf_op jit(solution)/shard_map/ppermute | solution.py:497
  41.5 1.7 %collective-permute-done.12.second = f32[32,512]{1,0:T(8,128)S(1)} collective-permute-done((f32[32,512]{1,0:T(8,128)S(1)}, f32[32,512]{1,0:T(8,128)S(1)}, u32[]{:S(2)}, u32[]{:S(2)}) %collective-permute-start.12) | collective-permute-done | bytes 65568 | tf_op jit(solution)/shard_map/ppermute | solution.py:497
  43.2 4.7 %collective-permute-start.13 = (f32[64,512]{1,0:T(8,128)S(1)}, f32[64,512]{1,0:T(8,128)S(1)}, u32[]{:S(2)}, u32[]{:S(2)}) collective-permute-start(f32[64,512]{1,0:T(8,128)S(1)} %get-tuple-element.72.first), channel_id=1, source_target_pairs={{0,2},{1,3},{2,0},{3,1},{4,6},{5,7},{6,4},{7,5},{8,10},{9,11},{10,... | collective-permute-start | bytes 393224 | tf_op jit(solution)/shard_map/ppermute | solution.py:497
  49.3 6.8 %all-to-all-start.4 = ((f32[8,8,128]{2,1,0:T(8,128)}), f32[8,8,128]{2,1,0:T(8,128)S(1)}, u32[]{:S(2)}, u32[]{:S(2)}) async-start(f32[8,8,128]{2,1,0:T(8,128)} %pieces.3.after), calls=%async_computation.4 | async-start | bytes 65536 | tf_op jit(solution)/shard_map/all_to_all | solution.py:511
  56.1 1.5 %plan.7.late = s32[1024]{0:T(1024)S(1)} custom-call(s32[256]{0:T(256)S(1)} %copy-done.9, s32[1024]{0:T(1024)S(1)} %plan.6.table.early, f32[8,8,128]{2,1,0:T(8,128)} %pieces.3.after), custom_call_target="tpu_custom_call" | custom-call | bytes 16777216 | tf_op jit(solution)/shard_map/plan/pallas_call | solution.py:126
  57.6 2.2 %collect.3.blocks = f32[4,376,128]{2,1,0:T(8,128)} custom-call(s32[1024]{0:T(1024)S(1)} %plan.6.table.early, s32[1024]{0:T(1024)S(1)} %plan.7.late, f32[8,128]{1,0:T(8,128)S(1)} %get-tuple-element.73.token, f32[8,120,128]{2,1,0:T(8,128)S(1)} %all-to-all-done.3.got), custom_call_target="tpu_custom_call" | custom-call | bytes 2097152 | tf_op jit(solution)/shard_map/collect/pallas_call | solution.py:431
  59.8 3.1 %all-to-all-done.4.pieces = f32[8,8,128]{2,1,0:T(8,128)S(1)} async-done(((f32[8,8,128]{2,1,0:T(8,128)}), f32[8,8,128]{2,1,0:T(8,128)S(1)}, u32[]{:S(2)}, u32[]{:S(2)}) %all-to-all-start.4) | async-done | bytes 32800 | tf_op jit(solution)/shard_map/all_to_all | solution.py:511
  63.0 0.7 append.3
  63.6 7.1 %all-to-all-start.5 = ((f32[4,376,128]{2,1,0:T(8,128)}), f32[4,376,128]{2,1,0:T(8,128)S(1)}, u32[]{:S(2)}, u32[]{:S(2)}) async-start(f32[4,376,128]{2,1,0:T(8,128)} %append.3), calls=%async_computation.5 | async-start | bytes 1540096 | tf_op jit(solution)/shard_map/all_to_all | solution.py:514
  70.7 2.2 %collective-permute-start.14 = (f32[128,512]{1,0:T(8,128)S(1)}, f32[128,512]{1,0:T(8,128)S(1)}, u32[]{:S(2)}, u32[]{:S(2)}) collective-permute-start(f32[128,512]{1,0:T(8,128)S(1)} %get-tuple-element.74.first), channel_id=1, source_target_pairs={{0,1},{1,0},{2,3},{3,2},{4,5},{5,4},{6,7},{7,6},{8,9},{9,8},{10,11... | collective-permute-start | bytes 786440 | tf_op jit(solution)/shard_map/ppermute | solution.py:497
  72.9 5.3 %collective-permute-done.14.second = f32[128,512]{1,0:T(8,128)S(1)} collective-permute-done((f32[128,512]{1,0:T(8,128)S(1)}, f32[128,512]{1,0:T(8,128)S(1)}, u32[]{:S(2)}, u32[]{:S(2)}) %collective-permute-start.14) | collective-permute-done | bytes 262176 | tf_op jit(solution)/shard_map/ppermute | solution.py:497
  79.1 1.3 %all-to-all-done.5.own = f32[4,376,128]{2,1,0:T(8,128)S(1)} async-done(((f32[4,376,128]{2,1,0:T(8,128)}), f32[4,376,128]{2,1,0:T(8,128)S(1)}, u32[]{:S(2)}, u32[]{:S(2)}) %all-to-all-start.5) | async-done | bytes 770080 | tf_op jit(solution)/shard_map/all_to_all | solution.py:514
  80.4 5.3 %collective-permute-start.15 = (f32[4,376,128]{2,1,0:T(8,128)S(1)}, f32[4,376,128]{2,1,0:T(8,128)S(1)}, u32[]{:S(2)}, u32[]{:S(2)}) collective-permute-start(f32[4,376,128]{2,1,0:T(8,128)S(1)} %all-to-all-done.5.own), channel_id=1, source_target_pairs={{0,8},{8,0},{1,9},{9,1},{2,10},{10,2},{3,11},{11,3},{4,12},{12,4},... | collective-permute-start | bytes 2310152 | tf_op jit(solution)/shard_map/ppermute | solution.py:484
  87.6 6.8 %finish.3 = f32[512,1024]{1,0:T(8,128)} custom-call(s32[264]{0:T(512)S(1)} %get-tuple-element.71.mine, f32[4,376,128]{2,1,0:T(8,128)S(1)} %all-to-all-done.5.own, f32[4,376,128]{2,1,0:T(8,128)S(1)} %collective-permute-done.15.other, f32[512,256]{1,0:T(8,128)S(1)} %turn.3.multipliers, f32[512,1024]{1,0:T(8,128)} %trailing.3), custom_call_target="tpu_custom_call" | custom-call | bytes 16777216 | tf_op jit(solution)/shard_map/finish/pallas_call | solution.py:431
  (17 shorter events, 3.5 us)
Async XLA Ops:
  0.0 22.4 %copy-start.9 = (s32[256]{0:T(256)S(1)}, s32[256]{0:T(256)}, u32[]{:S(2)}) copy-start(s32[256]{0:T(256)} %pivots.5) | copy-start | bytes 3076
  0.0 28.1 %copy-start.8 = (f32[512,32]{0,1:T(8,128)S(1)}, f32[512,32]{0,1:T(8,128)}, u32[]{:S(2)}) copy-start(f32[512,32]{0,1:T(8,128)} %param.5) | copy-start | bytes 196612
  3.3 10.6 %collective-permute-start.8 = (f32[4,320,128]{2,1,0:T(8,128)S(1)}, f32[4,320,128]{2,1,0:T(8,128)S(1)}, u32[]{:S(2)}, u32[]{:S(2)}) collective-permute-start(f32[4,320,128]{2,1,0:T(8,128)S(1)} %get-tuple-element.63), channel_id=1, source_target_pairs={{0,8},{8,0},{1,9},{9,1},{2,10},{10,2},{3,11},{11,3},{4,12},{12,4},... | collective-permute-start | bytes 1966088 | tf_op jit(solution)/shard_map/ppermute | solution.py:484
  13.9 13.0 %collective-permute-start.9 = (f32[320,128]{1,0:T(8,128)S(1)}, f32[320,128]{1,0:T(8,128)S(1)}, u32[]{:S(2)}, u32[]{:S(2)}) collective-permute-start(f32[320,128]{1,0:T(8,128)S(1)} %get-tuple-element.65), channel_id=1, source_target_pairs={{0,128},{128,256},{256,384},{384,0},{1,129},{129,257},{257,385},{3... | collective-permute-start | bytes 491528 | tf_op jit(solution)/shard_map/ppermute | solution.py:491
  15.8 11.1 %collective-permute-start.10 = (f32[320,128]{1,0:T(8,128)S(1)}, f32[320,128]{1,0:T(8,128)S(1)}, u32[]{:S(2)}, u32[]{:S(2)}) collective-permute-start(f32[320,128]{1,0:T(8,128)S(1)} %get-tuple-element.66), channel_id=1, source_target_pairs={{0,256},{128,384},{256,0},{384,128},{1,257},{129,385},{257,1},{385... | collective-permute-start | bytes 491528 | tf_op jit(solution)/shard_map/ppermute | solution.py:491
  17.8 10.3 %collective-permute-start.11 = (f32[320,128]{1,0:T(8,128)S(1)}, f32[320,128]{1,0:T(8,128)S(1)}, u32[]{:S(2)}, u32[]{:S(2)}) collective-permute-start(f32[320,128]{1,0:T(8,128)S(1)} %get-tuple-element.67), channel_id=1, source_target_pairs={{0,384},{128,0},{256,128},{384,256},{1,385},{129,1},{257,129},{385... | collective-permute-start | bytes 491528 | tf_op jit(solution)/shard_map/ppermute | solution.py:491
  30.4 18.2 %all-to-all-start.3 = ((f32[8,120,128]{2,1,0:T(8,128)}), f32[8,120,128]{2,1,0:T(8,128)S(1)}, u32[]{:S(2)}, u32[]{:S(2)}) async-start(f32[8,120,128]{2,1,0:T(8,128)} %get-tuple-element.70), calls=%async_computation.3 | async-start | bytes 983040 | tf_op jit(solution)/shard_map/all_to_all | solution.py:507
  34.1 9.2 %collective-permute-start.12 = (f32[32,512]{1,0:T(8,128)S(1)}, f32[32,512]{1,0:T(8,128)S(1)}, u32[]{:S(2)}, u32[]{:S(2)}) collective-permute-start(f32[32,512]{1,0:T(8,128)S(1)} %get-tuple-element.68.first), channel_id=1, source_target_pairs={{0,4},{1,5},{2,6},{3,7},{4,0},{5,1},{6,2},{7,3},{8,12},{9,13},{10,... | collective-permute-start | bytes 196616 | tf_op jit(solution)/shard_map/ppermute | solution.py:497
  43.2 12.8 %collective-permute-start.13 = (f32[64,512]{1,0:T(8,128)S(1)}, f32[64,512]{1,0:T(8,128)S(1)}, u32[]{:S(2)}, u32[]{:S(2)}) collective-permute-start(f32[64,512]{1,0:T(8,128)S(1)} %get-tuple-element.72.first), channel_id=1, source_target_pairs={{0,2},{1,3},{2,0},{3,1},{4,6},{5,7},{6,4},{7,5},{8,10},{9,11},{10,... | collective-permute-start | bytes 393224 | tf_op jit(solution)/shard_map/ppermute | solution.py:497
  49.3 13.7 %all-to-all-start.4 = ((f32[8,8,128]{2,1,0:T(8,128)}), f32[8,8,128]{2,1,0:T(8,128)S(1)}, u32[]{:S(2)}, u32[]{:S(2)}) async-start(f32[8,8,128]{2,1,0:T(8,128)} %pieces.3.after), calls=%async_computation.4 | async-start | bytes 65536 | tf_op jit(solution)/shard_map/all_to_all | solution.py:511
  63.6 16.7 %all-to-all-start.5 = ((f32[4,376,128]{2,1,0:T(8,128)}), f32[4,376,128]{2,1,0:T(8,128)S(1)}, u32[]{:S(2)}, u32[]{:S(2)}) async-start(f32[4,376,128]{2,1,0:T(8,128)} %append.3), calls=%async_computation.5 | async-start | bytes 1540096 | tf_op jit(solution)/shard_map/all_to_all | solution.py:514
  70.7 7.5 %collective-permute-start.14 = (f32[128,512]{1,0:T(8,128)S(1)}, f32[128,512]{1,0:T(8,128)S(1)}, u32[]{:S(2)}, u32[]{:S(2)}) collective-permute-start(f32[128,512]{1,0:T(8,128)S(1)} %get-tuple-element.74.first), channel_id=1, source_target_pairs={{0,1},{1,0},{2,3},{3,2},{4,5},{5,4},{6,7},{7,6},{8,9},{9,8},{10,11... | collective-permute-start | bytes 786440 | tf_op jit(solution)/shard_map/ppermute | solution.py:497
  80.4 7.2 %collective-permute-start.15 = (f32[4,376,128]{2,1,0:T(8,128)S(1)}, f32[4,376,128]{2,1,0:T(8,128)S(1)}, u32[]{:S(2)}, u32[]{:S(2)}) collective-permute-start(f32[4,376,128]{2,1,0:T(8,128)S(1)} %all-to-all-done.5.own), channel_id=1, source_target_pairs={{0,8},{8,0},{1,9},{9,1},{2,10},{10,2},{3,11},{11,3},{4,12},{12,4},... | collective-permute-start | bytes 2310152 | tf_op jit(solution)/shard_map/ppermute | solution.py:484
